TPU v7x, 128 devices: a whole 4x4x4 slice. The times are simulated.
128 devices in a mesh: kv: 16 (over x, z), head: 8 (over y, core).
Axes of the slice: x: 4, y: 4, z: 4, core: 2. Of those that a mesh axis runs over, the one named last changes fastest.
Arguments:
- queries: bfloat16 [32, 16384], P(None, 'head'), may hold values from -100 to 100
- key_cache: bfloat16 [384, 8, 128, 128], P('kv', 'head'), may hold values from -6 to 6
- value_cache: bfloat16 [384, 8, 128, 128], P('kv', 'head'), may hold values from -6 to 6
- block_table: int32 [2, 384], P(None, 'kv'), may hold values from 0 to 128, as said below
- lengths: int32 [16], replicated, may hold values from 2 to 16384, as said below
- new_keys: bfloat16 [32, 1024], P(None, 'head'), may hold values from -4 to 4
- new_values: bfloat16 [32, 1024], P(None, 'head'), may hold values from -6 to 6
- residual: bfloat16 [32, 16384], P(None, ('kv', 'head')), may hold values from -2 to 2
- out_weight: bfloat16 [8, 16, 128, 16384], P('head', 'kv'), may hold values from -0.0625 to 0.0625
- norm_gain: bfloat16 [16384], P(('kv', 'head')), may hold values from 0.5 to 1.5
- w_gate: bfloat16 [16384, 26624], P('kv', 'head'), may hold values from -0.046875 to 0.046875
- w_up: bfloat16 [16384, 26624], P('kv', 'head'), may hold values from -0.046875 to 0.046875
- w_down: bfloat16 [26624, 16384], P('head', 'kv'), may hold values from -0.0546875 to 0.0546875
Outputs:
- layer_out: bfloat16 [32, 16384], P(None, ('kv', 'head'))
Inputs may be any that keep to these rules, and one draw needn't show every extreme that they name: `block_table`: each sequence's tokens fill blocks 0 to ceil(length / 128) - 1 of it; each such block is held by exactly one slot. Every other slot, and there is at least one, names sequence 0 and block position 128, so it holds no live token. Slots are spread over the devices in no particular order. `lengths`: the longest sequence has exactly 16384 tokens.
All inputs are finite; a program needn't handle non-finite values.
Results may differ from a plain program's by a relative error of at most 0.03.
Values may be sent and summed in bfloat16 or wider, within the bound.
No kernel may reach another device: no remote copies, remote signals or barrier semaphores. Data moves between devices by JAX's collectives and lax.ppermute only.
A program may use at most 128 MiB of HBM per device.

v0:
```python
import math

import jax
import jax.numpy as jnp
from jax import lax
from jax.sharding import PartitionSpec as P

HQ = 128
KVH = 8
SEQS = 16


def joined(value, axis, join):
    pieces = jax.tree.map(lambda part: lax.all_gather(part, axis), value)
    head = jax.tree.map(lambda part: part[0], pieces)
    tail = jax.tree.map(lambda part: part[1:], pieces)
    total, _ = lax.scan(lambda total, section: (join(total, section), None), head, tail)
    return total


def block_partials(queries, key_cache, value_cache, block_table, lengths):
    highest = lax.Precision.HIGHEST
    blocks_here, kv_local, block_len, head_dim = key_cache.shape
    group = HQ // KVH
    query_five = queries.reshape(SEQS, 2, kv_local, group, head_dim)
    seq_ids = block_table[0]
    pos_ids = block_table[1]
    picked = query_five[seq_ids]
    scores = jnp.einsum(
        "btkgd,bkud->btkgu", picked, key_cache, preferred_element_type=jnp.float32
    ) / math.sqrt(head_dim)
    token_pos = pos_ids[:, None] * block_len + jnp.arange(block_len, dtype=jnp.int32)[None, :]
    live_mask = (token_pos < lengths[seq_ids][:, None])[:, None, None, None, :]
    block_max = jnp.max(jnp.where(live_mask, scores, -1e30), axis=-1)
    expo_vals = jnp.where(live_mask, jnp.exp(scores - block_max[..., None]), 0.0)
    block_sum = jnp.sum(expo_vals, axis=-1)
    probs_low = expo_vals.astype(jnp.bfloat16)
    block_out = jnp.einsum(
        "btkgu,bkud->btkgd", probs_low, value_cache, preferred_element_type=jnp.float32
    )
    member = (seq_ids[:, None] == jnp.arange(SEQS, dtype=jnp.int32)[None, :])[
        :, :, None, None, None
    ]
    seq_max = jnp.max(jnp.where(member, block_max[:, None], -1e30), axis=0)
    weights = jnp.where(member, jnp.exp(block_max[:, None] - seq_max[None]), 0.0)
    numer = jnp.einsum("bstkg,btkgd->stkgd", weights, block_out, precision=highest)
    denom = jnp.einsum("bstkg,btkg->stkg", weights, block_sum, precision=highest)
    heads_here = kv_local * group
    return (
        numer.reshape(SEQS * 2, heads_here, head_dim),
        denom.reshape(SEQS * 2, heads_here),
        seq_max.reshape(SEQS * 2, heads_here),
    )


def join_partials(earlier, latter):
    numer_a, denom_a, max_a = earlier
    numer_b, denom_b, max_b = latter
    overall = jnp.maximum(max_a, max_b)
    scale_a = jnp.exp(max_a - overall)
    scale_b = jnp.exp(max_b - overall)
    return (
        numer_a * scale_a[..., None] + numer_b * scale_b[..., None],
        denom_a * scale_a + denom_b * scale_b,
        overall,
    )


def on_device(
    queries,
    key_cache,
    value_cache,
    block_table,
    lengths,
    new_keys,
    new_values,
    residual,
    out_weight,
    norm_gain,
    w_gate,
    w_up,
    w_down,
):
    head_dim = key_cache.shape[3]
    kv_local = key_cache.shape[1]
    group = HQ // KVH
    heads_here = kv_local * group
    own_count = heads_here // lax.axis_size("kv")
    start = lax.axis_index("kv") * own_count
    numer, denom, seq_max = block_partials(queries, key_cache, value_cache, block_table, lengths)
    merged_numer, merged_denom, merged_max = joined((numer, denom, seq_max), "kv", join_partials)
    numer_own = lax.dynamic_slice_in_dim(merged_numer, start, own_count, 1)
    denom_own = lax.dynamic_slice_in_dim(merged_denom, start, own_count, 1)
    max_own = lax.dynamic_slice_in_dim(merged_max, start, own_count, 1)
    query_heads = queries.reshape(SEQS * 2, heads_here, head_dim)
    query_own = lax.dynamic_slice_in_dim(query_heads, start, own_count, 1).reshape(
        SEQS, 2, own_count, head_dim
    )
    kv_pick = (start + jnp.arange(own_count, dtype=jnp.int32)) // group
    fresh_keys = jnp.take(new_keys.reshape(SEQS, 2, kv_local, head_dim), kv_pick, axis=2)
    fresh_vals = jnp.take(new_values.reshape(SEQS, 2, kv_local, head_dim), kv_pick, axis=2)
    fresh_scores = jnp.einsum(
        "sted,sued->steu", query_own, fresh_keys, preferred_element_type=jnp.float32
    ) / math.sqrt(head_dim)
    causal = (jnp.arange(2)[:, None] >= jnp.arange(2)[None, :])[None, :, None, :]
    fresh_max = jnp.max(jnp.where(causal, fresh_scores, -1e30), axis=-1)
    fresh_expo = jnp.where(causal, jnp.exp(fresh_scores - fresh_max[..., None]), 0.0)
    fresh_sum = jnp.sum(fresh_expo, axis=-1).reshape(SEQS * 2, own_count)
    fresh_out = jnp.einsum(
        "steu,sued->sted",
        fresh_expo.astype(jnp.bfloat16),
        fresh_vals,
        preferred_element_type=jnp.float32,
    ).reshape(SEQS * 2, own_count, head_dim)
    fresh_max = fresh_max.reshape(SEQS * 2, own_count)
    overall_max = jnp.maximum(max_own, fresh_max)
    cache_scale = jnp.exp(max_own - overall_max)
    fresh_scale = jnp.exp(fresh_max - overall_max)
    total_numer = numer_own * cache_scale[..., None] + fresh_out * fresh_scale[..., None]
    total_denom = denom_own * cache_scale + fresh_sum * fresh_scale
    attn = (
        (total_numer / total_denom[..., None])
        .astype(jnp.bfloat16)
        .reshape(SEQS * 2, own_count * head_dim)
    )
    proj_rows = out_weight.reshape(own_count * head_dim, out_weight.shape[3])
    proj = jnp.dot(attn, proj_rows, preferred_element_type=jnp.float32)
    proj_share = lax.psum_scatter(proj, ("kv", "head"), scatter_dimension=1, tiled=True)
    hidden_one = residual.astype(jnp.float32) + proj_share
    full_width = residual.shape[1] * lax.axis_size("kv") * lax.axis_size("head")
    square_total = lax.psum(jnp.sum(hidden_one * hidden_one, axis=1), ("kv", "head"))
    mean_sq = square_total / full_width
    normed = (
        hidden_one * lax.rsqrt(mean_sq[:, None] + 1e-05) * norm_gain.astype(jnp.float32)
    ).astype(jnp.bfloat16)
    piece = lax.all_gather(normed, "head", axis=1, tiled=True)
    gate_part = jnp.dot(piece, w_gate, preferred_element_type=jnp.float32)
    upper_part = jnp.dot(piece, w_up, preferred_element_type=jnp.float32)
    gate_full, upper_full = (
        lax.psum(gate_part.astype(jnp.bfloat16), "kv").astype(jnp.float32),
        lax.psum(upper_part.astype(jnp.bfloat16), "kv").astype(jnp.float32),
    )
    hidden = (jax.nn.silu(gate_full) * upper_full).astype(jnp.bfloat16)
    down_part = jnp.dot(hidden, w_down, preferred_element_type=jnp.float32)
    down_share = lax.psum_scatter(
        down_part.astype(jnp.bfloat16), "head", scatter_dimension=1, tiled=True
    ).astype(jnp.float32)
    return (hidden_one + down_share).astype(jnp.bfloat16)


def solution(mesh):
    in_specs = (
        P(None, "head"),
        P("kv", "head", None, None),
        P("kv", "head", None, None),
        P(None, "kv"),
        P(),
        P(None, "head"),
        P(None, "head"),
        P(None, ("kv", "head")),
        P("head", "kv", None, None),
        P(("kv", "head")),
        P("kv", "head"),
        P("kv", "head"),
        P("head", "kv"),
    )
    out_specs = P(None, ("kv", "head"))
    return jax.shard_map(
        on_device, mesh=mesh, in_specs=in_specs, out_specs=out_specs, check_vma=False
    )
```

profile of v0, /device:TPU:1, one launch (start us, length us, event | category | flops | bytes accessed | tf_op | source)
XLA Modules:
  0.0 949.1 jit_solution(5675313705542814087)
XLA Ops:
  9.0 1.4 gather_fusion
  12.0 1.5 fusion.6
  17.7 21.6 %all_gather.13 = f32[16,32,16]{1,2,0:T(8,128)S(1)} all-gather(f32[1,32,16]{1,2,0:T(8,128)S(1)} %copy.80), channel_id=1, replica_groups=mesh['kv'=16,'head'=8] {'kv'}, dimensions={0}, use_global_device_ids=true | all-gather | bytes 34816 | tf_op jit(solution)/shard_map/all_gather | solution.py:14
  39.4 18.0 %all_gather.14 = f32[16,32,16]{1,2,0:T(8,128)S(1)} all-gather(f32[1,32,16]{1,2,0:T(8,128)S(1)} %copy.81), channel_id=1, replica_groups=mesh['kv'=16,'head'=8] {'kv'}, dimensions={0}, use_global_device_ids=true | all-gather | bytes 34816 | tf_op jit(solution)/shard_map/all_gather | solution.py:14
  57.6 13.1 %all-gather.2.cloned.1.call-done = f32[16,32,16,128]{3,2,1,0:T(8,128)} async-done(((f32[1,32,16,128]{3,2,1,0:T(8,128)}), f32[16,32,16,128]{3,2,1,0:T(8,128)}) %all-gather.2.cloned.1.call-update) | async-done | bytes 4194320 | tf_op jit(solution)/shard_map/all_gather | solution.py:14
  71.7 4.3 slice.40
  76.0 21.5 %while.14 = (s32[]{:T(128)}, f32[32,16,128]{2,1,0:T(8,128)S(1)}, f32[32,16]{1,0:T(8,128)S(1)}, f32[32,16]{1,0:T(8,128)S(1)}, f32[15,32,16]{1,2,0:T(8,128)S(1)}, ...) while((s32[]{:T(128)}, f32[32,16,128]{2,1,0:T(8,128)S(1)}, f32[32,16]{1,0:T(8,128)S(1)}, ...), condition=%wide.region_4.5_spmd, body=%wide.region_3.4_spmd.sunk | while | flops 199682 | bytes 823397 | solution.py:17
  76.2 1.2 fusion.60
  77.6 1.2 fusion.60
  79.1 1.2 fusion.60
  80.5 1.2 fusion.60
  81.9 1.2 fusion.60
  83.4 1.2 fusion.60
  87.7 1.2 fusion.60
  96.3 1.2 fusion.60
  97.8 4.3 fusion.3
  102.1 632.7 %reduce-scatter.5.cloned.1.call-done = f32[32,128]{1,0:T(8,128)} async-done(((f32[32,16384]{1,0:T(8,128)}), f32[32,128]{1,0:T(8,128)}) %reduce-scatter.5.cloned.1.call-update) | async-done | bytes 16400 | tf_op jit(solution)/shard_map/reduce_scatter | solution.py:128
  735.7 69.2 %psum.21 = f32[32]{0:T(128)S(1)} all-reduce(f32[32]{0:T(128)S(1)} %multiply_reduce_fusion.1), channel_id=1, replica_groups=mesh['kv'=16,'head'=8] {'kv','head'}, use_global_device_ids=true, to_apply=%region_9.10 | all-reduce | flops 32 | bytes 256 | tf_op jit(solution)/shard_map/psum | solution.py:131
  805.7 12.1 %all_gather.15 = bf16[32,1024]{1,0:T(8,128)(2,1)S(1)} all-gather(bf16[32,128]{1,0:T(8,128)(2,1)S(1)} %multiply_convert_fusion), channel_id=1, replica_groups=mesh['kv'=16,'head'=8] {'head'}, dimensions={1}, use_global_device_ids=true | all-gather | bytes 73728 | tf_op jit(solution)/shard_map/all_gather | solution.py:136
  817.8 4.9 convolution_convert_fusion
  822.7 4.9 convolution_convert_fusion.1
  827.7 80.2 %all-reduce.3.cloned.1.call-done = (bf16[32,3328]{1,0:T(8,128)(2,1)}, bf16[32,3328]{1,0:T(8,128)(2,1)}) async-done(((bf16[32,3328]{1,0:T(8,128)(2,1)}, bf16[32,3328]{1,0:T(8,128)(2,1)}), (bf16[32,3328]{1,0:T(8,128)(2,1)}, bf16[32,3328]{1,0:T(8,128)(2,1)})) %all-reduce.3.cloned.1.call-update) | async-done | bytes 426000 | tf_op jit(solution)/shard_map/psum | solution.py:141
  907.9 4.4 convolution_convert_fusion.2
  913.2 27.9 %reduce-scatter.7.cloned.1.call-done = bf16[128,32]{1,0:T(8,128)(2,1)} async-done(((bf16[1024,32]{1,0:T(8,128)(2,1)}), bf16[128,32]{1,0:T(8,128)(2,1)}) %reduce-scatter.7.cloned.1.call-update) | async-done | bytes 8208
  (134 shorter events, 25.0 us)
Async XLA Ops:
  6.5 4.5 copy-start
  6.5 64.2 %all-gather.2.cloned.1.call-start = ((), (), s32[]{:S(2)}) async-start(), calls=%async_computation.2 | async-start | bytes 4456448 | tf_op jit(solution)/shard_map/all_gather | solution.py:14
  15.0 719.8 %reduce-scatter.5.cloned.1.call-start = ((), (), s32[]{:S(2)}) async-start(), calls=%async_computation.3 | async-start | bytes 2113536 | tf_op jit(solution)/shard_map/reduce_scatter | solution.py:128
  76.0 658.9 %copy-start.2 = (bf16[32,128]{1,0:T(8,128)(2,1)S(1)}, bf16[32,128]{1,0:T(8,128)(2,1)}, u32[]{:S(2)}) copy-start(bf16[32,128]{1,0:T(8,128)(2,1)} %param.22) | copy-start | bytes 24580
  76.0 659.7 %copy-start.3 = (bf16[128]{0:T(256)(128)(2,1)S(1)}, bf16[128]{0:T(256)(128)(2,1)}, u32[]{:S(2)}) copy-start(bf16[128]{0:T(256)(128)(2,1)} %param.24) | copy-start | bytes 772
  102.1 805.8 %all-reduce.3.cloned.1.call-start = ((), (), s32[]{:S(2)}) async-start(), calls=%async_computation.5 | async-start | bytes 851968 | tf_op jit(solution)/shard_map/psum | solution.py:141
  822.7 119.2 %copy-start.1 = (f32[32,128]{1,0:T(8,128)S(1)}, f32[32,128]{1,0:T(8,128)}, u32[]{:S(2)}) copy-start(f32[32,128]{1,0:T(8,128)} %reduce-scatter.5.cloned.1.call-done) | copy-start | bytes 49156
  827.6 113.5 %reduce-scatter.7.cloned.1.call-start = ((), (), s32[]{:S(2)}) async-start(), calls=%async_computation.4 | async-start | bytes 294912
Sparse Core Ops, SparseCore 0:
  15.1 55.5 all-gather.1
  102.2 632.6 reduce-scatter.4
  827.8 80.0 all-reduce.2
  913.3 27.7 reduce-scatter.6
where the time goes:
time: 952 us; the launch traced here: 949 us
  waiting for transfers between devices  754 us (79%)
  blocking collectives  121 us (13%)
  other arithmetic  24.3 us (3%)
  matrix products  21.6 us (2%)
  local copies, waits for them, and re-layouts  14.4 us (2%)
  between operations  13.3 us (1%)
    reduce_scatter x1, waiting for transfers between devices, on_device(): lax.psum_scatter(proj, ('kv', 'head'), scatter_dimension=1, tiled=True)  633 us
    psum x1, waiting for transfers between devices, on_device(): lax.psum(upper_part.astype(jnp.bfloat16), 'kv').astype(jnp.float32)  80.2 us
    psum x1, blocking collectives, on_device(): lax.psum(jnp.sum(hidden_one * hidden_one, axis=1), ('kv', 'head'))  69.2 us
    all_gather x2, blocking collectives, joined(): pieces = jax.tree.map(lambda part: lax.all_gather(part, axis), value)  39.6 us
    unnamed x5, waiting for transfers between devices  28 us
  transfers between devices with their start and end apart: 4, of which 4 were waited for; matrix products, arithmetic and copies ran while one was open for 0% of the time, Pallas kernels for 0%

commit v1 on v0

v1 whole, which is shorter than its diff:
```python
import math

import jax
import jax.numpy as jnp
from jax import lax
from jax.experimental import pallas as pl
from jax.experimental.pallas import tpu as pltpu
from jax.sharding import PartitionSpec as P

HQ = 128
KVH = 8
SEQS = 16
ROWS = 2 * SEQS
GROUP = HQ // KVH
HD = 128
SLOTS = 24
OWN = 128
HALF = 4 * OWN
N_KV = 16
UNITS = 3328
PART = UNITS // 2
EXTRA = 128
TILE = 256

F32 = jnp.float32
BF16 = jnp.bfloat16
MIB = 1 << 20


def whole(shape, space=pltpu.VMEM):
    zeros = (0,) * len(shape)
    return pl.BlockSpec(shape, lambda *_: zeros, memory_space=space)


def scalars():
    return pl.BlockSpec(memory_space=pltpu.SMEM)


def params(mib, steps=0):
    kinds = ("arbitrary",) * steps if steps else None
    return pltpu.CompilerParams(vmem_limit_bytes=mib * MIB, dimension_semantics=kinds)


def shape(dims, kind):
    return jax.ShapeDtypeStruct(dims, kind)


def attention_kernel(table, lengths, q_ref, k_ref, v_ref, out_ref, q_rows, scores, tops, sums, numer):
    for g in range(GROUP):
        q_rows[pl.ds(g, ROWS, stride=GROUP), :] = q_ref[:, g * HD : (g + 1) * HD].astype(F32)
    tops[...] = jnp.full(tops.shape, -1e30, F32)
    sums[...] = jnp.zeros(sums.shape, F32)
    numer[...] = jnp.zeros(numer.shape, F32)
    lane = lax.broadcasted_iota(jnp.int32, (ROWS, HD), 1)
    rows_of = []
    for b in range(SLOTS):
        seq = table[0, b]
        limit = lengths[seq] - table[1, b] * HD
        here = pl.ds(pl.multiple_of(seq * ROWS, ROWS), ROWS)
        rows_of.append(here)
        raw = lax.dot_general(
            q_rows[here, :].astype(BF16), k_ref[b, 0], (((1,), (1,)), ((), ())),
            preferred_element_type=F32,
        )
        masked = jnp.where(lane < limit, raw * (1.0 / math.sqrt(HD)), -1e30)
        scores[b] = masked
        tops[here, :] = jnp.maximum(tops[here, :], jnp.max(masked, axis=1, keepdims=True))
    tops[...] = tops[...].astype(BF16).astype(F32)
    for b in range(SLOTS):
        here = rows_of[b]
        masked = scores[b]
        expo = jnp.where(masked > -1e29, jnp.exp(masked - tops[here, :]), 0.0)
        sums[here, :] += jnp.sum(expo, axis=1, keepdims=True)
        numer[here, :] += jnp.dot(expo.astype(BF16), v_ref[b, 0], preferred_element_type=F32)
    for g in range(GROUP):
        pick = pl.ds(g, ROWS, stride=GROUP)
        out_ref[g, :, :HD] = numer[pick, :].astype(BF16)
        high = sums[pick, :].astype(BF16).astype(F32)
        stats = jnp.where(lane < 32, tops[pick, :], jnp.where(lane < 64, high, sums[pick, :] - high))
        out_ref[g, :, HD:] = stats.astype(BF16)


def attention_partials(table, lengths, queries, key_cache, value_cache):
    tall = pltpu.VMEM((ROWS * GROUP, HD), F32)
    return pl.pallas_call(
        attention_kernel,
        out_shape=shape((GROUP, ROWS, 2 * HD), BF16),
        in_specs=[scalars(), scalars()] + [whole(a.shape) for a in (queries, key_cache, value_cache)],
        out_specs=whole((GROUP, ROWS, 2 * HD)),
        scratch_shapes=[tall, pltpu.VMEM((SLOTS, ROWS, HD), F32), tall, tall, tall],
        compiler_params=params(16),
        name="attention",
    )(table, lengths, queries, key_cache, value_cache)


def project_kernel(place, got_ref, q_ref, k_ref, v_ref, w_ref, keep_ref, give_ref, attn):
    @pl.when(pl.program_id(0) == 0)
    def _():
        start = pl.multiple_of(place[0] * HD, HD)
        query = q_ref[:, pl.ds(start, HD)].astype(F32)
        keys, values = k_ref[...].astype(F32), v_ref[...].astype(F32)
        odd = lax.broadcasted_iota(jnp.int32, (ROWS, 1), 0) % 2 == 1
        unit = 1.0 / math.sqrt(HD)
        at_own = jnp.sum(query * keys, axis=1, keepdims=True) * unit
        at_prev = jnp.sum(query * pltpu.roll(keys, 1, 0), axis=1, keepdims=True) * unit
        new_max = jnp.where(odd, jnp.maximum(at_own, at_prev), at_own)
        expo_own = jnp.exp(at_own - new_max)
        expo_prev = jnp.where(odd, jnp.exp(at_prev - new_max), 0.0)
        new_out = expo_own.astype(BF16).astype(F32) * values
        new_out += expo_prev.astype(BF16).astype(F32) * pltpu.roll(values, 1, 0)
        maxes = [got_ref[i, :, HD : HD + 1].astype(F32) for i in range(N_KV)]
        peak = new_max
        for top in maxes:
            peak = jnp.maximum(peak, top)
        scale = jnp.exp(new_max - peak)
        total = scale * new_out
        denom = scale * (expo_own + expo_prev)
        for i in range(N_KV):
            scale = jnp.exp(maxes[i] - peak)
            high = got_ref[i, :, HD + 32 : HD + 33].astype(F32)
            low = got_ref[i, :, HD + 64 : HD + 65].astype(F32)
            total += scale * got_ref[i, :, :HD].astype(F32)
            denom += scale * (high + low)
        attn[...] = (total / denom).astype(BF16)

    even = place[2] == 0
    for d in range(w_ref.shape[1] // (2 * HALF)):
        for y in range(4):
            at = d * 2 * HALF + y * TILE
            both = jnp.dot(attn[...], w_ref[:, at : at + TILE], preferred_element_type=F32)
            here = slice(y * OWN, (y + 1) * OWN)
            keep_ref[d, :, here] = jnp.where(even, both[:, :OWN], both[:, OWN:])
            give_ref[d, :, here] = jnp.where(even, both[:, OWN:], both[:, :OWN]).astype(BF16)


def project(place, got, queries, new_keys, new_values, weight):
    steps, each = 8, N_KV // 8
    block = pl.BlockSpec((each, ROWS, HALF), lambda i: (i, 0, 0))
    return pl.pallas_call(
        project_kernel,
        grid=(steps,),
        out_shape=[shape((N_KV, ROWS, HALF), F32), shape((N_KV, ROWS, HALF), BF16)],
        in_specs=[scalars()]
        + [whole(a.shape) for a in (got, queries, new_keys, new_values)]
        + [pl.BlockSpec((HD, each * 2 * HALF), lambda i: (0, i))],
        out_specs=[block, block],
        scratch_shapes=[pltpu.VMEM((ROWS, HD), BF16)],
        compiler_params=params(16, 1),
        name="project",
    )(place, got, queries, new_keys, new_values, weight)


def pair_kernel(keep_ref, got_ref, out_ref):
    out_ref[...] = (keep_ref[...] + got_ref[...].astype(F32)).astype(BF16)


def add_pair(keep, got):
    return pl.pallas_call(
        pair_kernel,
        out_shape=shape(keep.shape, BF16),
        in_specs=[whole(keep.shape), whole(got.shape)],
        out_specs=whole(keep.shape),
        compiler_params=params(16),
        name="add_pair",
    )(keep, got)


def stream_kernel(place, parts_ref, res_ref, gain_ref, out_ref):
    total = parts_ref[0].astype(F32)
    for i in range(1, N_KV):
        total += parts_ref[i].astype(F32)
    for y in range(4):
        here = slice(y * OWN, (y + 1) * OWN)
        mine = place[3] == y
        rest = jnp.where(mine, res_ref[...].astype(F32), 0.0)
        out_ref[:ROWS, here] = (total[:, here] + rest).astype(BF16)
        gain = jnp.where(mine, gain_ref[...].astype(F32), 0.0)
        out_ref[ROWS:, here] = jnp.broadcast_to(gain, (16, OWN)).astype(BF16)


def stream(place, parts, residual, gain):
    return pl.pallas_call(
        stream_kernel,
        out_shape=shape((ROWS + 16, HALF), BF16),
        in_specs=[scalars()] + [whole(a.shape) for a in (parts, residual, gain)],
        out_specs=whole((ROWS + 16, HALF)),
        compiler_params=params(16),
        name="stream",
    )(place, parts, residual, gain)


def gate_kernel(place, mine_ref, other_ref, gate_ref, up_ref, out_ref, own_ref, x, gate, up, squares):
    step = pl.program_id(0)

    @pl.when(step == 0)
    def _():
        even = place[2] == 0
        mine, other = mine_ref[...].astype(F32), other_ref[...].astype(F32)
        halves = (jnp.where(even, mine, other), jnp.where(even, other, mine))
        square = jnp.zeros((ROWS, OWN), F32)
        own = jnp.zeros((ROWS, OWN), F32)
        for y in range(4):
            for c in range(2):
                block = halves[c][:ROWS, y * OWN : (y + 1) * OWN]
                gain = halves[c][ROWS : ROWS + 1, y * OWN : (y + 1) * OWN]
                at = (2 * y + c) * OWN
                x[:, at : at + OWN] = (block * gain).astype(BF16)
                square += block * block
            own += jnp.where(place[3] == y, mine[:ROWS, y * OWN : (y + 1) * OWN], 0.0)
        own_ref[...] = own
        total = jnp.sum(square, axis=1, keepdims=True)
        high = total.astype(BF16).astype(F32)
        lane = lax.broadcasted_iota(jnp.int32, (ROWS, EXTRA), 1)
        squares[...] = jnp.where(lane < 64, high, total - high)

    gate[step] = jnp.dot(x[...], gate_ref[...], preferred_element_type=F32)
    up[step] = jnp.dot(x[...], up_ref[...], preferred_element_type=F32)

    @pl.when(step == pl.num_programs(0) - 1)
    def _():
        for d in range(N_KV):
            rows = slice(4 * (d // 2), 4 * (d // 2) + 4)
            for t in range(13):
                tile = 13 * (d % 2) + t
                lanes = slice((tile % 2) * 128, (tile % 2) * 128 + 128)
                out_ref[d, :, t * 128 : (t + 1) * 128] = gate[tile // 2, rows, lanes].astype(BF16)
                at = PART + t * 128
                out_ref[d, :, at : at + 128] = up[tile // 2, rows, lanes].astype(BF16)
            out_ref[d, :, 2 * PART :] = squares[rows, :].astype(BF16)


def gate_up(place, mine, other, w_gate, w_up):
    steps = UNITS // TILE
    block = pl.BlockSpec((w_gate.shape[0], TILE), lambda i: (0, i))
    held = pltpu.VMEM((steps, ROWS, TILE), F32)
    wide = (N_KV, 4, 2 * PART + EXTRA)
    return pl.pallas_call(
        gate_kernel,
        grid=(steps,),
        out_shape=[shape(wide, BF16), shape((ROWS, OWN), F32)],
        in_specs=[scalars(), whole(mine.shape), whole(other.shape), block, block],
        out_specs=[whole(wide), whole((ROWS, OWN))],
        scratch_shapes=[
            pltpu.VMEM((ROWS, w_gate.shape[0]), BF16), held, held, pltpu.VMEM((ROWS, EXTRA), F32),
        ],
        compiler_params=params(16, 1),
        name="gate_up",
    )(place, mine, other, w_gate, w_up)


def hidden_kernel(parts_ref, out_ref):
    total = parts_ref[0].astype(F32)
    for i in range(1, N_KV):
        total += parts_ref[i].astype(F32)
    squares = total[:, 2 * PART : 2 * PART + 1] + total[:, 2 * PART + 64 : 2 * PART + 65]
    scale = lax.rsqrt(squares / (HQ * HD) + 1e-05)
    gate, up = total[:, :PART] * scale, total[:, PART : 2 * PART] * scale
    hidden = (gate / (1.0 + jnp.exp(-gate)) * up).astype(BF16)
    for i in range(N_KV):
        out_ref[i] = hidden


def hidden_units(parts):
    return pl.pallas_call(
        hidden_kernel,
        out_shape=shape((N_KV, 4, PART), BF16),
        in_specs=[whole(parts.shape)],
        out_specs=whole((N_KV, 4, PART)),
        compiler_params=params(16),
        name="hidden_units",
    )(parts)


def down_kernel(place, parts_ref, w_ref, keep_ref, give_ref, x, total):
    step = pl.program_id(0)

    @pl.when(step == 0)
    def _():
        for d in range(N_KV):
            piece = parts_ref[d].astype(F32)
            rows = slice(4 * (d // 2), 4 * (d // 2) + 4)
            for t in range(13):
                tile = 13 * (d % 2) + t
                lanes = slice((tile % 2) * 128, (tile % 2) * 128 + 128)
                x[tile // 2, rows, lanes] = piece[:, t * 128 : (t + 1) * 128]
        total[...] = jnp.zeros(total.shape, F32)

    total[...] += jnp.dot(x[step].astype(BF16), w_ref[...], preferred_element_type=F32)

    @pl.when(step == pl.num_programs(0) - 1)
    def _():
        even = place[2] == 0
        for y in range(4):
            zero = total[:, (2 * y) * OWN : (2 * y + 1) * OWN]
            one = total[:, (2 * y + 1) * OWN : (2 * y + 2) * OWN]
            keep_ref[y] = jnp.where(even, zero, one)
            give_ref[y] = jnp.where(even, one, zero).astype(BF16)


def down(place, parts, w_down):
    steps = UNITS // TILE
    out = (4, ROWS, OWN)
    return pl.pallas_call(
        down_kernel,
        grid=(steps,),
        out_shape=[shape(out, F32), shape(out, BF16)],
        in_specs=[
            scalars(), whole(parts.shape),
            pl.BlockSpec((TILE, w_down.shape[1]), lambda i: (i, 0)),
        ],
        out_specs=[whole(out), whole(out)],
        scratch_shapes=[
            pltpu.VMEM((steps, ROWS, TILE), F32), pltpu.VMEM((ROWS, w_down.shape[1]), F32),
        ],
        compiler_params=params(16, 1),
        name="down",
    )(place, parts, w_down)


def split_kernel(place, keep_ref, got_ref, *outs):
    for i, out_ref in enumerate(outs):
        at = place[3] ^ i
        out_ref[...] = (keep_ref[at] + got_ref[at].astype(F32)).astype(out_ref.dtype)


def split(place, keep, got):
    each = (ROWS, OWN)
    return pl.pallas_call(
        split_kernel,
        out_shape=[shape(each, F32)] + [shape(each, BF16)] * 3,
        in_specs=[scalars(), whole(keep.shape), whole(got.shape)],
        out_specs=[whole(each)] * 4,
        compiler_params=params(16),
        name="split",
    )(place, keep, got)


def exchange(value, axis):
    return lax.all_to_all(value, axis, 0, 0, tiled=True)


def swap(value, step):
    return lax.ppermute(value, "head", [(j, j ^ step) for j in range(KVH)])


def on_device(
    queries,
    key_cache,
    value_cache,
    block_table,
    lengths,
    new_keys,
    new_values,
    residual,
    out_weight,
    norm_gain,
    w_gate,
    w_up,
    w_down,
):
    me_kv, me_head = lax.axis_index("kv"), lax.axis_index("head")
    place = jnp.stack([me_kv, me_head, me_head % 2, me_head // 2]).astype(jnp.int32)
    partials = attention_partials(block_table, lengths, queries, key_cache, value_cache)
    keep, give = project(place, exchange(partials, "kv"), queries, new_keys, new_values, out_weight[0, 0])
    parts = exchange(add_pair(keep, swap(give, 1)), "kv")
    here = stream(place, parts, residual, norm_gain[None])
    here = (here.astype(F32) + swap(here, 2).astype(F32)).astype(BF16)
    here = (here.astype(F32) + swap(here, 4).astype(F32)).astype(BF16)
    gates, own = gate_up(place, here, swap(here, 1), w_gate, w_up)
    hidden = exchange(hidden_units(exchange(gates, "kv")), "kv")
    keep, give = down(place, hidden, w_down)
    mine, one, two, three = split(place, keep, swap(give, 1))
    total = own + mine
    for piece, step in ((one, 2), (two, 4), (three, 6)):
        total = total + swap(piece, step).astype(F32)
    return total.astype(BF16)


def solution(mesh):
    in_specs = (
        P(None, "head"),
        P("kv", "head", None, None),
        P("kv", "head", None, None),
        P(None, "kv"),
        P(),
        P(None, "head"),
        P(None, "head"),
        P(None, ("kv", "head")),
        P("head", "kv", None, None),
        P(("kv", "head")),
        P("kv", "head"),
        P("kv", "head"),
        P("head", "kv"),
    )
    out_specs = P(None, ("kv", "head"))
    return jax.shard_map(
        on_device, mesh=mesh, in_specs=in_specs, out_specs=out_specs, check_vma=False
    )
```

time: 952 us -> 111 us (0.12)
  waiting for transfers between devices: 754 us -> 17.7 us
  blocking collectives: 121 us -> 36 us
  starting transfers between devices: 0.13 us -> 27.2 us
  other arithmetic: 24.3 us -> 0.71 us
  matrix products: 21.6 us -> 0 us
  Pallas kernels: 0 us -> 16 us
  between operations: 13.3 us -> 0.11 us
    reduce_scatter x1 -> x0, waiting for transfers between devices: 633 us -> none  [on_device(): lax.psum_scatter(proj, ('kv', 'head'), scatter_dimension=1, tiled=True)]
    psum x1 -> x0, waiting for transfers between devices: 80.2 us -> none  [on_device(): lax.psum(upper_part.astype(jnp.bfloat16), 'kv').astype(jnp.float32)]
    psum x1 -> x0, blocking collectives: 69.2 us -> none  [on_device(): lax.psum(jnp.sum(hidden_one * hidden_one, axis=1), ('kv', 'head'))]
    all_gather x3 -> x0, blocking collectives: 51.7 us -> none  [the longest x2 39.6 us: joined(): pieces = jax.tree.map(lambda part: lax.all_gather(part, axis), value)]
    all_to_all x0 -> x3, blocking collectives: none -> 36 us  [exchange(): return lax.all_to_all(value, axis, 0, 0, tiled=True)]
    unnamed x5 -> x0, waiting for transfers between devices: 28 us -> none
    dot_general x9 -> x0, matrix products: 21.6 us -> none  [the longest x1 4.89 us: on_device(): gate_part = jnp.dot(piece, w_gate, preferred_element_type=jnp.float32)]
    ppermute x0 -> x8, starting transfers between devices: none -> 18.7 us  [swap(): return lax.ppermute(value, 'head', [(j, j ^ step) for j in range(KVH)])]
  transfers between devices with their start and end apart: 4 -> 9, of which waited for: 4 -> 8; matrix products, arithmetic and copies ran while one was open for 0% -> 0% of each run, Pallas kernels for 0% -> 0%
where the time goes in v1:
time: 111 us; the launch traced here: 110 us
  blocking collectives  36 us (32%)
  starting transfers between devices  27.2 us (25%)
  waiting for transfers between devices  17.7 us (16%)
  Pallas kernels  16 us (14%)
  local copies, waits for them, and re-layouts  12.3 us (11%)
    all_to_all x3, blocking collectives, exchange(): return lax.all_to_all(value, axis, 0, 0, tiled=True)  36 us
    ppermute x8, starting transfers between devices, swap(): return lax.ppermute(value, 'head', [(j, j ^ step) for j in range(KVH)])  18.7 us
    unnamed x30, local copies, waits for them, and re-layouts  12.3 us
    ppermute x8, waiting for transfers between devices, swap(): return lax.ppermute(value, 'head', [(j, j ^ step) for j in range(KVH)])  10.3 us
    all_to_all x1, starting transfers between devices, exchange(): return lax.all_to_all(value, axis, 0, 0, tiled=True)  8.44 us
    all_to_all x1, waiting for transfers between devices, exchange(): return lax.all_to_all(value, axis, 0, 0, tiled=True)  7.36 us
    pallas_call x1, Pallas kernels, gate_up(): pl.pallas_call(gate_kernel, grid=(steps,), out_shape=[shape(wide, BF16),...  5.54 us
    pallas_call x1, Pallas kernels, down(): pl.pallas_call(down_kernel, grid=(steps,), out_shape=[shape(out, F32), sh...  3.4 us
  transfers between devices with their start and end apart: 9, of which 8 were waited for; matrix products, arithmetic and copies ran while one was open for 0% of the time, Pallas kernels for 0%

profile of v1, /device:TPU:1, one launch (start us, length us, event | category | flops | bytes accessed | tf_op | source)
XLA Modules:
  0.0 110.0 jit_solution(14020100479499313443)
XLA Ops:
  0.0 1.1 %copy-done.3 = bf16[24,1,128,128]{3,2,1,0:T(8,128)(2,1)S(1)} copy-done((bf16[24,1,128,128]{3,2,1,0:T(8,128)(2,1)S(1)}, bf16[24,1,128,128]{3,2,1,0:T(8,128)(2,1)}, u32[]{:S(2)}) %copy-start.3) | copy-done | bytes 786456
  1.1 1.1 %copy-done.4 = bf16[24,1,128,128]{3,2,1,0:T(8,128)(2,1)S(1)} copy-done((bf16[24,1,128,128]{3,2,1,0:T(8,128)(2,1)S(1)}, bf16[24,1,128,128]{3,2,1,0:T(8,128)(2,1)}, u32[]{:S(2)}) %copy-start.4) | copy-done | bytes 786456
  4.5 2.5 %attention.1 = bf16[16,32,256]{2,1,0:T(8,128)(2,1)} custom-call(s32[2,24]{1,0:T(2,128)S(1)} %copy-done.10, s32[16]{0:T(128)S(1)} %copy-done.12, bf16[32,2048]{1,0:T(8,128)(2,1)S(1)} %copy-done.5, bf16[24,1,128,128]{3,2,1,0:T(8,128)(2,1)S(1)} %copy-done.3, bf16[24,1,128,128]{3,2,1,0:T(8,128)(2,1)S(1)} %copy-done.4), custom_call_target="tpu_custom_call" | custom-call | tf_op jit(solution)/shard_map/attention/pallas_call | solution.py:85
  7.0 8.4 %all-to-all-start = ((bf16[16,32,256]{2,1,0:T(8,128)(2,1)}), bf16[16,32,256]{2,1,0:T(8,128)(2,1)S(1)}, u32[]{:S(2)}, u32[]{:S(2)}) async-start(bf16[16,32,256]{2,1,0:T(8,128)(2,1)} %attention.1), calls=%async_computation | async-start | bytes 524288 | tf_op jit(solution)/shard_map/all_to_all | solution.py:339
  15.6 7.4 %all-to-all-done.got_ref = bf16[16,32,256]{2,1,0:T(8,128)(2,1)S(1)} async-done(((bf16[16,32,256]{2,1,0:T(8,128)(2,1)}), bf16[16,32,256]{2,1,0:T(8,128)(2,1)S(1)}, u32[]{:S(2)}, u32[]{:S(2)}) %all-to-all-start) | async-done | bytes 262176 | tf_op jit(solution)/shard_map/all_to_all | solution.py:339
  22.9 2.3 %copy-done.2 = bf16[1,1,128,16384]{3,2,1,0:T(8,128)(2,1)S(1)} copy-done((bf16[1,1,128,16384]{3,2,1,0:T(8,128)(2,1)S(1)}, bf16[1,1,128,16384]{3,2,1,0:T(8,128)(2,1)}, u32[]{:S(2)}) %copy-start.2) | copy-done | bytes 4194328
  27.8 3.1 %project.1 = (f32[16,32,512]{2,1,0:T(8,128)S(1)}, bf16[16,32,512]{2,1,0:T(8,128)(2,1)S(1)}) custom-call(s32[4]{0:T(128)S(1)} %pad_add_fusion.place, bf16[16,32,256]{2,1,0:T(8,128)(2,1)S(1)} %all-to-all-done.got_ref, bf16[32,2048]{1,0:T(8,128)(2,1)S(1)} %copy-done.6, bf16[32,128]{1,0:T(8,128)(2,1)S(1)} %copy-done.7, bf16[32,128]{1,0:T(8,128)(2,1)S(1)} %copy-done.8, ...), custom_call_target="tpu_custom_call" | custom-call | tf_op jit(solution)/shard_map/project/pallas_call | solution.py:139
  30.9 2.1 %collective-permute-start = (bf16[16,32,512]{2,1,0:T(8,128)(2,1)S(1)}, bf16[16,32,512]{2,1,0:T(8,128)(2,1)S(1)}, u32[]{:S(2)}, u32[]{:S(2)}) collective-permute-start(bf16[16,32,512]{2,1,0:T(8,128)(2,1)S(1)} %get-tuple-element.16), channel_id=1, source_target_pairs={{0,1},{1,0},{2,3},{3,2},{4,5},{5,4},{6,7},{7,6},{8,9},{9,8},{10,11... | collective-permute-start | bytes 1572872 | tf_op jit(solution)/shard_map/ppermute | solution.py:343
  33.0 1.5 %collective-permute-done.got_ref = bf16[16,32,512]{2,1,0:T(8,128)(2,1)S(1)} collective-permute-done((bf16[16,32,512]{2,1,0:T(8,128)(2,1)S(1)}, bf16[16,32,512]{2,1,0:T(8,128)(2,1)S(1)}, u32[]{:S(2)}, u32[]{:S(2)}) %collective-permute-start) | collective-permute-done | bytes 524320 | tf_op jit(solution)/shard_map/ppermute | solution.py:343
  34.6 13.5 %all_to_all.20.parts_ref = bf16[16,32,512]{2,1,0:T(8,128)(2,1)S(1)} all-to-all(bf16[16,32,512]{2,1,0:T(8,128)(2,1)S(1)} %add_pair.1), channel_id=1, replica_groups=mesh['kv'=16,'head'=8] {'kv'}, dimensions={0} | all-to-all | bytes 1048576 | tf_op jit(solution)/shard_map/all_to_all | solution.py:339
  48.8 1.4 %collective-permute-start.1 = (bf16[48,512]{1,0:T(8,128)(2,1)S(1)}, bf16[48,512]{1,0:T(8,128)(2,1)S(1)}, u32[]{:S(2)}, u32[]{:S(2)}) collective-permute-start(bf16[48,512]{1,0:T(8,128)(2,1)S(1)} %stream.1), channel_id=1, source_target_pairs={{0,2},{1,3},{2,0},{3,1},{4,6},{5,7},{6,4},{7,5},{8,10},{9,11},{10,... | collective-permute-start | bytes 147464 | tf_op jit(solution)/shard_map/ppermute | solution.py:343
  50.2 1.6 %collective-permute-done.1 = bf16[48,512]{1,0:T(8,128)(2,1)S(1)} collective-permute-done((bf16[48,512]{1,0:T(8,128)(2,1)S(1)}, bf16[48,512]{1,0:T(8,128)(2,1)S(1)}, u32[]{:S(2)}, u32[]{:S(2)}) %collective-permute-start.1) | collective-permute-done | bytes 49184 | tf_op jit(solution)/shard_map/ppermute | solution.py:343
  51.8 3.0 %collective-permute-start.2 = (bf16[48,512]{1,0:T(8,128)(2,1)S(1)}, bf16[48,512]{1,0:T(8,128)(2,1)S(1)}, u32[]{:S(2)}, u32[]{:S(2)}) collective-permute-start(bf16[48,512]{1,0:T(8,128)(2,1)S(1)} %add_convert_fusion.1), channel_id=1, source_target_pairs={{0,4},{1,5},{2,6},{3,7},{4,0},{5,1},{6,2},{7,3},{8,12},{9,13},{10,... | collective-permute-start | bytes 147464 | tf_op jit(solution)/shard_map/ppermute | solution.py:343
  54.8 1.7 %collective-permute-done.2 = bf16[48,512]{1,0:T(8,128)(2,1)S(1)} collective-permute-done((bf16[48,512]{1,0:T(8,128)(2,1)S(1)}, bf16[48,512]{1,0:T(8,128)(2,1)S(1)}, u32[]{:S(2)}, u32[]{:S(2)}) %collective-permute-start.2) | collective-permute-done | bytes 49184 | tf_op jit(solution)/shard_map/ppermute | solution.py:343
  56.5 4.3 %collective-permute-start.3 = (bf16[48,512]{1,0:T(8,128)(2,1)S(1)}, bf16[48,512]{1,0:T(8,128)(2,1)S(1)}, u32[]{:S(2)}, u32[]{:S(2)}) collective-permute-start(bf16[48,512]{1,0:T(8,128)(2,1)S(1)} %add_convert_fusion.mine_ref), channel_id=1, source_target_pairs={{0,1},{1,0},{2,3},{3,2},{4,5},{5,4},{6,7},{7,6},{8,9},{9,8},{10,11... | collective-permute-start | bytes 147464 | tf_op jit(solution)/shard_map/ppermute | solution.py:343
  61.7 2.9 %copy-done.1 = bf16[1024,3328]{1,0:T(8,128)(2,1)S(1)} copy-done((bf16[1024,3328]{1,0:T(8,128)(2,1)S(1)}, bf16[1024,3328]{1,0:T(8,128)(2,1)}, u32[]{:S(2)}) %copy-start.1) | copy-done | bytes 6815768
  64.7 5.5 %gate_up.1 = (bf16[16,4,3456]{2,1,0:T(4,128)(2,1)S(1)}, f32[32,128]{1,0:T(8,128)S(1)}) custom-call(s32[4]{0:T(128)S(1)} %pad_add_fusion.place, bf16[48,512]{1,0:T(8,128)(2,1)S(1)} %add_convert_fusion.mine_ref, bf16[48,512]{1,0:T(8,128)(2,1)S(1)} %collective-permute-done.3.other_ref, bf16[1024,3328]{1,0:T(8,128)(2,1)S(1)} %copy-done, ...), custom_call_target="tpu_custom_call" | custom-call | tf_op jit(solution)/shard_map/gate_up/pallas_call | solution.py:237
  70.2 11.2 %all_to_all.21.parts_ref = bf16[16,4,3456]{2,1,0:T(4,128)(2,1)S(1)} all-to-all(bf16[16,4,3456]{2,1,0:T(4,128)(2,1)S(1)} %get-tuple-element.18), channel_id=1, replica_groups=mesh['kv'=16,'head'=8] {'kv'}, dimensions={0} | all-to-all | bytes 884736 | tf_op jit(solution)/shard_map/all_to_all | solution.py:339
  81.6 11.3 %all_to_all.22.parts_ref = bf16[16,4,1664]{2,1,0:T(4,128)(2,1)S(1)} all-to-all(bf16[16,4,1664]{2,1,0:T(4,128)(2,1)S(1)} %hidden_units.1), channel_id=1, replica_groups=mesh['kv'=16,'head'=8] {'kv'}, dimensions={0} | all-to-all | bytes 425984 | tf_op jit(solution)/shard_map/all_to_all | solution.py:339
  92.9 3.4 %down.1 = (f32[4,32,128]{2,1,0:T(8,128)S(1)}, bf16[4,32,128]{2,1,0:T(8,128)(2,1)S(1)}) custom-call(s32[4]{0:T(128)S(1)} %pad_add_fusion.place, bf16[16,4,1664]{2,1,0:T(4,128)(2,1)S(1)} %all_to_all.22.parts_ref, bf16[3328,1024]{1,0:T(8,128)(2,1)S(1)} %bitcast.7), custom_call_target="tpu_custom_call" | custom-call | tf_op jit(solution)/shard_map/down/pallas_call | solution.py:303
  96.3 3.5 %collective-permute-start.4 = (bf16[4,32,128]{2,1,0:T(8,128)(2,1)S(1)}, bf16[4,32,128]{2,1,0:T(8,128)(2,1)S(1)}, u32[]{:S(2)}, u32[]{:S(2)}) collective-permute-start(bf16[4,32,128]{2,1,0:T(8,128)(2,1)S(1)} %get-tuple-element.20), channel_id=1, source_target_pairs={{0,1},{1,0},{2,3},{3,2},{4,5},{5,4},{6,7},{7,6},{8,9},{9,8},{10,11... | collective-permute-start | bytes 98312 | tf_op jit(solution)/shard_map/ppermute | solution.py:343
  101.3 1.4 %collective-permute-start.5 = (bf16[32,128]{1,0:T(8,128)(2,1)S(1)}, bf16[32,128]{1,0:T(8,128)(2,1)S(1)}, u32[]{:S(2)}, u32[]{:S(2)}) collective-permute-start(bf16[32,128]{1,0:T(8,128)(2,1)S(1)} %get-tuple-element.22), channel_id=1, source_target_pairs={{0,2},{1,3},{2,0},{3,1},{4,6},{5,7},{6,4},{7,5},{8,10},{9,11},{10,... | collective-permute-start | bytes 24584 | tf_op jit(solution)/shard_map/ppermute | solution.py:343
  102.7 3.0 %collective-permute-start.6 = (bf16[32,128]{1,0:T(8,128)(2,1)S(1)}, bf16[32,128]{1,0:T(8,128)(2,1)S(1)}, u32[]{:S(2)}, u32[]{:S(2)}) collective-permute-start(bf16[32,128]{1,0:T(8,128)(2,1)S(1)} %get-tuple-element.23), channel_id=1, source_target_pairs={{0,4},{1,5},{2,6},{3,7},{4,0},{5,1},{6,2},{7,3},{8,12},{9,13},{10,... | collective-permute-start | bytes 24584 | tf_op jit(solution)/shard_map/ppermute | solution.py:343
  106.8 2.6 %collective-permute-done.7 = bf16[32,128]{1,0:T(8,128)(2,1)S(1)} collective-permute-done((bf16[32,128]{1,0:T(8,128)(2,1)S(1)}, bf16[32,128]{1,0:T(8,128)(2,1)S(1)}, u32[]{:S(2)}, u32[]{:S(2)}) %collective-permute-start.7) | collective-permute-done | bytes 8224 | tf_op jit(solution)/shard_map/ppermute | solution.py:343
  (40 shorter events, 9.9 us)
Async XLA Ops:
  0.0 1.1 %copy-start.3 = (bf16[24,1,128,128]{3,2,1,0:T(8,128)(2,1)S(1)}, bf16[24,1,128,128]{3,2,1,0:T(8,128)(2,1)}, u32[]{:S(2)}) copy-start(bf16[24,1,128,128]{3,2,1,0:T(8,128)(2,1)} %k_ref.2) | copy-start | bytes 2359300
  1.1 1.1 %copy-start.4 = (bf16[24,1,128,128]{3,2,1,0:T(8,128)(2,1)S(1)}, bf16[24,1,128,128]{3,2,1,0:T(8,128)(2,1)}, u32[]{:S(2)}) copy-start(bf16[24,1,128,128]{3,2,1,0:T(8,128)(2,1)} %v_ref.2) | copy-start | bytes 2359300
  2.3 0.9 copy-start.5
  3.2 0.7 copy-start.10
  3.9 0.7 copy-start.12
  4.5 43.6 %copy-start.9 = (bf16[32,128]{1,0:T(8,128)(2,1)S(1)}, bf16[32,128]{1,0:T(8,128)(2,1)}, u32[]{:S(2)}) copy-start(bf16[32,128]{1,0:T(8,128)(2,1)} %res_ref.1) | copy-start | bytes 24580
  4.5 43.6 %copy-start.11 = (bf16[128]{0:T(256)(128)(2,1)S(1)}, bf16[128]{0:T(256)(128)(2,1)}, u32[]{:S(2)}) copy-start(bf16[128]{0:T(256)(128)(2,1)} %param.22) | copy-start | bytes 772
  7.0 15.9 %all-to-all-start = ((bf16[16,32,256]{2,1,0:T(8,128)(2,1)}), bf16[16,32,256]{2,1,0:T(8,128)(2,1)S(1)}, u32[]{:S(2)}, u32[]{:S(2)}) async-start(bf16[16,32,256]{2,1,0:T(8,128)(2,1)} %attention.1), calls=%async_computation | async-start | bytes 524288 | tf_op jit(solution)/shard_map/all_to_all | solution.py:339
  22.9 38.8 %copy-start = (bf16[1024,3328]{1,0:T(8,128)(2,1)S(1)}, bf16[1024,3328]{1,0:T(8,128)(2,1)}, u32[]{:S(2)}) copy-start(bf16[1024,3328]{1,0:T(8,128)(2,1)} %gate_ref.1) | copy-start | bytes 20447236
  22.9 2.3 %copy-start.2 = (bf16[1,1,128,16384]{3,2,1,0:T(8,128)(2,1)S(1)}, bf16[1,1,128,16384]{3,2,1,0:T(8,128)(2,1)}, u32[]{:S(2)}) copy-start(bf16[1,1,128,16384]{3,2,1,0:T(8,128)(2,1)} %param.21) | copy-start | bytes 12582916
  25.3 1.1 %copy-start.6 = (bf16[32,2048]{1,0:T(8,128)(2,1)S(1)}, bf16[32,2048]{1,0:T(8,128)(2,1)}, u32[]{:S(2)}) copy-start(bf16[32,2048]{1,0:T(8,128)(2,1)} %q_ref.3) | copy-start | bytes 393220
  26.4 0.7 copy-start.7
  27.1 0.7 copy-start.8
  30.9 3.6 %collective-permute-start = (bf16[16,32,512]{2,1,0:T(8,128)(2,1)S(1)}, bf16[16,32,512]{2,1,0:T(8,128)(2,1)S(1)}, u32[]{:S(2)}, u32[]{:S(2)}) collective-permute-start(bf16[16,32,512]{2,1,0:T(8,128)(2,1)S(1)} %get-tuple-element.16), channel_id=1, source_target_pairs={{0,1},{1,0},{2,3},{3,2},{4,5},{5,4},{6,7},{7,6},{8,9},{9,8},{10,11... | collective-permute-start | bytes 1572872 | tf_op jit(solution)/shard_map/ppermute | solution.py:343
  48.8 3.0 %collective-permute-start.1 = (bf16[48,512]{1,0:T(8,128)(2,1)S(1)}, bf16[48,512]{1,0:T(8,128)(2,1)S(1)}, u32[]{:S(2)}, u32[]{:S(2)}) collective-permute-start(bf16[48,512]{1,0:T(8,128)(2,1)S(1)} %stream.1), channel_id=1, source_target_pairs={{0,2},{1,3},{2,0},{3,1},{4,6},{5,7},{6,4},{7,5},{8,10},{9,11},{10,... | collective-permute-start | bytes 147464 | tf_op jit(solution)/shard_map/ppermute | solution.py:343
  51.8 4.7 %collective-permute-start.2 = (bf16[48,512]{1,0:T(8,128)(2,1)S(1)}, bf16[48,512]{1,0:T(8,128)(2,1)S(1)}, u32[]{:S(2)}, u32[]{:S(2)}) collective-permute-start(bf16[48,512]{1,0:T(8,128)(2,1)S(1)} %add_convert_fusion.1), channel_id=1, source_target_pairs={{0,4},{1,5},{2,6},{3,7},{4,0},{5,1},{6,2},{7,3},{8,12},{9,13},{10,... | collective-permute-start | bytes 147464 | tf_op jit(solution)/shard_map/ppermute | solution.py:343
  56.5 36.4 %slice-start = ((s8[6815744]{0:T(1024)(128)(4,1)}), s8[4194304]{0:T(1024)(128)(4,1)S(1)}, s32[]{:S(2)}) async-start(s8[6815744]{0:T(1024)(128)(4,1)} %bitcast.6), calls=%async_computation.4 | async-start | bytes 8388608
  56.5 36.4 %slice-start.1 = ((s8[6815744]{0:T(1024)(128)(4,1)}), s8[2621440]{0:T(1024)(128)(4,1)S(1)}, s32[]{:S(2)}) async-start(s8[6815744]{0:T(1024)(128)(4,1)} %bitcast.6), calls=%async_computation.5 | async-start | bytes 5242880
  56.5 5.2 %collective-permute-start.3 = (bf16[48,512]{1,0:T(8,128)(2,1)S(1)}, bf16[48,512]{1,0:T(8,128)(2,1)S(1)}, u32[]{:S(2)}, u32[]{:S(2)}) collective-permute-start(bf16[48,512]{1,0:T(8,128)(2,1)S(1)} %add_convert_fusion.mine_ref), channel_id=1, source_target_pairs={{0,1},{1,0},{2,3},{3,2},{4,5},{5,4},{6,7},{7,6},{8,9},{9,8},{10,11... | collective-permute-start | bytes 147464 | tf_op jit(solution)/shard_map/ppermute | solution.py:343
  61.7 2.9 %copy-start.1 = (bf16[1024,3328]{1,0:T(8,128)(2,1)S(1)}, bf16[1024,3328]{1,0:T(8,128)(2,1)}, u32[]{:S(2)}) copy-start(bf16[1024,3328]{1,0:T(8,128)(2,1)} %up_ref.1) | copy-start | bytes 20447236
  96.3 4.4 %collective-permute-start.4 = (bf16[4,32,128]{2,1,0:T(8,128)(2,1)S(1)}, bf16[4,32,128]{2,1,0:T(8,128)(2,1)S(1)}, u32[]{:S(2)}, u32[]{:S(2)}) collective-permute-start(bf16[4,32,128]{2,1,0:T(8,128)(2,1)S(1)} %get-tuple-element.20), channel_id=1, source_target_pairs={{0,1},{1,0},{2,3},{3,2},{4,5},{5,4},{6,7},{7,6},{8,9},{9,8},{10,11... | collective-permute-start | bytes 98312 | tf_op jit(solution)/shard_map/ppermute | solution.py:343
  101.3 4.4 %collective-permute-start.5 = (bf16[32,128]{1,0:T(8,128)(2,1)S(1)}, bf16[32,128]{1,0:T(8,128)(2,1)S(1)}, u32[]{:S(2)}, u32[]{:S(2)}) collective-permute-start(bf16[32,128]{1,0:T(8,128)(2,1)S(1)} %get-tuple-element.22), channel_id=1, source_target_pairs={{0,2},{1,3},{2,0},{3,1},{4,6},{5,7},{6,4},{7,5},{8,10},{9,11},{10,... | collective-permute-start | bytes 24584 | tf_op jit(solution)/shard_map/ppermute | solution.py:343
  102.7 4.2 %collective-permute-start.6 = (bf16[32,128]{1,0:T(8,128)(2,1)S(1)}, bf16[32,128]{1,0:T(8,128)(2,1)S(1)}, u32[]{:S(2)}, u32[]{:S(2)}) collective-permute-start(bf16[32,128]{1,0:T(8,128)(2,1)S(1)} %get-tuple-element.23), channel_id=1, source_target_pairs={{0,4},{1,5},{2,6},{3,7},{4,0},{5,1},{6,2},{7,3},{8,12},{9,13},{10,... | collective-permute-start | bytes 24584 | tf_op jit(solution)/shard_map/ppermute | solution.py:343
  105.7 3.7 %collective-permute-start.7 = (bf16[32,128]{1,0:T(8,128)(2,1)S(1)}, bf16[32,128]{1,0:T(8,128)(2,1)S(1)}, u32[]{:S(2)}, u32[]{:S(2)}) collective-permute-start(bf16[32,128]{1,0:T(8,128)(2,1)S(1)} %get-tuple-element.24), channel_id=1, source_target_pairs={{0,6},{1,7},{2,4},{3,5},{4,2},{5,3},{6,0},{7,1},{8,14},{9,15},{10,... | collective-permute-start | bytes 24584 | tf_op jit(solution)/shard_map/ppermute | solution.py:343

commit v2 on v1

v2 whole, which is shorter than its diff:
```python
import functools
import math

import jax
import jax.numpy as jnp
from jax import lax
from jax.experimental import pallas as pl
from jax.experimental.pallas import tpu as pltpu
from jax.sharding import PartitionSpec as P

HQ = 128
KVH = 8
SEQS = 16
ROWS = 2 * SEQS
GROUP = HQ // KVH
HD = 128
SLOTS = 24
OWN = 128
HALF = 4 * OWN
N_KV = 16
UNITS = 3328
PART = UNITS // 2
EXTRA = 128
TILE = 256

F32 = jnp.float32
BF16 = jnp.bfloat16
MIB = 1 << 20
W_SPACE = pltpu.HBM


def whole(shape, space=pltpu.VMEM):
    zeros = (0,) * len(shape)
    return pl.BlockSpec(shape, lambda *_: zeros, memory_space=space)


def is_even():
    return lax.axis_index("head") % 2 == 0


def own_y():
    return lax.axis_index("head") // 2


def params(mib, steps=0):
    kinds = ("arbitrary",) * steps if steps else None
    return pltpu.CompilerParams(vmem_limit_bytes=mib * MIB, dimension_semantics=kinds)


def in_hbm(array):
    return pltpu.with_memory_space_constraint(array, pltpu.HBM)


def cost(flops, moved):
    return pl.CostEstimate(flops=flops, bytes_accessed=moved, transcendentals=0)


def shape(dims, kind):
    return jax.ShapeDtypeStruct(dims, kind)


def parts_of_copy(src, dst, sems):
    count = sems.shape[0]
    deep = dst.shape[0] // count
    return [
        pltpu.make_async_copy(
            src.at[i * deep : (i + 1) * deep, :], dst.at[i * deep : (i + 1) * deep, :], sems.at[i]
        )
        for i in range(count)
    ]


def attention_kernel(
    table_hbm, lengths_hbm, q_hbm, k_hbm, v_hbm, new_k_hbm, new_v_hbm, w_hbm,
    out_ref, w_ref, table, lengths, q_ref, k_ref, v_ref, new_k, new_v, sems, w_sems,
    q_rows, scores, tops, sums, numer,
):
    pairs = (
        (table_hbm, table), (lengths_hbm, lengths), (q_hbm, q_ref), (k_hbm, k_ref), (v_hbm, v_ref),
        (new_k_hbm, new_k), (new_v_hbm, new_v),
    )
    copies = [pltpu.make_async_copy(src, dst, sems.at[i]) for i, (src, dst) in enumerate(pairs)]
    for i in (2, 0, 1, 5, 6, 3, 4):
        copies[i].start()
    w_copies = parts_of_copy(w_hbm, w_ref, w_sems)
    for copy in w_copies:
        copy.start()
    tops[...] = jnp.full(tops.shape, -1e30, F32)
    sums[...] = jnp.zeros(sums.shape, F32)
    numer[...] = jnp.zeros(numer.shape, F32)
    lane = lax.broadcasted_iota(jnp.int32, (ROWS, HD), 1)
    unit = 1.0 / math.sqrt(HD)
    copies[2].wait()
    for g in range(GROUP):
        q_rows[pl.ds(g, ROWS, stride=GROUP), :] = q_ref[:, g * HD : (g + 1) * HD].astype(F32)
    copies[5].wait()
    copies[6].wait()
    mine = pl.ds(lax.axis_index("kv"), ROWS, stride=GROUP)
    query = q_rows[mine, :]
    keys, values = new_k[...].astype(F32), new_v[...].astype(F32)
    odd = lax.broadcasted_iota(jnp.int32, (ROWS, 1), 0) % 2 == 1
    at_own = jnp.sum(query * keys, axis=1, keepdims=True) * unit
    at_prev = jnp.sum(query * pltpu.roll(keys, 1, 0), axis=1, keepdims=True) * unit
    new_max = jnp.where(odd, jnp.maximum(at_own, at_prev), at_own)
    expo_own = jnp.exp(at_own - new_max)
    expo_prev = jnp.where(odd, jnp.exp(at_prev - new_max), 0.0)
    new_out = expo_own.astype(BF16).astype(F32) * values
    new_out += expo_prev.astype(BF16).astype(F32) * pltpu.roll(values, 1, 0)
    tops[mine, :] = jnp.broadcast_to(new_max, (ROWS, HD))
    copies[0].wait()
    copies[1].wait()
    copies[3].wait()
    rows_of = []
    for b in range(SLOTS):
        seq = table[0, b]
        limit = lengths[seq] - table[1, b] * HD
        here = pl.ds(pl.multiple_of(seq * ROWS, ROWS), ROWS)
        rows_of.append(here)
        raw = lax.dot_general(
            q_rows[here, :].astype(BF16), k_ref[b, 0], (((1,), (1,)), ((), ())),
            preferred_element_type=F32,
        )
        masked = jnp.where(lane < limit, raw * unit, -1e30)
        scores[b] = masked
        tops[here, :] = jnp.maximum(tops[here, :], jnp.max(masked, axis=1, keepdims=True))
    tops[...] = tops[...].astype(BF16).astype(F32)
    new_scale = jnp.exp(new_max - tops[mine, :])
    sums[mine, :] = new_scale * (expo_own + expo_prev)
    numer[mine, :] = new_scale * new_out
    copies[4].wait()
    for b in range(SLOTS):
        here = rows_of[b]
        masked = scores[b]
        expo = jnp.where(masked > -1e29, jnp.exp(masked - tops[here, :]), 0.0)
        sums[here, :] += jnp.sum(expo, axis=1, keepdims=True)
        numer[here, :] += jnp.dot(expo.astype(BF16), v_ref[b, 0], preferred_element_type=F32)
    by_head = lax.broadcasted_iota(jnp.int32, (GROUP, HD), 1)
    stats = jnp.zeros((GROUP, HD), F32)
    for row in range(ROWS):
        heads = slice(row * GROUP, (row + 1) * GROUP)
        high = sums[heads, :].astype(BF16).astype(F32)
        stats = jnp.where(by_head == row, tops[heads, :], stats)
        stats = jnp.where(by_head == row + ROWS, high, stats)
        stats = jnp.where(by_head == row + 2 * ROWS, sums[heads, :] - high, stats)
    for g in range(GROUP):
        out_ref[g, :ROWS, :] = numer[pl.ds(g, ROWS, stride=GROUP), :].astype(BF16)
        out_ref[g, ROWS:, :] = jnp.broadcast_to(stats[g : g + 1, :], (16, HD)).astype(BF16)
    for copy in w_copies:
        copy.wait()


def attention_partials(
    table, lengths, queries, key_cache, value_cache, new_keys, new_values, weight
):
    tall = pltpu.VMEM((ROWS * GROUP, HD), F32)
    arrays = (queries, key_cache, value_cache, new_keys, new_values)
    return pl.pallas_call(
        attention_kernel,
        out_shape=[shape((GROUP, ROWS + 16, HD), BF16), shape(weight.shape, BF16)],
        in_specs=[pl.BlockSpec(memory_space=W_SPACE)] * 8,
        out_specs=[whole((GROUP, ROWS + 16, HD)), whole(weight.shape)],
        scratch_shapes=[pltpu.SMEM(table.shape, jnp.int32), pltpu.SMEM(lengths.shape, jnp.int32)]
        + [pltpu.VMEM(a.shape, BF16) for a in arrays]
        + [pltpu.SemaphoreType.DMA((7,)), pltpu.SemaphoreType.DMA((8,))]
        + [tall, pltpu.VMEM((SLOTS, ROWS, HD), F32), tall, tall, tall],
        compiler_params=params(16),
        cost_estimate=cost(SLOTS * ROWS * HD * HD * 4, 4 * SLOTS * HD * HD),
        name="attention",
    )(*[in_hbm(a) for a in (table, lengths, *arrays, weight)])


def project_kernel(got_ref, w_ref, keep_ref, give_ref):
    row = lax.broadcasted_iota(jnp.int32, (N_KV, HD), 0)
    stats = jnp.zeros((N_KV, HD), F32)
    for i in range(N_KV):
        stats = jnp.where(row == i, got_ref[i, ROWS:, :].astype(F32), stats)
    stats = jnp.concatenate([stats, jnp.zeros((HD - N_KV, HD), F32)], axis=0).T
    maxes = stats[:ROWS]
    lane = lax.broadcasted_iota(jnp.int32, (ROWS, HD), 1)
    real = lane < N_KV
    peak = jnp.max(jnp.where(real, maxes, -1e30), axis=1, keepdims=True)
    scales = jnp.where(real, jnp.exp(maxes - peak), 0.0)
    denom = jnp.sum(scales * (stats[ROWS : 2 * ROWS] + stats[2 * ROWS : 3 * ROWS]), axis=1, keepdims=True)
    total = jnp.zeros((ROWS, HD), F32)
    for i in range(N_KV):
        total += scales[:, i : i + 1] * got_ref[i, :ROWS, :].astype(F32)
    attn = (total / denom).astype(BF16)
    even = is_even()
    for d in range(N_KV):
        for y in range(4):
            at = d * 2 * HALF + y * TILE
            both = jnp.dot(attn, w_ref[:, at : at + TILE], preferred_element_type=F32)
            here = slice(y * OWN, (y + 1) * OWN)
            keep_ref[d, :, here] = jnp.where(even, both[:, :OWN], both[:, OWN:])
            give_ref[d, :, here] = jnp.where(even, both[:, OWN:], both[:, :OWN]).astype(BF16)


def project(got, weight):
    out = (N_KV, ROWS, HALF)
    return pl.pallas_call(
        project_kernel,
        out_shape=[shape(out, F32), shape(out, BF16)],
        in_specs=[whole(got.shape), whole(weight.shape)],
        out_specs=[whole(out), whole(out)],
        compiler_params=params(8),
        cost_estimate=cost(2 * ROWS * weight.size, 2 * weight.size),
        name="project",
    )(got, weight)


def pair_kernel(keep_ref, got_ref, out_ref):
    out_ref[...] = (keep_ref[...] + got_ref[...].astype(F32)).astype(BF16)


def add_pair(keep, got):
    return pl.pallas_call(
        pair_kernel,
        out_shape=shape(keep.shape, BF16),
        in_specs=[whole(keep.shape), whole(got.shape)],
        out_specs=whole(keep.shape),
        compiler_params=params(8),
        name="add_pair",
    )(keep, got)


def stream_kernel(parts_ref, res_ref, gain_ref, out_ref):
    total = parts_ref[0].astype(F32)
    for i in range(1, N_KV):
        total += parts_ref[i].astype(F32)
    me = own_y()
    blocks = []
    for y in range(4):
        rest = jnp.where(me == y, res_ref[...].astype(F32), 0.0)
        blocks.append(total[:, y * OWN : (y + 1) * OWN] + rest)
    row = lax.broadcasted_iota(jnp.int32, (ROWS, OWN), 0)
    blocks.append(jnp.where(row == me, gain_ref[...].astype(F32), 0.0))
    out_ref[...] = jnp.concatenate(blocks, axis=1).astype(BF16)


def stream(parts, residual, gain):
    out = (ROWS, HALF + OWN)
    return pl.pallas_call(
        stream_kernel,
        out_shape=shape(out, BF16),
        in_specs=[whole(a.shape) for a in (parts, residual, gain)],
        out_specs=whole(out),
        compiler_params=params(8),
        name="stream",
    )(parts, residual, gain)


def gate_kernel(mine_ref, other_ref, gate_a, gate_b, up_a, up_b, out_ref, own_ref):
    tiles = UNITS // TILE
    deep = gate_a.shape[0]
    even = is_even()
    mine, other = mine_ref[...].astype(F32), other_ref[...].astype(F32)
    halves = (jnp.where(even, mine, other), jnp.where(even, other, mine))
    square = jnp.zeros((ROWS, OWN), F32)
    own = jnp.zeros((ROWS, OWN), F32)
    blocks = []
    for y in range(4):
        for c in range(2):
            block = halves[c][:, y * OWN : (y + 1) * OWN]
            gain = halves[c][y : y + 1, HALF:]
            blocks.append((block * gain).astype(BF16))
            square += block * block
        own += jnp.where(own_y() == y, mine[:, y * OWN : (y + 1) * OWN], 0.0)
    own_ref[...] = own
    x = jnp.concatenate(blocks, axis=1)
    total = jnp.sum(square, axis=1, keepdims=True)
    high = total.astype(BF16).astype(F32)
    lane = lax.broadcasted_iota(jnp.int32, (ROWS, EXTRA), 1)
    squares = jnp.where(lane < 64, high, total - high).astype(BF16).astype(F32)
    for d in range(N_KV):
        out_ref[d, :, 2 * PART :] = squares[4 * (d // 2) : 4 * (d // 2) + 4, :].astype(BF16)
    for tile in range(tiles):
        for which in range(2):
            upper, lower = ((gate_a, gate_b), (up_a, up_b))[which]
            lanes = slice(tile * TILE, (tile + 1) * TILE)
            result = jnp.dot(x[:, :deep], upper[:, lanes], preferred_element_type=F32)
            result += jnp.dot(x[:, deep:], lower[:, lanes], preferred_element_type=F32)
            for part in range(2):
                column = 2 * tile + part
                at = which * PART + column % 13 * 128
                for r in range(8):
                    piece = result[4 * r : 4 * r + 4, part * 128 : (part + 1) * 128]
                    out_ref[2 * r + column // 13, :, at : at + 128] = piece.astype(BF16)


def gate_up(mine, other, gates, ups):
    wide = (N_KV, 4, 2 * PART + EXTRA)
    return pl.pallas_call(
        gate_kernel,
        out_shape=[shape(wide, BF16), shape((ROWS, OWN), F32)],
        in_specs=[whole(a.shape) for a in (mine, other, *gates, *ups)],
        out_specs=[whole(wide), whole((ROWS, OWN))],
        compiler_params=params(8),
        cost_estimate=cost(8 * ROWS * gates[0].size, 8 * gates[0].size),
        name="gate_up",
    )(mine, other, *gates, *ups)


def load_kernel(start, after_ref, w_hbm, out_ref, sems):
    copies = parts_of_copy(w_hbm.at[start : start + out_ref.shape[0], :], out_ref, sems)
    for copy in copies:
        copy.start()
    for copy in copies:
        copy.wait()


def load(weight, half, after):
    rows = weight.shape[0] // 2
    return pl.pallas_call(
        functools.partial(load_kernel, half * rows),
        out_shape=shape((rows, weight.shape[1]), BF16),
        in_specs=[pl.BlockSpec(memory_space=pl.ANY), pl.BlockSpec(memory_space=W_SPACE)],
        out_specs=whole((rows, weight.shape[1])),
        scratch_shapes=[pltpu.SemaphoreType.DMA((8,))],
        compiler_params=params(8),
        cost_estimate=cost(0, 2 * weight.size),
        name="load",
    )(after, in_hbm(weight))


def hidden_kernel(parts_ref, out_ref):
    total = parts_ref[0].astype(F32)
    for i in range(1, N_KV):
        total += parts_ref[i].astype(F32)
    squares = total[:, 2 * PART : 2 * PART + 1] + total[:, 2 * PART + 64 : 2 * PART + 65]
    scale = lax.rsqrt(squares / (HQ * HD) + 1e-05)
    gate, up = total[:, :PART] * scale, total[:, PART : 2 * PART] * scale
    hidden = (gate / (1.0 + jnp.exp(-gate)) * up).astype(BF16)
    for i in range(N_KV):
        out_ref[i] = hidden


def hidden_units(parts):
    return pl.pallas_call(
        hidden_kernel,
        out_shape=shape((N_KV, 4, PART), BF16),
        in_specs=[whole(parts.shape)],
        out_specs=whole((N_KV, 4, PART)),
        compiler_params=params(8),
        name="hidden_units",
    )(parts)


def down_kernel(parts_ref, w_ref, out_ref, x):
    for d in range(N_KV):
        x[4 * (d // 2) : 4 * (d // 2) + 4, d % 2 * PART : d % 2 * PART + PART] = parts_ref[d].astype(F32)
    total = jnp.dot(x[...].astype(BF16), w_ref[...], preferred_element_type=F32)
    for i in range(KVH):
        out_ref[i] = total[:, i * OWN : (i + 1) * OWN].astype(BF16)


def down(parts, w_down):
    out = (KVH, ROWS, OWN)
    return pl.pallas_call(
        down_kernel,
        out_shape=shape(out, BF16),
        in_specs=[whole(parts.shape), whole(w_down.shape)],
        out_specs=whole(out),
        scratch_shapes=[pltpu.VMEM((ROWS, UNITS), F32)],
        compiler_params=params(8),
        cost_estimate=cost(2 * ROWS * w_down.size, 2 * w_down.size),
        name="down",
    )(parts, w_down)


def finish_kernel(own_ref, parts_ref, out_ref):
    total = own_ref[...]
    for i in range(KVH):
        total += parts_ref[i].astype(F32)
    out_ref[...] = total.astype(BF16)


def finish(own, parts):
    return pl.pallas_call(
        finish_kernel,
        out_shape=shape(own.shape, BF16),
        in_specs=[whole(own.shape), whole(parts.shape)],
        out_specs=whole(own.shape),
        compiler_params=params(8),
        name="finish",
    )(own, parts)


def exchange(value, axis):
    return lax.all_to_all(value, axis, 0, 0, tiled=True)


def swap(value, step):
    return lax.ppermute(value, "head", [(j, j ^ step) for j in range(KVH)])


def swap_beside(value, step, weight, half):
    return lax.optimization_barrier((swap(value, step), load(weight, half, value)))


def on_device(
    queries,
    key_cache,
    value_cache,
    block_table,
    lengths,
    new_keys,
    new_values,
    residual,
    out_weight,
    norm_gain,
    w_gate,
    w_up,
    w_down,
):
    partials, weight = attention_partials(
        block_table, lengths, queries, key_cache, value_cache, new_keys, new_values, out_weight[0, 0]
    )
    keep, give = project(exchange(partials, "kv"), weight)
    swapped, up_a = swap_beside(give, 1, w_up, 0)
    parts = exchange(add_pair(keep, swapped), "kv")
    here = stream(parts, residual, norm_gain[None])
    swapped, up_b = swap_beside(here, 2, w_up, 1)
    here = (here.astype(F32) + swapped.astype(F32)).astype(BF16)
    swapped, gate_a = swap_beside(here, 6, w_gate, 0)
    here = (here.astype(F32) + swapped.astype(F32)).astype(BF16)
    other, gate_b = swap_beside(here, 1, w_gate, 1)
    gates, own = gate_up(here, other, (gate_a, gate_b), (up_a, up_b))
    hidden = exchange(hidden_units(exchange(gates, "kv")), "kv")
    parts = exchange(down(hidden, w_down), "head")
    return finish(own, parts)


def solution(mesh):
    in_specs = (
        P(None, "head"),
        P("kv", "head", None, None),
        P("kv", "head", None, None),
        P(None, "kv"),
        P(),
        P(None, "head"),
        P(None, "head"),
        P(None, ("kv", "head")),
        P("head", "kv", None, None),
        P(("kv", "head")),
        P("kv", "head"),
        P("kv", "head"),
        P("head", "kv"),
    )
    out_specs = P(None, ("kv", "head"))
    return jax.shard_map(
        on_device, mesh=mesh, in_specs=in_specs, out_specs=out_specs, check_vma=False
    )
```

time: 111 us -> 91.3 us (0.82)
  blocking collectives: 36 us -> 63.7 us
  waiting for transfers between devices: 17.7 us -> 0.01 us
  starting transfers between devices: 27.2 us -> 9.83 us
  local copies, waits for them, and re-layouts: 12.3 us -> 0.02 us
  Pallas kernels: 16 us -> 17.2 us
    all_to_all x3 -> x5, blocking collectives: 36 us -> 63.7 us  [exchange(): return lax.all_to_all(value, axis, 0, 0, tiled=True)]
    unnamed x30 -> x8, local copies, waits for them, and re-layouts: 12.3 us -> 0.02 us
    ppermute x8 -> x4, waiting for transfers between devices: 10.3 us -> 0.01 us  [swap(): return lax.ppermute(value, 'head', [(j, j ^ step) for j in range(KVH)])]
    ppermute x8 -> x4, starting transfers between devices: 18.7 us -> 9.83 us  [swap(): return lax.ppermute(value, 'head', [(j, j ^ step) for j in range(KVH)])]
    all_to_all x1 -> x0, starting transfers between devices: 8.44 us -> none  [exchange(): return lax.all_to_all(value, axis, 0, 0, tiled=True)]
    all_to_all x1 -> x0, waiting for transfers between devices: 7.36 us -> none  [exchange(): return lax.all_to_all(value, axis, 0, 0, tiled=True)]
    pallas_call x6 -> x10, Pallas kernels: 15.7 us -> 16.9 us  [the longest x4 8.04 us: load(): pl.pallas_call(functools.partial(load_kernel, half * rows), out_shape=sha...]
  transfers between devices with their start and end apart: 9 -> 4, of which waited for: 8 -> 0; matrix products, arithmetic and copies ran while one was open for 0% -> 0% of each run, Pallas kernels for 0% -> 9%
where the time goes in v2:
time: 91.3 us; the launch traced here: 90.9 us
  blocking collectives  63.7 us (70%)
  Pallas kernels  17.2 us (19%)
  starting transfers between devices  9.83 us (11%)
    all_to_all x5, blocking collectives, exchange(): return lax.all_to_all(value, axis, 0, 0, tiled=True)  63.7 us
    ppermute x4, starting transfers between devices, swap(): return lax.ppermute(value, 'head', [(j, j ^ step) for j in range(KVH)])  9.83 us
    pallas_call x4, Pallas kernels, load(): pl.pallas_call(functools.partial(load_kernel, half * rows), out_shape=sha...  8.04 us
    pallas_call x1, Pallas kernels, attention_partials(): pl.pallas_call(attention_kernel, out_shape=[shape((GROUP, ROWS + 16, HD),...  3.39 us
    pallas_call x1, Pallas kernels, gate_up(): pl.pallas_call(gate_kernel, out_shape=[shape(wide, BF16), shape((ROWS, OW...  2.48 us
  transfers between devices with their start and end apart: 4, of which 0 were waited for; matrix products, arithmetic and copies ran while one was open for 0% of the time, Pallas kernels for 9%

profile of v2, /device:TPU:1, one launch (start us, length us, event | category | flops | bytes accessed | tf_op | source)
XLA Modules:
  0.0 90.9 jit_solution(17545341270214922075)
XLA Ops:
  0.0 3.4 %attention.1 = (bf16[16,48,128]{2,1,0:T(8,128)(2,1)S(1)}, bf16[128,16384]{1,0:T(8,128)(2,1)S(1)}) custom-call(s32[2,24]{1,0:T(2,128)} %table_hbm.1, s32[16]{0:T(128)} %lengths_hbm.1, bf16[32,2048]{1,0:T(8,128)(2,1)} %q_hbm.1, bf16[24,1,128,128]{3,2,1,0:T(8,128)(2,1)} %k_hbm.1, bf16[24,1,128,128]{3,2,1,0:T(8,128)(2,1)} %v_hbm.1, bf16[32,128]{1,0:T(8,128)(2,1)} %new_k_hbm.1, ...), custom_call_target="tpu_custom_call" | custom-call | flops 50331648 | bytes 1572864 | tf_op jit(solution)/shard_map/attention/pallas_call | solution.py:157
  3.4 15.4 %all_to_all.25.got_ref = bf16[16,48,128]{2,1,0:T(8,128)(2,1)S(1)} all-to-all(bf16[16,48,128]{2,1,0:T(8,128)(2,1)S(1)} %get-tuple-element.19), channel_id=1, replica_groups=mesh['kv'=16,'head'=8] {'kv'}, dimensions={0} | all-to-all | bytes 393216 | tf_op jit(solution)/shard_map/all_to_all | solution.py:389
  18.8 1.1 %project.1 = (f32[16,32,512]{2,1,0:T(8,128)S(1)}, bf16[16,32,512]{2,1,0:T(8,128)(2,1)S(1)}) custom-call(bf16[16,48,128]{2,1,0:T(8,128)(2,1)S(1)} %all_to_all.25.got_ref, bf16[128,16384]{1,0:T(8,128)(2,1)S(1)} %get-tuple-element.20.w_ref), custom_call_target="tpu_custom_call" | custom-call | flops 134217728 | bytes 4194304 | tf_op jit(solution)/shard_map/project/pallas_call | solution.py:200
  19.8 0.0 copy-start
  19.8 0.0 copy-start.1
  19.8 2.1 %collective-permute-start = (bf16[16,32,512]{2,1,0:T(8,128)(2,1)S(1)}, bf16[16,32,512]{2,1,0:T(8,128)(2,1)S(1)}, u32[]{:S(2)}, u32[]{:S(2)}) collective-permute-start(bf16[16,32,512]{2,1,0:T(8,128)(2,1)S(1)} %get-tuple-element.22.after_ref), channel_id=1, source_target_pairs={{0,1},{1,0},{2,3},{3,2},{4,5},{5,4},{6,7},{7,6},{8,9},{9,8},{10,11... | collective-permute-start | bytes 1572872 | tf_op jit(solution)/shard_map/ppermute | solution.py:393
  21.9 2.0 %load.4.up_a = bf16[512,3328]{1,0:T(8,128)(2,1)S(1)} custom-call(bf16[16,32,512]{2,1,0:T(8,128)(2,1)S(1)} %get-tuple-element.22.after_ref, bf16[1024,3328]{1,0:T(8,128)(2,1)} %w_hbm.5), custom_call_target="tpu_custom_call" | custom-call | bytes 6815744 | tf_op jit(solution)/shard_map/load/pallas_call | solution.py:313
  23.9 0.1 add_pair.1
  24.0 13.3 %all_to_all.26.parts_ref = bf16[16,32,512]{2,1,0:T(8,128)(2,1)S(1)} all-to-all(bf16[16,32,512]{2,1,0:T(8,128)(2,1)S(1)} %add_pair.1), channel_id=1, replica_groups=mesh['kv'=16,'head'=8] {'kv'}, dimensions={0} | all-to-all | bytes 1048576 | tf_op jit(solution)/shard_map/all_to_all | solution.py:389
  37.3 0.1 stream.1.after_ref
  37.4 1.4 %collective-permute-start.1 = (bf16[32,640]{1,0:T(8,128)(2,1)S(1)}, bf16[32,640]{1,0:T(8,128)(2,1)S(1)}, u32[]{:S(2)}, u32[]{:S(2)}) collective-permute-start(bf16[32,640]{1,0:T(8,128)(2,1)S(1)} %stream.1.after_ref), channel_id=1, source_target_pairs={{0,2},{1,3},{2,0},{3,1},{4,6},{5,7},{6,4},{7,5},{8,10},{9,11},{10,... | collective-permute-start | bytes 122888 | tf_op jit(solution)/shard_map/ppermute | solution.py:393
  38.7 2.0 %load.5.up_b = bf16[512,3328]{1,0:T(8,128)(2,1)S(1)} custom-call(bf16[32,640]{1,0:T(8,128)(2,1)S(1)} %stream.1.after_ref, bf16[1024,3328]{1,0:T(8,128)(2,1)} %w_hbm.5), custom_call_target="tpu_custom_call" | custom-call | bytes 6815744 | tf_op jit(solution)/shard_map/load/pallas_call | solution.py:313
  40.7 2.4 %collective-permute-start.2 = (bf16[32,640]{1,0:T(8,128)(2,1)S(1)}, bf16[32,640]{1,0:T(8,128)(2,1)S(1)}, u32[]{:S(2)}, u32[]{:S(2)}) collective-permute-start(bf16[32,640]{1,0:T(8,128)(2,1)S(1)} %add_convert_fusion.1.after_ref), channel_id=1, source_target_pairs={{0,6},{1,7},{2,4},{3,5},{4,2},{5,3},{6,0},{7,1},{8,14},{9,15},{10,... | collective-permute-start | bytes 122888 | tf_op jit(solution)/shard_map/ppermute | solution.py:393
  43.1 2.0 %load.6.gate_a = bf16[512,3328]{1,0:T(8,128)(2,1)S(1)} custom-call(bf16[32,640]{1,0:T(8,128)(2,1)S(1)} %add_convert_fusion.1.after_ref, bf16[1024,3328]{1,0:T(8,128)(2,1)} %w_hbm.7), custom_call_target="tpu_custom_call" | custom-call | bytes 6815744 | tf_op jit(solution)/shard_map/load/pallas_call | solution.py:313
  45.1 4.0 %collective-permute-start.3 = (bf16[32,640]{1,0:T(8,128)(2,1)S(1)}, bf16[32,640]{1,0:T(8,128)(2,1)S(1)}, u32[]{:S(2)}, u32[]{:S(2)}) collective-permute-start(bf16[32,640]{1,0:T(8,128)(2,1)S(1)} %add_convert_fusion.after_ref.mine_ref), channel_id=1, source_target_pairs={{0,1},{1,0},{2,3},{3,2},{4,5},{5,4},{6,7},{7,6},{8,9},{9,8},{10,11... | collective-permute-start | bytes 122888 | tf_op jit(solution)/shard_map/ppermute | solution.py:393
  49.2 2.1 %load.7.gate_b = bf16[512,3328]{1,0:T(8,128)(2,1)S(1)} custom-call(bf16[32,640]{1,0:T(8,128)(2,1)S(1)} %add_convert_fusion.after_ref.mine_ref, bf16[1024,3328]{1,0:T(8,128)(2,1)} %w_hbm.7), custom_call_target="tpu_custom_call" | custom-call | bytes 6815744 | tf_op jit(solution)/shard_map/load/pallas_call | solution.py:313
  51.3 0.0 slice-start.1
  51.3 2.5 %gate_up.1 = (bf16[16,4,3456]{2,1,0:T(4,128)(2,1)S(1)}, f32[32,128]{1,0:T(8,128)S(1)}) custom-call(bf16[32,640]{1,0:T(8,128)(2,1)S(1)} %add_convert_fusion.after_ref.mine_ref, bf16[32,640]{1,0:T(8,128)(2,1)S(1)} %collective-permute-done.3.other_ref, bf16[512,3328]{1,0:T(8,128)(2,1)S(1)} %load.6.gate_a, bf16[512,3328]{1,0:T(8,128)(2,1)S(1)} %load.7.gate_b, ...), custom_call_target="tpu_custom_call" | custom-call | flops 436207616 | bytes 13631488 | tf_op jit(solution)/shard_map/gate_up/pallas_call | solution.py:292
  53.8 12.4 %all_to_all.27.parts_ref = bf16[16,4,3456]{2,1,0:T(4,128)(2,1)S(1)} all-to-all(bf16[16,4,3456]{2,1,0:T(4,128)(2,1)S(1)} %get-tuple-element.32), channel_id=1, replica_groups=mesh['kv'=16,'head'=8] {'kv'}, dimensions={0} | all-to-all | bytes 884736 | tf_op jit(solution)/shard_map/all_to_all | solution.py:389
  66.2 0.2 hidden_units.1
  66.5 11.0 %all_to_all.28.parts_ref = bf16[16,4,1664]{2,1,0:T(4,128)(2,1)S(1)} all-to-all(bf16[16,4,1664]{2,1,0:T(4,128)(2,1)S(1)} %hidden_units.1), channel_id=1, replica_groups=mesh['kv'=16,'head'=8] {'kv'}, dimensions={0} | all-to-all | bytes 425984 | tf_op jit(solution)/shard_map/all_to_all | solution.py:389
  77.5 1.3 %down.1 = bf16[8,32,128]{2,1,0:T(8,128)(2,1)S(1)} custom-call(bf16[16,4,1664]{2,1,0:T(4,128)(2,1)S(1)} %all_to_all.28.parts_ref, bf16[3328,1024]{1,0:T(8,128)(2,1)S(1)} %bitcast.3), custom_call_target="tpu_custom_call" | custom-call | flops 218103808 | bytes 6815744 | tf_op jit(solution)/shard_map/down/pallas_call | solution.py:358
  78.7 11.6 %all_to_all.29.parts_ref = bf16[8,32,128]{2,1,0:T(8,128)(2,1)S(1)} all-to-all(bf16[8,32,128]{2,1,0:T(8,128)(2,1)S(1)} %down.1), channel_id=1, replica_groups=mesh['kv'=16,'head'=8] {'head'}, dimensions={0} | all-to-all | bytes 131072 | tf_op jit(solution)/shard_map/all_to_all | solution.py:389
  90.3 0.6 finish.1
  (12 shorter events, 0.1 us)
Async XLA Ops:
  19.8 17.4 %copy-start = (bf16[32,128]{1,0:T(8,128)(2,1)S(1)}, bf16[32,128]{1,0:T(8,128)(2,1)}, u32[]{:S(2)}) copy-start(bf16[32,128]{1,0:T(8,128)(2,1)} %res_ref.1) | copy-start | bytes 24580
  19.8 17.4 %copy-start.1 = (bf16[128]{0:T(256)(128)(2,1)S(1)}, bf16[128]{0:T(256)(128)(2,1)}, u32[]{:S(2)}) copy-start(bf16[128]{0:T(256)(128)(2,1)} %param.22) | copy-start | bytes 772
  19.8 4.0 %collective-permute-start = (bf16[16,32,512]{2,1,0:T(8,128)(2,1)S(1)}, bf16[16,32,512]{2,1,0:T(8,128)(2,1)S(1)}, u32[]{:S(2)}, u32[]{:S(2)}) collective-permute-start(bf16[16,32,512]{2,1,0:T(8,128)(2,1)S(1)} %get-tuple-element.22.after_ref), channel_id=1, source_target_pairs={{0,1},{1,0},{2,3},{3,2},{4,5},{5,4},{6,7},{7,6},{8,9},{9,8},{10,11... | collective-permute-start | bytes 1572872 | tf_op jit(solution)/shard_map/ppermute | solution.py:393
  37.4 3.4 %collective-permute-start.1 = (bf16[32,640]{1,0:T(8,128)(2,1)S(1)}, bf16[32,640]{1,0:T(8,128)(2,1)S(1)}, u32[]{:S(2)}, u32[]{:S(2)}) collective-permute-start(bf16[32,640]{1,0:T(8,128)(2,1)S(1)} %stream.1.after_ref), channel_id=1, source_target_pairs={{0,2},{1,3},{2,0},{3,1},{4,6},{5,7},{6,4},{7,5},{8,10},{9,11},{10,... | collective-permute-start | bytes 122888 | tf_op jit(solution)/shard_map/ppermute | solution.py:393
  40.7 4.4 %collective-permute-start.2 = (bf16[32,640]{1,0:T(8,128)(2,1)S(1)}, bf16[32,640]{1,0:T(8,128)(2,1)S(1)}, u32[]{:S(2)}, u32[]{:S(2)}) collective-permute-start(bf16[32,640]{1,0:T(8,128)(2,1)S(1)} %add_convert_fusion.1.after_ref), channel_id=1, source_target_pairs={{0,6},{1,7},{2,4},{3,5},{4,2},{5,3},{6,0},{7,1},{8,14},{9,15},{10,... | collective-permute-start | bytes 122888 | tf_op jit(solution)/shard_map/ppermute | solution.py:393
  45.1 6.2 %collective-permute-start.3 = (bf16[32,640]{1,0:T(8,128)(2,1)S(1)}, bf16[32,640]{1,0:T(8,128)(2,1)S(1)}, u32[]{:S(2)}, u32[]{:S(2)}) collective-permute-start(bf16[32,640]{1,0:T(8,128)(2,1)S(1)} %add_convert_fusion.after_ref.mine_ref), channel_id=1, source_target_pairs={{0,1},{1,0},{2,3},{3,2},{4,5},{5,4},{6,7},{7,6},{8,9},{9,8},{10,11... | collective-permute-start | bytes 122888 | tf_op jit(solution)/shard_map/ppermute | solution.py:393
  49.2 28.3 %slice-start = ((s8[6815744]{0:T(1024)(128)(4,1)}), s8[4194304]{0:T(1024)(128)(4,1)S(1)}, s32[]{:S(2)}) async-start(s8[6815744]{0:T(1024)(128)(4,1)} %bitcast.2), calls=%async_computation.5 | async-start | bytes 8388608
  51.3 26.2 %slice-start.1 = ((s8[6815744]{0:T(1024)(128)(4,1)}), s8[2621440]{0:T(1024)(128)(4,1)S(1)}, s32[]{:S(2)}) async-start(s8[6815744]{0:T(1024)(128)(4,1)} %bitcast.2), calls=%async_computation.6 | async-start | bytes 5242880

commit v3 on v2

--- a/solution.py
+++ b/solution.py
@@ -1,4 +1,3 @@
-import functools
 import math
 
 import jax
@@ -27,6 +26,7 @@
 BF16 = jnp.bfloat16
 MIB = 1 << 20
 W_SPACE = pltpu.HBM
+ATTENTION_ROOM = 58
 
 
 def whole(shape, space=pltpu.VMEM):
@@ -49,6 +49,10 @@
 
 def in_hbm(array):
     return pltpu.with_memory_space_constraint(array, pltpu.HBM)
+
+
+def in_vmem(array):
+    return pltpu.with_memory_space_constraint(array, pltpu.VMEM)
 
 
 def cost(flops, moved):
@@ -156,14 +160,14 @@
     arrays = (queries, key_cache, value_cache, new_keys, new_values)
     return pl.pallas_call(
         attention_kernel,
-        out_shape=[shape((GROUP, ROWS + 16, HD), BF16), shape(weight.shape, BF16)],
+        out_shape=[shape((GROUP, ROWS + 16, HD), BF16), pltpu.VMEM(weight.shape, BF16)],
         in_specs=[pl.BlockSpec(memory_space=W_SPACE)] * 8,
         out_specs=[whole((GROUP, ROWS + 16, HD)), whole(weight.shape)],
         scratch_shapes=[pltpu.SMEM(table.shape, jnp.int32), pltpu.SMEM(lengths.shape, jnp.int32)]
         + [pltpu.VMEM(a.shape, BF16) for a in arrays]
         + [pltpu.SemaphoreType.DMA((7,)), pltpu.SemaphoreType.DMA((8,))]
         + [tall, pltpu.VMEM((SLOTS, ROWS, HD), F32), tall, tall, tall],
-        compiler_params=params(16),
+        compiler_params=params(ATTENTION_ROOM),
         cost_estimate=cost(SLOTS * ROWS * HD * HD * 4, 4 * SLOTS * HD * HD),
         name="attention",
     )(*[in_hbm(a) for a in (table, lengths, *arrays, weight)])
@@ -223,7 +227,7 @@
     )(keep, got)
 
 
-def stream_kernel(parts_ref, res_ref, gain_ref, out_ref):
+def stream_kernel(_, parts_ref, res_ref, gain_ref, out_ref):
     total = parts_ref[0].astype(F32)
     for i in range(1, N_KV):
         total += parts_ref[i].astype(F32)
@@ -232,26 +236,50 @@
     for y in range(4):
         rest = jnp.where(me == y, res_ref[...].astype(F32), 0.0)
         blocks.append(total[:, y * OWN : (y + 1) * OWN] + rest)
-    row = lax.broadcasted_iota(jnp.int32, (ROWS, OWN), 0)
-    blocks.append(jnp.where(row == me, gain_ref[...].astype(F32), 0.0))
-    out_ref[...] = jnp.concatenate(blocks, axis=1).astype(BF16)
-
-
-def stream(parts, residual, gain):
-    out = (ROWS, HALF + OWN)
+    blocks.append(jnp.broadcast_to(gain_ref[...].astype(F32), (ROWS, OWN)))
+    message = jnp.concatenate(blocks, axis=1).astype(BF16)
+    for y in range(4):
+        out_ref[y] = message
+
+
+def stream(parts, residual, gain, held):
+    out = (4, ROWS, HALF + OWN)
     return pl.pallas_call(
         stream_kernel,
         out_shape=shape(out, BF16),
-        in_specs=[whole(a.shape) for a in (parts, residual, gain)],
+        in_specs=[whole(a.shape) for a in (held, parts, residual, gain)],
         out_specs=whole(out),
         compiler_params=params(8),
         name="stream",
-    )(parts, residual, gain)
-
-
-def gate_kernel(mine_ref, other_ref, gate_a, gate_b, up_a, up_b, out_ref, own_ref):
+    )(in_vmem(held), parts, residual, gain)
+
+
+def column_kernel(parts_ref, out_ref):
+    total = parts_ref[0, :, :HALF].astype(F32)
+    for y in range(1, 4):
+        total += parts_ref[y, :, :HALF].astype(F32)
+    out_ref[:, :HALF] = total.astype(BF16)
+    row = lax.broadcasted_iota(jnp.int32, (ROWS, OWN), 0)
+    gains = jnp.zeros((ROWS, OWN), F32)
+    for y in range(4):
+        gains = jnp.where(row == y, parts_ref[y, :, HALF:].astype(F32), gains)
+    out_ref[:, HALF:] = gains.astype(BF16)
+
+
+def add_columns(parts):
+    out = parts.shape[1:]
+    return pl.pallas_call(
+        column_kernel,
+        out_shape=shape(out, BF16),
+        in_specs=[whole(parts.shape)],
+        out_specs=whole(out),
+        compiler_params=params(8),
+        name="add_columns",
+    )(parts)
+
+
+def gate_kernel(mine_ref, other_ref, gate_w, up_w, out_ref, own_ref):
     tiles = UNITS // TILE
-    deep = gate_a.shape[0]
     even = is_even()
     mine, other = mine_ref[...].astype(F32), other_ref[...].astype(F32)
     halves = (jnp.where(even, mine, other), jnp.where(even, other, mine))
@@ -275,10 +303,9 @@
         out_ref[d, :, 2 * PART :] = squares[4 * (d // 2) : 4 * (d // 2) + 4, :].astype(BF16)
     for tile in range(tiles):
         for which in range(2):
-            upper, lower = ((gate_a, gate_b), (up_a, up_b))[which]
+            weight = (gate_w, up_w)[which]
             lanes = slice(tile * TILE, (tile + 1) * TILE)
-            result = jnp.dot(x[:, :deep], upper[:, lanes], preferred_element_type=F32)
-            result += jnp.dot(x[:, deep:], lower[:, lanes], preferred_element_type=F32)
+            result = jnp.dot(x, weight[:, lanes], preferred_element_type=F32)
             for part in range(2):
                 column = 2 * tile + part
                 at = which * PART + column % 13 * 128
@@ -287,39 +314,17 @@
                     out_ref[2 * r + column // 13, :, at : at + 128] = piece.astype(BF16)
 
 
-def gate_up(mine, other, gates, ups):
+def gate_up(mine, other, w_gate, w_up):
     wide = (N_KV, 4, 2 * PART + EXTRA)
     return pl.pallas_call(
         gate_kernel,
         out_shape=[shape(wide, BF16), shape((ROWS, OWN), F32)],
-        in_specs=[whole(a.shape) for a in (mine, other, *gates, *ups)],
+        in_specs=[whole(a.shape) for a in (mine, other, w_gate, w_up)],
         out_specs=[whole(wide), whole((ROWS, OWN))],
         compiler_params=params(8),
-        cost_estimate=cost(8 * ROWS * gates[0].size, 8 * gates[0].size),
+        cost_estimate=cost(4 * ROWS * w_gate.size, 4 * w_gate.size),
         name="gate_up",
-    )(mine, other, *gates, *ups)
-
-
-def load_kernel(start, after_ref, w_hbm, out_ref, sems):
-    copies = parts_of_copy(w_hbm.at[start : start + out_ref.shape[0], :], out_ref, sems)
-    for copy in copies:
-        copy.start()
-    for copy in copies:
-        copy.wait()
-
-
-def load(weight, half, after):
-    rows = weight.shape[0] // 2
-    return pl.pallas_call(
-        functools.partial(load_kernel, half * rows),
-        out_shape=shape((rows, weight.shape[1]), BF16),
-        in_specs=[pl.BlockSpec(memory_space=pl.ANY), pl.BlockSpec(memory_space=W_SPACE)],
-        out_specs=whole((rows, weight.shape[1])),
-        scratch_shapes=[pltpu.SemaphoreType.DMA((8,))],
-        compiler_params=params(8),
-        cost_estimate=cost(0, 2 * weight.size),
-        name="load",
-    )(after, in_hbm(weight))
+    )(mine, other, in_vmem(w_gate), in_vmem(w_up))
 
 
 def hidden_kernel(parts_ref, out_ref):
@@ -364,7 +369,7 @@
         compiler_params=params(8),
         cost_estimate=cost(2 * ROWS * w_down.size, 2 * w_down.size),
         name="down",
-    )(parts, w_down)
+    )(parts, in_vmem(w_down))
 
 
 def finish_kernel(own_ref, parts_ref, out_ref):
@@ -385,16 +390,12 @@
     )(own, parts)
 
 
-def exchange(value, axis):
-    return lax.all_to_all(value, axis, 0, 0, tiled=True)
+def exchange(value, axis, groups=None):
+    return lax.all_to_all(value, axis, 0, 0, axis_index_groups=groups, tiled=True)
 
 
 def swap(value, step):
     return lax.ppermute(value, "head", [(j, j ^ step) for j in range(KVH)])
-
-
-def swap_beside(value, step, weight, half):
-    return lax.optimization_barrier((swap(value, step), load(weight, half, value)))
 
 
 def on_device(
@@ -416,15 +417,11 @@
         block_table, lengths, queries, key_cache, value_cache, new_keys, new_values, out_weight[0, 0]
     )
     keep, give = project(exchange(partials, "kv"), weight)
-    swapped, up_a = swap_beside(give, 1, w_up, 0)
-    parts = exchange(add_pair(keep, swapped), "kv")
-    here = stream(parts, residual, norm_gain[None])
-    swapped, up_b = swap_beside(here, 2, w_up, 1)
-    here = (here.astype(F32) + swapped.astype(F32)).astype(BF16)
-    swapped, gate_a = swap_beside(here, 6, w_gate, 0)
-    here = (here.astype(F32) + swapped.astype(F32)).astype(BF16)
-    other, gate_b = swap_beside(here, 1, w_gate, 1)
-    gates, own = gate_up(here, other, (gate_a, gate_b), (up_a, up_b))
+    parts = exchange(add_pair(keep, swap(give, 1)), "kv")
+    same_core = [[2 * y + c for y in range(4)] for c in range(2)]
+    parts = exchange(stream(parts, residual, norm_gain[None], w_up), "head", same_core)
+    here = add_columns(parts)
+    gates, own = gate_up(here, swap(here, 1), w_gate, w_up)
     hidden = exchange(hidden_units(exchange(gates, "kv")), "kv")
     parts = exchange(down(hidden, w_down), "head")
     return finish(own, parts)

time: 91.3 us -> 92.8 us (1.016)
  blocking collectives: 63.7 us -> 71.5 us
  Pallas kernels: 17.2 us -> 9.83 us
  starting transfers between devices: 9.83 us -> 5.66 us
  local copies, waits for them, and re-layouts: 0.02 us -> 2.96 us
  waiting for transfers between devices: 0.01 us -> 2.41 us
    pallas_call x4 -> x1, Pallas kernels: 8.04 us -> 0.02 us  [add_columns(): pl.pallas_call(column_kernel, out_shape=shape(out, BF16), in_specs=[whole...]
    all_to_all x5 -> x6, blocking collectives: 63.7 us -> 71.5 us  [exchange(): lax.all_to_all(value, axis, 0, 0, axis_index_groups=groups, tiled=True)]
    ppermute x4 -> x2, starting transfers between devices: 9.83 us -> 5.66 us  [swap(): return lax.ppermute(value, 'head', [(j, j ^ step) for j in range(KVH)])]
    unnamed x8 -> x12, local copies, waits for them, and re-layouts: 0.02 us -> 2.96 us
    ppermute x4 -> x2, waiting for transfers between devices: 0.01 us -> 2.41 us  [swap(): return lax.ppermute(value, 'head', [(j, j ^ step) for j in range(KVH)])]
  transfers between devices with their start and end apart: 4 -> 2, of which waited for: 0 -> 2; matrix products, arithmetic and copies ran while one was open for 0% -> 0% of each run, Pallas kernels for 9% -> 0%
where the time goes in v3:
time: 92.8 us; the launch traced here: 92.5 us
  blocking collectives  71.5 us (77%)
  Pallas kernels  9.83 us (11%)
  starting transfers between devices  5.66 us (6%)
  local copies, waits for them, and re-layouts  2.96 us (3%)
  waiting for transfers between devices  2.41 us (3%)
    all_to_all x6, blocking collectives, exchange(): lax.all_to_all(value, axis, 0, 0, axis_index_groups=groups, tiled=True)  71.5 us
    ppermute x2, starting transfers between devices, swap(): return lax.ppermute(value, 'head', [(j, j ^ step) for j in range(KVH)])  5.66 us
    pallas_call x1, Pallas kernels, attention_partials(): pl.pallas_call(attention_kernel, out_shape=[shape((GROUP, ROWS + 16, HD),...  4.06 us
    unnamed x12, local copies, waits for them, and re-layouts  2.96 us
    pallas_call x1, Pallas kernels, gate_up(): pl.pallas_call(gate_kernel, out_shape=[shape(wide, BF16), shape((ROWS, OW...  2.43 us
    ppermute x2, waiting for transfers between devices, swap(): return lax.ppermute(value, 'head', [(j, j ^ step) for j in range(KVH)])  2.41 us
  transfers between devices with their start and end apart: 2, of which 2 were waited for; matrix products, arithmetic and copies ran while one was open for 0% of the time, Pallas kernels for 0%

profile of v3, /device:TPU:1, one launch (start us, length us, event | category | flops | bytes accessed | tf_op | source)
XLA Modules:
  0.0 92.5 jit_solution(1046100445977986352)
XLA Ops:
  0.0 4.1 %attention.1 = (bf16[16,48,128]{2,1,0:T(8,128)(2,1)}, bf16[128,16384]{1,0:T(8,128)(2,1)S(1)}) custom-call(s32[2,24]{1,0:T(2,128)} %table_hbm.1, s32[16]{0:T(128)} %lengths_hbm.1, bf16[32,2048]{1,0:T(8,128)(2,1)} %q_hbm.1, bf16[24,1,128,128]{3,2,1,0:T(8,128)(2,1)} %k_hbm.1, bf16[24,1,128,128]{3,2,1,0:T(8,128)(2,1)} %v_hbm.1, bf16[32,128]{1,0:T(8,128)(2,1)} %new_k_hbm.1, ...), custom_call_target="tpu_custom_call" | custom-call | flops 50331648 | bytes 1572864 | tf_op jit(solution)/shard_map/attention/pallas_call | solution.py:161
  4.1 0.0 copy-start
  4.1 15.9 %all_to_all.30.got_ref = bf16[16,48,128]{2,1,0:T(8,128)(2,1)S(1)} all-to-all(bf16[16,48,128]{2,1,0:T(8,128)(2,1)} %get-tuple-element.11), channel_id=1, replica_groups=mesh['kv'=16,'head'=8] {'kv'}, dimensions={0} | all-to-all | bytes 393216 | tf_op jit(solution)/shard_map/all_to_all | solution.py:394
  20.0 1.1 %project.1 = (f32[16,32,512]{2,1,0:T(8,128)S(1)}, bf16[16,32,512]{2,1,0:T(8,128)(2,1)S(1)}) custom-call(bf16[16,48,128]{2,1,0:T(8,128)(2,1)S(1)} %all_to_all.30.got_ref, bf16[128,16384]{1,0:T(8,128)(2,1)S(1)} %get-tuple-element.12.w_ref), custom_call_target="tpu_custom_call" | custom-call | flops 134217728 | bytes 4194304 | tf_op jit(solution)/shard_map/project/pallas_call | solution.py:204
  21.0 2.1 %collective-permute-start = (bf16[16,32,512]{2,1,0:T(8,128)(2,1)S(1)}, bf16[16,32,512]{2,1,0:T(8,128)(2,1)S(1)}, u32[]{:S(2)}, u32[]{:S(2)}) collective-permute-start(bf16[16,32,512]{2,1,0:T(8,128)(2,1)S(1)} %get-tuple-element.14), channel_id=1, source_target_pairs={{0,1},{1,0},{2,3},{3,2},{4,5},{5,4},{6,7},{7,6},{8,9},{9,8},{10,11... | collective-permute-start | bytes 1572872 | tf_op jit(solution)/shard_map/ppermute | solution.py:398
  23.1 1.5 %collective-permute-done.got_ref = bf16[16,32,512]{2,1,0:T(8,128)(2,1)S(1)} collective-permute-done((bf16[16,32,512]{2,1,0:T(8,128)(2,1)S(1)}, bf16[16,32,512]{2,1,0:T(8,128)(2,1)S(1)}, u32[]{:S(2)}, u32[]{:S(2)}) %collective-permute-start) | collective-permute-done | bytes 524320 | tf_op jit(solution)/shard_map/ppermute | solution.py:398
  24.6 0.1 add_pair.1
  24.7 13.5 %all_to_all.31.parts_ref = bf16[16,32,512]{2,1,0:T(8,128)(2,1)S(1)} all-to-all(bf16[16,32,512]{2,1,0:T(8,128)(2,1)S(1)} %add_pair.1), channel_id=1, replica_groups=mesh['kv'=16,'head'=8] {'kv'}, dimensions={0} | all-to-all | bytes 1048576 | tf_op jit(solution)/shard_map/all_to_all | solution.py:394
  38.2 0.0 copy-done.2
  38.2 0.0 copy-done.3
  38.2 0.1 stream.1
  38.3 9.0 %all_to_all.32.parts_ref = bf16[4,32,640]{2,1,0:T(8,128)(2,1)S(1)} all-to-all(bf16[4,32,640]{2,1,0:T(8,128)(2,1)S(1)} %stream.1), channel_id=1, replica_groups={{0,2,4,6},{1,3,5,7},{8,10,12,14},{9,11,13,15},{16,18,20,22},{17,19,21,2..., dimensions={0} | all-to-all | bytes 327680 | tf_op jit(solution)/shard_map/all_to_all | solution.py:394
  47.3 0.0 slice-start.1
  47.3 3.6 %collective-permute-start.1 = (bf16[32,640]{1,0:T(8,128)(2,1)S(1)}, bf16[32,640]{1,0:T(8,128)(2,1)S(1)}, u32[]{:S(2)}, u32[]{:S(2)}) collective-permute-start(bf16[32,640]{1,0:T(8,128)(2,1)S(1)} %add_columns.1.mine_ref), channel_id=1, source_target_pairs={{0,1},{1,0},{2,3},{3,2},{4,5},{5,4},{6,7},{7,6},{8,9},{9,8},{10,11... | collective-permute-start | bytes 122888 | tf_op jit(solution)/shard_map/ppermute | solution.py:398
  50.9 0.9 collective-permute-done.1.other_ref
  51.8 2.9 %copy-done.1 = bf16[1024,3328]{1,0:T(8,128)(2,1)S(1)} copy-done((bf16[1024,3328]{1,0:T(8,128)(2,1)S(1)}, bf16[1024,3328]{1,0:T(8,128)(2,1)}, u32[]{:S(2)}) %copy-start.1) | copy-done | bytes 6815768
  54.7 2.4 %gate_up.1 = (bf16[16,4,3456]{2,1,0:T(4,128)(2,1)S(1)}, f32[32,128]{1,0:T(8,128)S(1)}) custom-call(bf16[32,640]{1,0:T(8,128)(2,1)S(1)} %add_columns.1.mine_ref, bf16[32,640]{1,0:T(8,128)(2,1)S(1)} %collective-permute-done.1.other_ref, bf16[1024,3328]{1,0:T(8,128)(2,1)S(1)} %copy-done.1, bf16[1024,3328]{1,0:T(8,128)(2,1)S(1)} %copy-done), custom_call_target="tpu_custom_call" | custom-call | flops 436207616 | bytes 13631488 | tf_op jit(solution)/shard_map/gate_up/pallas_call | solution.py:319
  57.2 11.5 %all_to_all.33.parts_ref = bf16[16,4,3456]{2,1,0:T(4,128)(2,1)S(1)} all-to-all(bf16[16,4,3456]{2,1,0:T(4,128)(2,1)S(1)} %get-tuple-element.16), channel_id=1, replica_groups=mesh['kv'=16,'head'=8] {'kv'}, dimensions={0} | all-to-all | bytes 884736 | tf_op jit(solution)/shard_map/all_to_all | solution.py:394
  68.7 0.2 hidden_units.1
  68.9 11.1 %all_to_all.34.parts_ref = bf16[16,4,1664]{2,1,0:T(4,128)(2,1)S(1)} all-to-all(bf16[16,4,1664]{2,1,0:T(4,128)(2,1)S(1)} %hidden_units.1), channel_id=1, replica_groups=mesh['kv'=16,'head'=8] {'kv'}, dimensions={0} | all-to-all | bytes 425984 | tf_op jit(solution)/shard_map/all_to_all | solution.py:394
  79.9 0.0 slice-done.1
  79.9 1.3 %down.1 = bf16[8,32,128]{2,1,0:T(8,128)(2,1)S(1)} custom-call(bf16[16,4,1664]{2,1,0:T(4,128)(2,1)S(1)} %all_to_all.34.parts_ref, bf16[3328,1024]{1,0:T(8,128)(2,1)S(1)} %bitcast.3), custom_call_target="tpu_custom_call" | custom-call | flops 218103808 | bytes 6815744 | tf_op jit(solution)/shard_map/down/pallas_call | solution.py:363
  81.2 10.6 %all_to_all.35.parts_ref = bf16[8,32,128]{2,1,0:T(8,128)(2,1)S(1)} all-to-all(bf16[8,32,128]{2,1,0:T(8,128)(2,1)S(1)} %down.1), channel_id=1, replica_groups=mesh['kv'=16,'head'=8] {'head'}, dimensions={0} | all-to-all | bytes 131072 | tf_op jit(solution)/shard_map/all_to_all | solution.py:394
  91.8 0.6 finish.1
  (8 shorter events, 0.0 us)
Async XLA Ops:
  0.0 38.2 %copy-start.2 = (bf16[32,128]{1,0:T(8,128)(2,1)S(1)}, bf16[32,128]{1,0:T(8,128)(2,1)}, u32[]{:S(2)}) copy-start(bf16[32,128]{1,0:T(8,128)(2,1)} %res_ref.1) | copy-start | bytes 24580
  0.0 38.2 %copy-start.3 = (bf16[128]{0:T(256)(128)(2,1)S(1)}, bf16[128]{0:T(256)(128)(2,1)}, u32[]{:S(2)}) copy-start(bf16[128]{0:T(256)(128)(2,1)} %param.22) | copy-start | bytes 772
  4.1 34.1 %copy-start = (bf16[1024,3328]{1,0:T(8,128)(2,1)S(1)}, bf16[1024,3328]{1,0:T(8,128)(2,1)}, u32[]{:S(2)}) copy-start(bf16[1024,3328]{1,0:T(8,128)(2,1)} %up_w.1) | copy-start | bytes 20447236
  21.0 3.6 %collective-permute-start = (bf16[16,32,512]{2,1,0:T(8,128)(2,1)S(1)}, bf16[16,32,512]{2,1,0:T(8,128)(2,1)S(1)}, u32[]{:S(2)}, u32[]{:S(2)}) collective-permute-start(bf16[16,32,512]{2,1,0:T(8,128)(2,1)S(1)} %get-tuple-element.14), channel_id=1, source_target_pairs={{0,1},{1,0},{2,3},{3,2},{4,5},{5,4},{6,7},{7,6},{8,9},{9,8},{10,11... | collective-permute-start | bytes 1572872 | tf_op jit(solution)/shard_map/ppermute | solution.py:398
  47.3 32.6 %slice-start = ((s8[6815744]{0:T(1024)(128)(4,1)}), s8[4194304]{0:T(1024)(128)(4,1)S(1)}, s32[]{:S(2)}) async-start(s8[6815744]{0:T(1024)(128)(4,1)} %bitcast.2), calls=%async_computation.6 | async-start | bytes 8388608
  47.3 32.6 %slice-start.1 = ((s8[6815744]{0:T(1024)(128)(4,1)}), s8[2621440]{0:T(1024)(128)(4,1)S(1)}, s32[]{:S(2)}) async-start(s8[6815744]{0:T(1024)(128)(4,1)} %bitcast.2), calls=%async_computation.7 | async-start | bytes 5242880
  47.3 4.5 %collective-permute-start.1 = (bf16[32,640]{1,0:T(8,128)(2,1)S(1)}, bf16[32,640]{1,0:T(8,128)(2,1)S(1)}, u32[]{:S(2)}, u32[]{:S(2)}) collective-permute-start(bf16[32,640]{1,0:T(8,128)(2,1)S(1)} %add_columns.1.mine_ref), channel_id=1, source_target_pairs={{0,1},{1,0},{2,3},{3,2},{4,5},{5,4},{6,7},{7,6},{8,9},{9,8},{10,11... | collective-permute-start | bytes 122888 | tf_op jit(solution)/shard_map/ppermute | solution.py:398
  51.8 2.9 %copy-start.1 = (bf16[1024,3328]{1,0:T(8,128)(2,1)S(1)}, bf16[1024,3328]{1,0:T(8,128)(2,1)}, u32[]{:S(2)}) copy-start(bf16[1024,3328]{1,0:T(8,128)(2,1)} %gate_w.1) | copy-start | bytes 20447236

commit v4 on v3

--- a/solution.py
+++ b/solution.py
@@ -26,7 +26,7 @@
 BF16 = jnp.bfloat16
 MIB = 1 << 20
 W_SPACE = pltpu.HBM
-ATTENTION_ROOM = 58
+ATTENTION_ROOM = 57
 
 
 def whole(shape, space=pltpu.VMEM):
@@ -160,7 +160,7 @@
     arrays = (queries, key_cache, value_cache, new_keys, new_values)
     return pl.pallas_call(
         attention_kernel,
-        out_shape=[shape((GROUP, ROWS + 16, HD), BF16), pltpu.VMEM(weight.shape, BF16)],
+        out_shape=[pltpu.VMEM((GROUP, ROWS + 16, HD), BF16), pltpu.VMEM(weight.shape, BF16)],
         in_specs=[pl.BlockSpec(memory_space=W_SPACE)] * 8,
         out_specs=[whole((GROUP, ROWS + 16, HD)), whole(weight.shape)],
         scratch_shapes=[pltpu.SMEM(table.shape, jnp.int32), pltpu.SMEM(lengths.shape, jnp.int32)]
@@ -254,7 +254,7 @@
     )(in_vmem(held), parts, residual, gain)
 
 
-def column_kernel(parts_ref, out_ref):
+def column_kernel(_, parts_ref, out_ref):
     total = parts_ref[0, :, :HALF].astype(F32)
     for y in range(1, 4):
         total += parts_ref[y, :, :HALF].astype(F32)
@@ -266,16 +266,16 @@
     out_ref[:, HALF:] = gains.astype(BF16)
 
 
-def add_columns(parts):
+def add_columns(parts, held):
     out = parts.shape[1:]
     return pl.pallas_call(
         column_kernel,
         out_shape=shape(out, BF16),
-        in_specs=[whole(parts.shape)],
+        in_specs=[whole(held.shape), whole(parts.shape)],
         out_specs=whole(out),
         compiler_params=params(8),
         name="add_columns",
-    )(parts)
+    )(in_vmem(held), parts)
 
 
 def gate_kernel(mine_ref, other_ref, gate_w, up_w, out_ref, own_ref):
@@ -420,7 +420,7 @@
     parts = exchange(add_pair(keep, swap(give, 1)), "kv")
     same_core = [[2 * y + c for y in range(4)] for c in range(2)]
     parts = exchange(stream(parts, residual, norm_gain[None], w_up), "head", same_core)
-    here = add_columns(parts)
+    here = add_columns(parts, w_gate)
     gates, own = gate_up(here, swap(here, 1), w_gate, w_up)
     hidden = exchange(hidden_units(exchange(gates, "kv")), "kv")
     parts = exchange(down(hidden, w_down), "head")

time: 92.8 us -> 89.1 us (0.960)
  local copies, waits for them, and re-layouts: 2.96 us -> 0.04 us
    unnamed x12 -> x14, local copies, waits for them, and re-layouts: 2.96 us -> 0.04 us
where the time goes in v4:
time: 89.1 us; the launch traced here: 88.8 us
  blocking collectives  71.4 us (80%)
  Pallas kernels  9.16 us (10%)
  starting transfers between devices  5.66 us (6%)
  waiting for transfers between devices  2.41 us (3%)
    all_to_all x6, blocking collectives, exchange(): lax.all_to_all(value, axis, 0, 0, axis_index_groups=groups, tiled=True)  71.4 us
    ppermute x2, starting transfers between devices, swap(): return lax.ppermute(value, 'head', [(j, j ^ step) for j in range(KVH)])  5.66 us
    pallas_call x1, Pallas kernels, attention_partials(): pl.pallas_call(attention_kernel, out_shape=[pltpu.VMEM((GROUP, ROWS + 16,...  3.4 us
    pallas_call x1, Pallas kernels, gate_up(): pl.pallas_call(gate_kernel, out_shape=[shape(wide, BF16), shape((ROWS, OW...  2.43 us
    ppermute x2, waiting for transfers between devices, swap(): return lax.ppermute(value, 'head', [(j, j ^ step) for j in range(KVH)])  2.41 us
  transfers between devices with their start and end apart: 2, of which 2 were waited for; matrix products, arithmetic and copies ran while one was open for 0% of the time, Pallas kernels for 0%

profile of v4, /device:TPU:1, one launch (start us, length us, event | category | flops | bytes accessed | tf_op | source)
XLA Modules:
  0.0 88.8 jit_solution(6892871668070072018)
XLA Ops:
  0.0 3.4 %attention.1 = (bf16[16,48,128]{2,1,0:T(8,128)(2,1)S(1)}, bf16[128,16384]{1,0:T(8,128)(2,1)S(1)}) custom-call(s32[2,24]{1,0:T(2,128)} %table_hbm.1, s32[16]{0:T(128)} %lengths_hbm.1, bf16[32,2048]{1,0:T(8,128)(2,1)} %q_hbm.1, bf16[24,1,128,128]{3,2,1,0:T(8,128)(2,1)} %k_hbm.1, bf16[24,1,128,128]{3,2,1,0:T(8,128)(2,1)} %v_hbm.1, bf16[32,128]{1,0:T(8,128)(2,1)} %new_k_hbm.1, ...), custom_call_target="tpu_custom_call" | custom-call | flops 50331648 | bytes 1572864 | tf_op jit(solution)/shard_map/attention/pallas_call | solution.py:161
  3.4 0.0 copy-start
  3.4 15.6 %all_to_all.30.got_ref = bf16[16,48,128]{2,1,0:T(8,128)(2,1)S(1)} all-to-all(bf16[16,48,128]{2,1,0:T(8,128)(2,1)S(1)} %get-tuple-element.11), channel_id=1, replica_groups=mesh['kv'=16,'head'=8] {'kv'}, dimensions={0} | all-to-all | bytes 393216 | tf_op jit(solution)/shard_map/all_to_all | solution.py:394
  19.1 1.1 %project.1 = (f32[16,32,512]{2,1,0:T(8,128)S(1)}, bf16[16,32,512]{2,1,0:T(8,128)(2,1)S(1)}) custom-call(bf16[16,48,128]{2,1,0:T(8,128)(2,1)S(1)} %all_to_all.30.got_ref, bf16[128,16384]{1,0:T(8,128)(2,1)S(1)} %get-tuple-element.12.w_ref), custom_call_target="tpu_custom_call" | custom-call | flops 134217728 | bytes 4194304 | tf_op jit(solution)/shard_map/project/pallas_call | solution.py:204
  20.1 2.1 %collective-permute-start = (bf16[16,32,512]{2,1,0:T(8,128)(2,1)S(1)}, bf16[16,32,512]{2,1,0:T(8,128)(2,1)S(1)}, u32[]{:S(2)}, u32[]{:S(2)}) collective-permute-start(bf16[16,32,512]{2,1,0:T(8,128)(2,1)S(1)} %get-tuple-element.14), channel_id=1, source_target_pairs={{0,1},{1,0},{2,3},{3,2},{4,5},{5,4},{6,7},{7,6},{8,9},{9,8},{10,11... | collective-permute-start | bytes 1572872 | tf_op jit(solution)/shard_map/ppermute | solution.py:398
  22.2 1.5 %collective-permute-done.got_ref = bf16[16,32,512]{2,1,0:T(8,128)(2,1)S(1)} collective-permute-done((bf16[16,32,512]{2,1,0:T(8,128)(2,1)S(1)}, bf16[16,32,512]{2,1,0:T(8,128)(2,1)S(1)}, u32[]{:S(2)}, u32[]{:S(2)}) %collective-permute-start) | collective-permute-done | bytes 524320 | tf_op jit(solution)/shard_map/ppermute | solution.py:398
  23.7 0.1 add_pair.1
  23.8 13.5 %all_to_all.31.parts_ref = bf16[16,32,512]{2,1,0:T(8,128)(2,1)S(1)} all-to-all(bf16[16,32,512]{2,1,0:T(8,128)(2,1)S(1)} %add_pair.1), channel_id=1, replica_groups=mesh['kv'=16,'head'=8] {'kv'}, dimensions={0} | all-to-all | bytes 1048576 | tf_op jit(solution)/shard_map/all_to_all | solution.py:394
  37.3 0.0 copy-done
  37.3 0.0 slice-start.1
  37.3 0.1 stream.1
  37.4 9.1 %all_to_all.32.parts_ref = bf16[4,32,640]{2,1,0:T(8,128)(2,1)S(1)} all-to-all(bf16[4,32,640]{2,1,0:T(8,128)(2,1)S(1)} %stream.1), channel_id=1, replica_groups={{0,2,4,6},{1,3,5,7},{8,10,12,14},{9,11,13,15},{16,18,20,22},{17,19,21,2..., dimensions={0} | all-to-all | bytes 327680 | tf_op jit(solution)/shard_map/all_to_all | solution.py:394
  46.5 0.0 slice-done.1
  46.6 0.0 slice-start.3
  46.6 3.6 %collective-permute-start.1 = (bf16[32,640]{1,0:T(8,128)(2,1)S(1)}, bf16[32,640]{1,0:T(8,128)(2,1)S(1)}, u32[]{:S(2)}, u32[]{:S(2)}) collective-permute-start(bf16[32,640]{1,0:T(8,128)(2,1)S(1)} %add_columns.1.mine_ref), channel_id=1, source_target_pairs={{0,1},{1,0},{2,3},{3,2},{4,5},{5,4},{6,7},{7,6},{8,9},{9,8},{10,11... | collective-permute-start | bytes 122888 | tf_op jit(solution)/shard_map/ppermute | solution.py:398
  50.2 0.9 collective-permute-done.1.other_ref
  51.1 2.4 %gate_up.1 = (bf16[16,4,3456]{2,1,0:T(4,128)(2,1)S(1)}, f32[32,128]{1,0:T(8,128)S(1)}) custom-call(bf16[32,640]{1,0:T(8,128)(2,1)S(1)} %add_columns.1.mine_ref, bf16[32,640]{1,0:T(8,128)(2,1)S(1)} %collective-permute-done.1.other_ref, bf16[1024,3328]{1,0:T(8,128)(2,1)S(1)} %bitcast.3, bf16[1024,3328]{1,0:T(8,128)(2,1)S(1)} %copy-done), custom_call_target="tpu_custom_call" | custom-call | flops 436207616 | bytes 13631488 | tf_op jit(solution)/shard_map/gate_up/pallas_call | solution.py:319
  53.5 12.7 %all_to_all.33.parts_ref = bf16[16,4,3456]{2,1,0:T(4,128)(2,1)S(1)} all-to-all(bf16[16,4,3456]{2,1,0:T(4,128)(2,1)S(1)} %get-tuple-element.16), channel_id=1, replica_groups=mesh['kv'=16,'head'=8] {'kv'}, dimensions={0} | all-to-all | bytes 884736 | tf_op jit(solution)/shard_map/all_to_all | solution.py:394
  66.2 0.2 hidden_units.1
  66.4 10.4 %all_to_all.34.parts_ref = bf16[16,4,1664]{2,1,0:T(4,128)(2,1)S(1)} all-to-all(bf16[16,4,1664]{2,1,0:T(4,128)(2,1)S(1)} %hidden_units.1), channel_id=1, replica_groups=mesh['kv'=16,'head'=8] {'kv'}, dimensions={0} | all-to-all | bytes 425984 | tf_op jit(solution)/shard_map/all_to_all | solution.py:394
  76.8 0.0 slice-done.2
  76.8 1.3 %down.1 = bf16[8,32,128]{2,1,0:T(8,128)(2,1)S(1)} custom-call(bf16[16,4,1664]{2,1,0:T(4,128)(2,1)S(1)} %all_to_all.34.parts_ref, bf16[3328,1024]{1,0:T(8,128)(2,1)S(1)} %bitcast.5), custom_call_target="tpu_custom_call" | custom-call | flops 218103808 | bytes 6815744 | tf_op jit(solution)/shard_map/down/pallas_call | solution.py:363
  78.1 10.1 %all_to_all.35.parts_ref = bf16[8,32,128]{2,1,0:T(8,128)(2,1)S(1)} all-to-all(bf16[8,32,128]{2,1,0:T(8,128)(2,1)S(1)} %down.1), channel_id=1, replica_groups=mesh['kv'=16,'head'=8] {'head'}, dimensions={0} | all-to-all | bytes 131072 | tf_op jit(solution)/shard_map/all_to_all | solution.py:394
  88.2 0.6 finish.1
  (11 shorter events, 0.0 us)
Async XLA Ops:
  0.0 37.3 %copy-start.1 = (bf16[32,128]{1,0:T(8,128)(2,1)S(1)}, bf16[32,128]{1,0:T(8,128)(2,1)}, u32[]{:S(2)}) copy-start(bf16[32,128]{1,0:T(8,128)(2,1)} %res_ref.1) | copy-start | bytes 24580
  0.0 37.3 %copy-start.2 = (bf16[128]{0:T(256)(128)(2,1)S(1)}, bf16[128]{0:T(256)(128)(2,1)}, u32[]{:S(2)}) copy-start(bf16[128]{0:T(256)(128)(2,1)} %param.22) | copy-start | bytes 772
  3.4 33.9 %copy-start = (bf16[1024,3328]{1,0:T(8,128)(2,1)S(1)}, bf16[1024,3328]{1,0:T(8,128)(2,1)}, u32[]{:S(2)}) copy-start(bf16[1024,3328]{1,0:T(8,128)(2,1)} %up_w.1) | copy-start | bytes 20447236
  19.1 27.5 %slice-start = ((s8[6815744]{0:T(1024)(128)(4,1)}), s8[4194304]{0:T(1024)(128)(4,1)S(1)}, s32[]{:S(2)}) async-start(s8[6815744]{0:T(1024)(128)(4,1)} %bitcast.2), calls=%async_computation.6 | async-start | bytes 8388608
  20.1 3.6 %collective-permute-start = (bf16[16,32,512]{2,1,0:T(8,128)(2,1)S(1)}, bf16[16,32,512]{2,1,0:T(8,128)(2,1)S(1)}, u32[]{:S(2)}, u32[]{:S(2)}) collective-permute-start(bf16[16,32,512]{2,1,0:T(8,128)(2,1)S(1)} %get-tuple-element.14), channel_id=1, source_target_pairs={{0,1},{1,0},{2,3},{3,2},{4,5},{5,4},{6,7},{7,6},{8,9},{9,8},{10,11... | collective-permute-start | bytes 1572872 | tf_op jit(solution)/shard_map/ppermute | solution.py:398
  37.3 9.2 %slice-start.1 = ((s8[6815744]{0:T(1024)(128)(4,1)}), s8[2621440]{0:T(1024)(128)(4,1)S(1)}, s32[]{:S(2)}) async-start(s8[6815744]{0:T(1024)(128)(4,1)} %bitcast.2), calls=%async_computation.7 | async-start | bytes 5242880
  46.5 30.3 %slice-start.2 = ((s8[6815744]{0:T(1024)(128)(4,1)}), s8[4194304]{0:T(1024)(128)(4,1)S(1)}, s32[]{:S(2)}) async-start(s8[6815744]{0:T(1024)(128)(4,1)} %bitcast.4), calls=%async_computation.8 | async-start | bytes 8388608
  46.6 30.2 %slice-start.3 = ((s8[6815744]{0:T(1024)(128)(4,1)}), s8[2621440]{0:T(1024)(128)(4,1)S(1)}, s32[]{:S(2)}) async-start(s8[6815744]{0:T(1024)(128)(4,1)} %bitcast.4), calls=%async_computation.9 | async-start | bytes 5242880
  46.6 4.5 %collective-permute-start.1 = (bf16[32,640]{1,0:T(8,128)(2,1)S(1)}, bf16[32,640]{1,0:T(8,128)(2,1)S(1)}, u32[]{:S(2)}, u32[]{:S(2)}) collective-permute-start(bf16[32,640]{1,0:T(8,128)(2,1)S(1)} %add_columns.1.mine_ref), channel_id=1, source_target_pairs={{0,1},{1,0},{2,3},{3,2},{4,5},{5,4},{6,7},{7,6},{8,9},{9,8},{10,11... | collective-permute-start | bytes 122888 | tf_op jit(solution)/shard_map/ppermute | solution.py:398

commit v5 on v4

--- a/solution.py
+++ b/solution.py
@@ -236,14 +236,13 @@
     for y in range(4):
         rest = jnp.where(me == y, res_ref[...].astype(F32), 0.0)
         blocks.append(total[:, y * OWN : (y + 1) * OWN] + rest)
-    blocks.append(jnp.broadcast_to(gain_ref[...].astype(F32), (ROWS, OWN)))
-    message = jnp.concatenate(blocks, axis=1).astype(BF16)
-    for y in range(4):
-        out_ref[y] = message
+    row = lax.broadcasted_iota(jnp.int32, (ROWS, OWN), 0)
+    blocks.append(jnp.where(row == me, gain_ref[...].astype(F32), 0.0))
+    out_ref[...] = jnp.concatenate(blocks, axis=1).astype(BF16)
 
 
 def stream(parts, residual, gain, held):
-    out = (4, ROWS, HALF + OWN)
+    out = (ROWS, HALF + OWN)
     return pl.pallas_call(
         stream_kernel,
         out_shape=shape(out, BF16),
@@ -254,28 +253,19 @@
     )(in_vmem(held), parts, residual, gain)
 
 
-def column_kernel(_, parts_ref, out_ref):
-    total = parts_ref[0, :, :HALF].astype(F32)
-    for y in range(1, 4):
-        total += parts_ref[y, :, :HALF].astype(F32)
-    out_ref[:, :HALF] = total.astype(BF16)
-    row = lax.broadcasted_iota(jnp.int32, (ROWS, OWN), 0)
-    gains = jnp.zeros((ROWS, OWN), F32)
-    for y in range(4):
-        gains = jnp.where(row == y, parts_ref[y, :, HALF:].astype(F32), gains)
-    out_ref[:, HALF:] = gains.astype(BF16)
-
-
-def add_columns(parts, held):
-    out = parts.shape[1:]
-    return pl.pallas_call(
-        column_kernel,
-        out_shape=shape(out, BF16),
-        in_specs=[whole(held.shape), whole(parts.shape)],
-        out_specs=whole(out),
-        compiler_params=params(8),
-        name="add_columns",
-    )(in_vmem(held), parts)
+def sum_kernel(_, mine_ref, got_ref, out_ref):
+    out_ref[...] = (mine_ref[...].astype(F32) + got_ref[...].astype(F32)).astype(BF16)
+
+
+def add_swapped(mine, got, held):
+    return pl.pallas_call(
+        sum_kernel,
+        out_shape=shape(mine.shape, BF16),
+        in_specs=[whole(a.shape) for a in (held, mine, got)],
+        out_specs=whole(mine.shape),
+        compiler_params=params(8),
+        name="add_swapped",
+    )(in_vmem(held), mine, got)
 
 
 def gate_kernel(mine_ref, other_ref, gate_w, up_w, out_ref, own_ref):
@@ -390,8 +380,8 @@
     )(own, parts)
 
 
-def exchange(value, axis, groups=None):
-    return lax.all_to_all(value, axis, 0, 0, axis_index_groups=groups, tiled=True)
+def exchange(value, axis):
+    return lax.all_to_all(value, axis, 0, 0, tiled=True)
 
 
 def swap(value, step):
@@ -418,9 +408,9 @@
     )
     keep, give = project(exchange(partials, "kv"), weight)
     parts = exchange(add_pair(keep, swap(give, 1)), "kv")
-    same_core = [[2 * y + c for y in range(4)] for c in range(2)]
-    parts = exchange(stream(parts, residual, norm_gain[None], w_up), "head", same_core)
-    here = add_columns(parts, w_gate)
+    here = stream(parts, residual, norm_gain[None], w_up)
+    here = add_swapped(here, swap(here, 2), w_gate)
+    here = add_swapped(here, swap(here, 6), w_gate)
     gates, own = gate_up(here, swap(here, 1), w_gate, w_up)
     hidden = exchange(hidden_units(exchange(gates, "kv")), "kv")
     parts = exchange(down(hidden, w_down), "head")

time: 89.1 us -> 89.9 us (level)
  blocking collectives: 71.4 us -> 64.3 us
  starting transfers between devices: 5.66 us -> 10.7 us
  waiting for transfers between devices: 2.41 us -> 5.35 us
    all_to_all x6 -> x5, blocking collectives: 71.4 us -> 64.3 us  [exchange(): return lax.all_to_all(value, axis, 0, 0, tiled=True)]
    ppermute x2 -> x4, starting transfers between devices: 5.66 us -> 10.7 us  [swap(): return lax.ppermute(value, 'head', [(j, j ^ step) for j in range(KVH)])]
    ppermute x2 -> x4, waiting for transfers between devices: 2.41 us -> 5.35 us  [swap(): return lax.ppermute(value, 'head', [(j, j ^ step) for j in range(KVH)])]
  transfers between devices with their start and end apart: 2 -> 4, of which waited for: 2 -> 4; matrix products, arithmetic and copies ran while one was open for 0% -> 0% of each run, Pallas kernels for 0% -> 0%
where the time goes in v5:
time: 89.9 us; the launch traced here: 89.6 us
  blocking collectives  64.3 us (72%)
  starting transfers between devices  10.7 us (12%)
  Pallas kernels  9.15 us (10%)
  waiting for transfers between devices  5.35 us (6%)
    all_to_all x5, blocking collectives, exchange(): return lax.all_to_all(value, axis, 0, 0, tiled=True)  64.3 us
    ppermute x4, starting transfers between devices, swap(): return lax.ppermute(value, 'head', [(j, j ^ step) for j in range(KVH)])  10.7 us
    ppermute x4, waiting for transfers between devices, swap(): return lax.ppermute(value, 'head', [(j, j ^ step) for j in range(KVH)])  5.35 us
    pallas_call x1, Pallas kernels, attention_partials(): pl.pallas_call(attention_kernel, out_shape=[pltpu.VMEM((GROUP, ROWS + 16,...  3.38 us
    pallas_call x1, Pallas kernels, gate_up(): pl.pallas_call(gate_kernel, out_shape=[shape(wide, BF16), shape((ROWS, OW...  2.44 us
  transfers between devices with their start and end apart: 4, of which 4 were waited for; matrix products, arithmetic and copies ran while one was open for 0% of the time, Pallas kernels for 0%

profile of v5, /device:TPU:1, one launch (start us, length us, event | category | flops | bytes accessed | tf_op | source)
XLA Modules:
  0.0 89.6 jit_solution(8512900747053328996)
XLA Ops:
  0.0 3.4 %attention.1 = (bf16[16,48,128]{2,1,0:T(8,128)(2,1)S(1)}, bf16[128,16384]{1,0:T(8,128)(2,1)S(1)}) custom-call(s32[2,24]{1,0:T(2,128)} %table_hbm.1, s32[16]{0:T(128)} %lengths_hbm.1, bf16[32,2048]{1,0:T(8,128)(2,1)} %q_hbm.1, bf16[24,1,128,128]{3,2,1,0:T(8,128)(2,1)} %k_hbm.1, bf16[24,1,128,128]{3,2,1,0:T(8,128)(2,1)} %v_hbm.1, bf16[32,128]{1,0:T(8,128)(2,1)} %new_k_hbm.1, ...), custom_call_target="tpu_custom_call" | custom-call | flops 50331648 | bytes 1572864 | tf_op jit(solution)/shard_map/attention/pallas_call | solution.py:161
  3.4 0.0 copy-start
  3.4 15.7 %all_to_all.25.got_ref = bf16[16,48,128]{2,1,0:T(8,128)(2,1)S(1)} all-to-all(bf16[16,48,128]{2,1,0:T(8,128)(2,1)S(1)} %get-tuple-element.11), channel_id=1, replica_groups=mesh['kv'=16,'head'=8] {'kv'}, dimensions={0} | all-to-all | bytes 393216 | tf_op jit(solution)/shard_map/all_to_all | solution.py:384
  19.1 1.1 %project.1 = (f32[16,32,512]{2,1,0:T(8,128)S(1)}, bf16[16,32,512]{2,1,0:T(8,128)(2,1)S(1)}) custom-call(bf16[16,48,128]{2,1,0:T(8,128)(2,1)S(1)} %all_to_all.25.got_ref, bf16[128,16384]{1,0:T(8,128)(2,1)S(1)} %get-tuple-element.12.w_ref), custom_call_target="tpu_custom_call" | custom-call | flops 134217728 | bytes 4194304 | tf_op jit(solution)/shard_map/project/pallas_call | solution.py:204
  20.1 2.1 %collective-permute-start = (bf16[16,32,512]{2,1,0:T(8,128)(2,1)S(1)}, bf16[16,32,512]{2,1,0:T(8,128)(2,1)S(1)}, u32[]{:S(2)}, u32[]{:S(2)}) collective-permute-start(bf16[16,32,512]{2,1,0:T(8,128)(2,1)S(1)} %get-tuple-element.14), channel_id=1, source_target_pairs={{0,1},{1,0},{2,3},{3,2},{4,5},{5,4},{6,7},{7,6},{8,9},{9,8},{10,11... | collective-permute-start | bytes 1572872 | tf_op jit(solution)/shard_map/ppermute | solution.py:388
  22.2 1.5 %collective-permute-done.got_ref = bf16[16,32,512]{2,1,0:T(8,128)(2,1)S(1)} collective-permute-done((bf16[16,32,512]{2,1,0:T(8,128)(2,1)S(1)}, bf16[16,32,512]{2,1,0:T(8,128)(2,1)S(1)}, u32[]{:S(2)}, u32[]{:S(2)}) %collective-permute-start) | collective-permute-done | bytes 524320 | tf_op jit(solution)/shard_map/ppermute | solution.py:388
  23.7 0.1 add_pair.1
  23.8 0.0 slice-start.1
  23.8 13.8 %all_to_all.26.parts_ref = bf16[16,32,512]{2,1,0:T(8,128)(2,1)S(1)} all-to-all(bf16[16,32,512]{2,1,0:T(8,128)(2,1)S(1)} %add_pair.1), channel_id=1, replica_groups=mesh['kv'=16,'head'=8] {'kv'}, dimensions={0} | all-to-all | bytes 1048576 | tf_op jit(solution)/shard_map/all_to_all | solution.py:384
  37.6 0.1 stream.1.mine_ref
  37.7 1.4 %collective-permute-start.1 = (bf16[32,640]{1,0:T(8,128)(2,1)S(1)}, bf16[32,640]{1,0:T(8,128)(2,1)S(1)}, u32[]{:S(2)}, u32[]{:S(2)}) collective-permute-start(bf16[32,640]{1,0:T(8,128)(2,1)S(1)} %stream.1.mine_ref), channel_id=1, source_target_pairs={{0,2},{1,3},{2,0},{3,1},{4,6},{5,7},{6,4},{7,5},{8,10},{9,11},{10,... | collective-permute-start | bytes 122888 | tf_op jit(solution)/shard_map/ppermute | solution.py:388
  39.1 1.6 %collective-permute-done.1.got_ref = bf16[32,640]{1,0:T(8,128)(2,1)S(1)} collective-permute-done((bf16[32,640]{1,0:T(8,128)(2,1)S(1)}, bf16[32,640]{1,0:T(8,128)(2,1)S(1)}, u32[]{:S(2)}, u32[]{:S(2)}) %collective-permute-start.1) | collective-permute-done | bytes 40992 | tf_op jit(solution)/shard_map/ppermute | solution.py:388
  40.6 2.8 %collective-permute-start.2 = (bf16[32,640]{1,0:T(8,128)(2,1)S(1)}, bf16[32,640]{1,0:T(8,128)(2,1)S(1)}, u32[]{:S(2)}, u32[]{:S(2)}) collective-permute-start(bf16[32,640]{1,0:T(8,128)(2,1)S(1)} %add_swapped.2.mine_ref), channel_id=1, source_target_pairs={{0,6},{1,7},{2,4},{3,5},{4,2},{5,3},{6,0},{7,1},{8,14},{9,15},{10,... | collective-permute-start | bytes 122888 | tf_op jit(solution)/shard_map/ppermute | solution.py:388
  43.5 1.4 %collective-permute-done.2.got_ref = bf16[32,640]{1,0:T(8,128)(2,1)S(1)} collective-permute-done((bf16[32,640]{1,0:T(8,128)(2,1)S(1)}, bf16[32,640]{1,0:T(8,128)(2,1)S(1)}, u32[]{:S(2)}, u32[]{:S(2)}) %collective-permute-start.2) | collective-permute-done | bytes 40992 | tf_op jit(solution)/shard_map/ppermute | solution.py:388
  44.9 0.0 slice-start.3
  44.9 4.4 %collective-permute-start.3 = (bf16[32,640]{1,0:T(8,128)(2,1)S(1)}, bf16[32,640]{1,0:T(8,128)(2,1)S(1)}, u32[]{:S(2)}, u32[]{:S(2)}) collective-permute-start(bf16[32,640]{1,0:T(8,128)(2,1)S(1)} %add_swapped.3.mine_ref), channel_id=1, source_target_pairs={{0,1},{1,0},{2,3},{3,2},{4,5},{5,4},{6,7},{7,6},{8,9},{9,8},{10,11... | collective-permute-start | bytes 122888 | tf_op jit(solution)/shard_map/ppermute | solution.py:388
  49.3 0.9 collective-permute-done.3.other_ref
  50.2 2.4 %gate_up.1 = (bf16[16,4,3456]{2,1,0:T(4,128)(2,1)S(1)}, f32[32,128]{1,0:T(8,128)S(1)}) custom-call(bf16[32,640]{1,0:T(8,128)(2,1)S(1)} %add_swapped.3.mine_ref, bf16[32,640]{1,0:T(8,128)(2,1)S(1)} %collective-permute-done.3.other_ref, bf16[1024,3328]{1,0:T(8,128)(2,1)S(1)} %bitcast.3, bf16[1024,3328]{1,0:T(8,128)(2,1)S(1)} %copy-done), custom_call_target="tpu_custom_call" | custom-call | flops 436207616 | bytes 13631488 | tf_op jit(solution)/shard_map/gate_up/pallas_call | solution.py:309
  52.6 12.7 %all_to_all.27.parts_ref = bf16[16,4,3456]{2,1,0:T(4,128)(2,1)S(1)} all-to-all(bf16[16,4,3456]{2,1,0:T(4,128)(2,1)S(1)} %get-tuple-element.16), channel_id=1, replica_groups=mesh['kv'=16,'head'=8] {'kv'}, dimensions={0} | all-to-all | bytes 884736 | tf_op jit(solution)/shard_map/all_to_all | solution.py:384
  65.3 0.2 hidden_units.1
  65.5 10.4 %all_to_all.28.parts_ref = bf16[16,4,1664]{2,1,0:T(4,128)(2,1)S(1)} all-to-all(bf16[16,4,1664]{2,1,0:T(4,128)(2,1)S(1)} %hidden_units.1), channel_id=1, replica_groups=mesh['kv'=16,'head'=8] {'kv'}, dimensions={0} | all-to-all | bytes 425984 | tf_op jit(solution)/shard_map/all_to_all | solution.py:384
  75.9 1.3 %down.1 = bf16[8,32,128]{2,1,0:T(8,128)(2,1)S(1)} custom-call(bf16[16,4,1664]{2,1,0:T(4,128)(2,1)S(1)} %all_to_all.28.parts_ref, bf16[3328,1024]{1,0:T(8,128)(2,1)S(1)} %bitcast.5), custom_call_target="tpu_custom_call" | custom-call | flops 218103808 | bytes 6815744 | tf_op jit(solution)/shard_map/down/pallas_call | solution.py:353
  77.2 11.8 %all_to_all.29.parts_ref = bf16[8,32,128]{2,1,0:T(8,128)(2,1)S(1)} all-to-all(bf16[8,32,128]{2,1,0:T(8,128)(2,1)S(1)} %down.1), channel_id=1, replica_groups=mesh['kv'=16,'head'=8] {'head'}, dimensions={0} | all-to-all | bytes 131072 | tf_op jit(solution)/shard_map/all_to_all | solution.py:384
  89.0 0.6 finish.1
  (15 shorter events, 0.0 us)
Async XLA Ops:
  0.0 37.6 %copy-start.1 = (bf16[32,128]{1,0:T(8,128)(2,1)S(1)}, bf16[32,128]{1,0:T(8,128)(2,1)}, u32[]{:S(2)}) copy-start(bf16[32,128]{1,0:T(8,128)(2,1)} %res_ref.1) | copy-start | bytes 24580
  0.0 37.6 %copy-start.2 = (bf16[128]{0:T(256)(128)(2,1)S(1)}, bf16[128]{0:T(256)(128)(2,1)}, u32[]{:S(2)}) copy-start(bf16[128]{0:T(256)(128)(2,1)} %param.22) | copy-start | bytes 772
  3.4 34.2 %copy-start = (bf16[1024,3328]{1,0:T(8,128)(2,1)S(1)}, bf16[1024,3328]{1,0:T(8,128)(2,1)}, u32[]{:S(2)}) copy-start(bf16[1024,3328]{1,0:T(8,128)(2,1)} %up_w.1) | copy-start | bytes 20447236
  19.1 21.6 %slice-start = ((s8[6815744]{0:T(1024)(128)(4,1)}), s8[4194304]{0:T(1024)(128)(4,1)S(1)}, s32[]{:S(2)}) async-start(s8[6815744]{0:T(1024)(128)(4,1)} %bitcast.2), calls=%async_computation.5 | async-start | bytes 8388608
  20.1 3.6 %collective-permute-start = (bf16[16,32,512]{2,1,0:T(8,128)(2,1)S(1)}, bf16[16,32,512]{2,1,0:T(8,128)(2,1)S(1)}, u32[]{:S(2)}, u32[]{:S(2)}) collective-permute-start(bf16[16,32,512]{2,1,0:T(8,128)(2,1)S(1)} %get-tuple-element.14), channel_id=1, source_target_pairs={{0,1},{1,0},{2,3},{3,2},{4,5},{5,4},{6,7},{7,6},{8,9},{9,8},{10,11... | collective-permute-start | bytes 1572872 | tf_op jit(solution)/shard_map/ppermute | solution.py:388
  23.8 16.8 %slice-start.1 = ((s8[6815744]{0:T(1024)(128)(4,1)}), s8[2621440]{0:T(1024)(128)(4,1)S(1)}, s32[]{:S(2)}) async-start(s8[6815744]{0:T(1024)(128)(4,1)} %bitcast.2), calls=%async_computation.6 | async-start | bytes 5242880
  37.7 2.9 %collective-permute-start.1 = (bf16[32,640]{1,0:T(8,128)(2,1)S(1)}, bf16[32,640]{1,0:T(8,128)(2,1)S(1)}, u32[]{:S(2)}, u32[]{:S(2)}) collective-permute-start(bf16[32,640]{1,0:T(8,128)(2,1)S(1)} %stream.1.mine_ref), channel_id=1, source_target_pairs={{0,2},{1,3},{2,0},{3,1},{4,6},{5,7},{6,4},{7,5},{8,10},{9,11},{10,... | collective-permute-start | bytes 122888 | tf_op jit(solution)/shard_map/ppermute | solution.py:388
  40.6 4.2 %collective-permute-start.2 = (bf16[32,640]{1,0:T(8,128)(2,1)S(1)}, bf16[32,640]{1,0:T(8,128)(2,1)S(1)}, u32[]{:S(2)}, u32[]{:S(2)}) collective-permute-start(bf16[32,640]{1,0:T(8,128)(2,1)S(1)} %add_swapped.2.mine_ref), channel_id=1, source_target_pairs={{0,6},{1,7},{2,4},{3,5},{4,2},{5,3},{6,0},{7,1},{8,14},{9,15},{10,... | collective-permute-start | bytes 122888 | tf_op jit(solution)/shard_map/ppermute | solution.py:388
  44.9 31.1 %slice-start.2 = ((s8[6815744]{0:T(1024)(128)(4,1)}), s8[4194304]{0:T(1024)(128)(4,1)S(1)}, s32[]{:S(2)}) async-start(s8[6815744]{0:T(1024)(128)(4,1)} %bitcast.4), calls=%async_computation.7 | async-start | bytes 8388608
  44.9 31.0 %slice-start.3 = ((s8[6815744]{0:T(1024)(128)(4,1)}), s8[2621440]{0:T(1024)(128)(4,1)S(1)}, s32[]{:S(2)}) async-start(s8[6815744]{0:T(1024)(128)(4,1)} %bitcast.4), calls=%async_computation.8 | async-start | bytes 5242880
  44.9 5.3 %collective-permute-start.3 = (bf16[32,640]{1,0:T(8,128)(2,1)S(1)}, bf16[32,640]{1,0:T(8,128)(2,1)S(1)}, u32[]{:S(2)}, u32[]{:S(2)}) collective-permute-start(bf16[32,640]{1,0:T(8,128)(2,1)S(1)} %add_swapped.3.mine_ref), channel_id=1, source_target_pairs={{0,1},{1,0},{2,3},{3,2},{4,5},{5,4},{6,7},{7,6},{8,9},{9,8},{10,11... | collective-permute-start | bytes 122888 | tf_op jit(solution)/shard_map/ppermute | solution.py:388

commit v6 on v4

--- a/solution.py
+++ b/solution.py
@@ -26,7 +26,7 @@
 BF16 = jnp.bfloat16
 MIB = 1 << 20
 W_SPACE = pltpu.HBM
-ATTENTION_ROOM = 57
+ATTENTION_ROOM = 58
 
 
 def whole(shape, space=pltpu.VMEM):
@@ -77,7 +77,7 @@
 def attention_kernel(
     table_hbm, lengths_hbm, q_hbm, k_hbm, v_hbm, new_k_hbm, new_v_hbm, w_hbm,
     out_ref, w_ref, table, lengths, q_ref, k_ref, v_ref, new_k, new_v, sems, w_sems,
-    q_rows, scores, tops, sums, numer,
+    q_rows, scores, outs, tops, sums, numer,
 ):
     pairs = (
         (table_hbm, table), (lengths_hbm, lengths), (q_hbm, q_ref), (k_hbm, k_ref), (v_hbm, v_ref),
@@ -86,9 +86,6 @@
     copies = [pltpu.make_async_copy(src, dst, sems.at[i]) for i, (src, dst) in enumerate(pairs)]
     for i in (2, 0, 1, 5, 6, 3, 4):
         copies[i].start()
-    w_copies = parts_of_copy(w_hbm, w_ref, w_sems)
-    for copy in w_copies:
-        copy.start()
     tops[...] = jnp.full(tops.shape, -1e30, F32)
     sums[...] = jnp.zeros(sums.shape, F32)
     numer[...] = jnp.zeros(numer.shape, F32)
@@ -114,6 +111,9 @@
     copies[0].wait()
     copies[1].wait()
     copies[3].wait()
+    w_copies = parts_of_copy(w_hbm, w_ref, w_sems)
+    for copy in w_copies:
+        copy.start()
     rows_of = []
     for b in range(SLOTS):
         seq = table[0, b]
@@ -126,18 +126,22 @@
         )
         masked = jnp.where(lane < limit, raw * unit, -1e30)
         scores[b] = masked
-        tops[here, :] = jnp.maximum(tops[here, :], jnp.max(masked, axis=1, keepdims=True))
+        outs[b] = jnp.broadcast_to(jnp.max(masked, axis=1, keepdims=True), (ROWS, HD))
+    for b in range(SLOTS):
+        tops[rows_of[b], :] = jnp.maximum(tops[rows_of[b], :], outs[b])
     tops[...] = tops[...].astype(BF16).astype(F32)
     new_scale = jnp.exp(new_max - tops[mine, :])
     sums[mine, :] = new_scale * (expo_own + expo_prev)
     numer[mine, :] = new_scale * new_out
     copies[4].wait()
     for b in range(SLOTS):
-        here = rows_of[b]
         masked = scores[b]
-        expo = jnp.where(masked > -1e29, jnp.exp(masked - tops[here, :]), 0.0)
-        sums[here, :] += jnp.sum(expo, axis=1, keepdims=True)
-        numer[here, :] += jnp.dot(expo.astype(BF16), v_ref[b, 0], preferred_element_type=F32)
+        expo = jnp.where(masked > -1e29, jnp.exp(masked - tops[rows_of[b], :]), 0.0)
+        scores[b] = jnp.broadcast_to(jnp.sum(expo, axis=1, keepdims=True), (ROWS, HD))
+        outs[b] = jnp.dot(expo.astype(BF16), v_ref[b, 0], preferred_element_type=F32)
+    for b in range(SLOTS):
+        sums[rows_of[b], :] += scores[b]
+        numer[rows_of[b], :] += outs[b]
     by_head = lax.broadcasted_iota(jnp.int32, (GROUP, HD), 1)
     stats = jnp.zeros((GROUP, HD), F32)
     for row in range(ROWS):
@@ -157,6 +161,7 @@
     table, lengths, queries, key_cache, value_cache, new_keys, new_values, weight
 ):
     tall = pltpu.VMEM((ROWS * GROUP, HD), F32)
+    by_slot = pltpu.VMEM((SLOTS, ROWS, HD), F32)
     arrays = (queries, key_cache, value_cache, new_keys, new_values)
     return pl.pallas_call(
         attention_kernel,
@@ -166,14 +171,25 @@
         scratch_shapes=[pltpu.SMEM(table.shape, jnp.int32), pltpu.SMEM(lengths.shape, jnp.int32)]
         + [pltpu.VMEM(a.shape, BF16) for a in arrays]
         + [pltpu.SemaphoreType.DMA((7,)), pltpu.SemaphoreType.DMA((8,))]
-        + [tall, pltpu.VMEM((SLOTS, ROWS, HD), F32), tall, tall, tall],
+        + [tall, by_slot, by_slot, tall, tall, tall],
         compiler_params=params(ATTENTION_ROOM),
         cost_estimate=cost(SLOTS * ROWS * HD * HD * 4, 4 * SLOTS * HD * HD),
         name="attention",
     )(*[in_hbm(a) for a in (table, lengths, *arrays, weight)])
 
 
-def project_kernel(got_ref, w_ref, keep_ref, give_ref):
+def project_part(first, attn, w_ref, keep_ref, give_ref):
+    even = is_even()
+    for d in range(N_KV // 2):
+        for y in range(4):
+            at = (first + d) * 2 * HALF + y * TILE
+            both = jnp.dot(attn, w_ref[:, at : at + TILE], preferred_element_type=F32)
+            here = slice(y * OWN, (y + 1) * OWN)
+            keep_ref[d, :, here] = jnp.where(even, both[:, :OWN], both[:, OWN:])
+            give_ref[d, :, here] = jnp.where(even, both[:, OWN:], both[:, :OWN]).astype(BF16)
+
+
+def early_kernel(got_ref, w_ref, keep_ref, give_ref, attn_ref):
     row = lax.broadcasted_iota(jnp.int32, (N_KV, HD), 0)
     stats = jnp.zeros((N_KV, HD), F32)
     for i in range(N_KV):
@@ -189,45 +205,49 @@
     for i in range(N_KV):
         total += scales[:, i : i + 1] * got_ref[i, :ROWS, :].astype(F32)
     attn = (total / denom).astype(BF16)
-    even = is_even()
-    for d in range(N_KV):
-        for y in range(4):
-            at = d * 2 * HALF + y * TILE
-            both = jnp.dot(attn, w_ref[:, at : at + TILE], preferred_element_type=F32)
-            here = slice(y * OWN, (y + 1) * OWN)
-            keep_ref[d, :, here] = jnp.where(even, both[:, :OWN], both[:, OWN:])
-            give_ref[d, :, here] = jnp.where(even, both[:, OWN:], both[:, :OWN]).astype(BF16)
-
-
-def project(got, weight):
+    attn_ref[...] = attn
+    project_part(0, attn, w_ref, keep_ref, give_ref)
+
+
+def late_kernel(attn_ref, w_ref, keep_ref, give_ref):
+    project_part(N_KV // 2, attn_ref[...], w_ref, keep_ref, give_ref)
+
+
+def project(kernel, given, weight, name):
+    out = (N_KV // 2, ROWS, HALF)
+    outs = [shape(out, F32), shape(out, BF16)]
+    if kernel is early_kernel:
+        outs.append(shape((ROWS, HD), BF16))
+    return pl.pallas_call(
+        kernel,
+        out_shape=outs,
+        in_specs=[whole(given.shape), whole(weight.shape)],
+        out_specs=[whole(o.shape) for o in outs],
+        compiler_params=params(8),
+        cost_estimate=cost(ROWS * weight.size, weight.size),
+        name=name,
+    )(given, in_vmem(weight))
+
+
+def pair_kernel(keep_a, got_a, keep_b, got_b, out_ref):
+    half = N_KV // 2
+    out_ref[:half] = (keep_a[...] + got_a[...].astype(F32)).astype(BF16)
+    out_ref[half:] = (keep_b[...] + got_b[...].astype(F32)).astype(BF16)
+
+
+def add_pair(*parts):
     out = (N_KV, ROWS, HALF)
     return pl.pallas_call(
-        project_kernel,
-        out_shape=[shape(out, F32), shape(out, BF16)],
-        in_specs=[whole(got.shape), whole(weight.shape)],
-        out_specs=[whole(out), whole(out)],
-        compiler_params=params(8),
-        cost_estimate=cost(2 * ROWS * weight.size, 2 * weight.size),
-        name="project",
-    )(got, weight)
-
-
-def pair_kernel(keep_ref, got_ref, out_ref):
-    out_ref[...] = (keep_ref[...] + got_ref[...].astype(F32)).astype(BF16)
-
-
-def add_pair(keep, got):
-    return pl.pallas_call(
         pair_kernel,
-        out_shape=shape(keep.shape, BF16),
-        in_specs=[whole(keep.shape), whole(got.shape)],
-        out_specs=whole(keep.shape),
+        out_shape=shape(out, BF16),
+        in_specs=[whole(a.shape) for a in parts],
+        out_specs=whole(out),
         compiler_params=params(8),
         name="add_pair",
-    )(keep, got)
-
-
-def stream_kernel(_, parts_ref, res_ref, gain_ref, out_ref):
+    )(*parts)
+
+
+def stream_kernel(parts_ref, res_ref, gain_ref, out_ref):
     total = parts_ref[0].astype(F32)
     for i in range(1, N_KV):
         total += parts_ref[i].astype(F32)
@@ -242,16 +262,16 @@
         out_ref[y] = message
 
 
-def stream(parts, residual, gain, held):
+def stream(parts, residual, gain):
     out = (4, ROWS, HALF + OWN)
     return pl.pallas_call(
         stream_kernel,
         out_shape=shape(out, BF16),
-        in_specs=[whole(a.shape) for a in (held, parts, residual, gain)],
+        in_specs=[whole(a.shape) for a in (parts, residual, gain)],
         out_specs=whole(out),
         compiler_params=params(8),
         name="stream",
-    )(in_vmem(held), parts, residual, gain)
+    )(parts, residual, gain)
 
 
 def column_kernel(_, parts_ref, out_ref):
@@ -416,11 +436,12 @@
     partials, weight = attention_partials(
         block_table, lengths, queries, key_cache, value_cache, new_keys, new_values, out_weight[0, 0]
     )
-    keep, give = project(exchange(partials, "kv"), weight)
-    parts = exchange(add_pair(keep, swap(give, 1)), "kv")
+    keep_a, give_a, attn = project(early_kernel, exchange(partials, "kv"), weight, "project_early")
+    keep_b, give_b = project(late_kernel, attn, weight, "project_late")
+    parts = exchange(add_pair(keep_a, swap(give_a, 1), keep_b, swap(give_b, 1)), "kv")
     same_core = [[2 * y + c for y in range(4)] for c in range(2)]
-    parts = exchange(stream(parts, residual, norm_gain[None], w_up), "head", same_core)
-    here = add_columns(parts, w_gate)
+    parts = exchange(stream(parts, residual, norm_gain[None]), "head", same_core)
+    here = add_columns(parts, w_up)
     gates, own = gate_up(here, swap(here, 1), w_gate, w_up)
     hidden = exchange(hidden_units(exchange(gates, "kv")), "kv")
     parts = exchange(down(hidden, w_down), "head")

time: 89.1 us -> 90 us (1.010)
    ppermute x2 -> x3, starting transfers between devices: 5.66 us -> 5.97 us  [swap(): return lax.ppermute(value, 'head', [(j, j ^ step) for j in range(KVH)])]
    ppermute x2 -> x3, waiting for transfers between devices: 2.41 us -> 2.36 us  [swap(): return lax.ppermute(value, 'head', [(j, j ^ step) for j in range(KVH)])]
  transfers between devices with their start and end apart: 2 -> 3, of which waited for: 2 -> 3; matrix products, arithmetic and copies ran while one was open for 0% -> 0% of each run, Pallas kernels for 0% -> 0%
where the time goes in v6:
time: 90 us; the launch traced here: 89.6 us
  blocking collectives  71.3 us (79%)
  Pallas kernels  9.91 us (11%)
  starting transfers between devices  5.97 us (7%)
  waiting for transfers between devices  2.36 us (3%)
    all_to_all x6, blocking collectives, exchange(): lax.all_to_all(value, axis, 0, 0, axis_index_groups=groups, tiled=True)  71.3 us
    ppermute x3, starting transfers between devices, swap(): return lax.ppermute(value, 'head', [(j, j ^ step) for j in range(KVH)])  5.97 us
    pallas_call x1, Pallas kernels, attention_partials(): pl.pallas_call(attention_kernel, out_shape=[pltpu.VMEM((GROUP, ROWS + 16,...  4.01 us
    pallas_call x1, Pallas kernels, gate_up(): pl.pallas_call(gate_kernel, out_shape=[shape(wide, BF16), shape((ROWS, OW...  2.44 us
    ppermute x3, waiting for transfers between devices, swap(): return lax.ppermute(value, 'head', [(j, j ^ step) for j in range(KVH)])  2.36 us
  transfers between devices with their start and end apart: 3, of which 3 were waited for; matrix products, arithmetic and copies ran while one was open for 0% of the time, Pallas kernels for 0%

profile of v6, /device:TPU:1, one launch (start us, length us, event | category | flops | bytes accessed | tf_op | source)
XLA Modules:
  0.0 89.6 jit_solution(8968703436003455955)
XLA Ops:
  0.0 4.0 %attention.1 = (bf16[16,48,128]{2,1,0:T(8,128)(2,1)S(1)}, bf16[128,16384]{1,0:T(8,128)(2,1)S(1)}) custom-call(s32[2,24]{1,0:T(2,128)} %table_hbm.1, s32[16]{0:T(128)} %lengths_hbm.1, bf16[32,2048]{1,0:T(8,128)(2,1)} %q_hbm.1, bf16[24,1,128,128]{3,2,1,0:T(8,128)(2,1)} %k_hbm.1, bf16[24,1,128,128]{3,2,1,0:T(8,128)(2,1)} %v_hbm.1, bf16[32,128]{1,0:T(8,128)(2,1)} %new_k_hbm.1, ...), custom_call_target="tpu_custom_call" | custom-call | flops 50331648 | bytes 1572864 | tf_op jit(solution)/shard_map/attention/pallas_call | solution.py:166
  4.0 0.0 copy-start
  4.0 0.0 slice-start
  4.1 15.6 %all_to_all.30.got_ref = bf16[16,48,128]{2,1,0:T(8,128)(2,1)S(1)} all-to-all(bf16[16,48,128]{2,1,0:T(8,128)(2,1)S(1)} %get-tuple-element.14), channel_id=1, replica_groups=mesh['kv'=16,'head'=8] {'kv'}, dimensions={0} | all-to-all | bytes 393216 | tf_op jit(solution)/shard_map/all_to_all | solution.py:414
  19.7 0.8 project_early.1
  20.5 2.1 %collective-permute-start = (bf16[8,32,512]{2,1,0:T(8,128)(2,1)S(1)}, bf16[8,32,512]{2,1,0:T(8,128)(2,1)S(1)}, u32[]{:S(2)}, u32[]{:S(2)}) collective-permute-start(bf16[8,32,512]{2,1,0:T(8,128)(2,1)S(1)} %get-tuple-element.17), channel_id=1, source_target_pairs={{0,1},{1,0},{2,3},{3,2},{4,5},{5,4},{6,7},{7,6},{8,9},{9,8},{10,11... | collective-permute-start | bytes 786440 | tf_op jit(solution)/shard_map/ppermute | solution.py:418
  22.6 0.4 project_late.1
  23.0 0.1 collective-permute-start.1
  23.1 0.6 collective-permute-done.got_a
  23.7 0.9 collective-permute-done.1.got_b
  24.6 0.1 add_pair.1
  24.7 13.3 %all_to_all.31.parts_ref = bf16[16,32,512]{2,1,0:T(8,128)(2,1)S(1)} all-to-all(bf16[16,32,512]{2,1,0:T(8,128)(2,1)S(1)} %add_pair.1), channel_id=1, replica_groups=mesh['kv'=16,'head'=8] {'kv'}, dimensions={0} | all-to-all | bytes 1048576 | tf_op jit(solution)/shard_map/all_to_all | solution.py:414
  38.0 0.1 stream.1
  38.1 9.1 %all_to_all.32.parts_ref = bf16[4,32,640]{2,1,0:T(8,128)(2,1)S(1)} all-to-all(bf16[4,32,640]{2,1,0:T(8,128)(2,1)S(1)} %stream.1), channel_id=1, replica_groups={{0,2,4,6},{1,3,5,7},{8,10,12,14},{9,11,13,15},{16,18,20,22},{17,19,21,2..., dimensions={0} | all-to-all | bytes 327680 | tf_op jit(solution)/shard_map/all_to_all | solution.py:414
  47.2 0.0 slice-start.3
  47.3 3.8 %collective-permute-start.2 = (bf16[32,640]{1,0:T(8,128)(2,1)S(1)}, bf16[32,640]{1,0:T(8,128)(2,1)S(1)}, u32[]{:S(2)}, u32[]{:S(2)}) collective-permute-start(bf16[32,640]{1,0:T(8,128)(2,1)S(1)} %add_columns.1.mine_ref), channel_id=1, source_target_pairs={{0,1},{1,0},{2,3},{3,2},{4,5},{5,4},{6,7},{7,6},{8,9},{9,8},{10,11... | collective-permute-start | bytes 122888 | tf_op jit(solution)/shard_map/ppermute | solution.py:418
  51.0 0.9 collective-permute-done.2.other_ref
  51.9 2.4 %gate_up.1 = (bf16[16,4,3456]{2,1,0:T(4,128)(2,1)S(1)}, f32[32,128]{1,0:T(8,128)S(1)}) custom-call(bf16[32,640]{1,0:T(8,128)(2,1)S(1)} %add_columns.1.mine_ref, bf16[32,640]{1,0:T(8,128)(2,1)S(1)} %collective-permute-done.2.other_ref, bf16[1024,3328]{1,0:T(8,128)(2,1)S(1)} %bitcast.7, bf16[1024,3328]{1,0:T(8,128)(2,1)S(1)} %bitcast.3), custom_call_target="tpu_custom_call" | custom-call | flops 436207616 | bytes 13631488 | tf_op jit(solution)/shard_map/gate_up/pallas_call | solution.py:339
  54.4 12.7 %all_to_all.33.parts_ref = bf16[16,4,3456]{2,1,0:T(4,128)(2,1)S(1)} all-to-all(bf16[16,4,3456]{2,1,0:T(4,128)(2,1)S(1)} %get-tuple-element.22), channel_id=1, replica_groups=mesh['kv'=16,'head'=8] {'kv'}, dimensions={0} | all-to-all | bytes 884736 | tf_op jit(solution)/shard_map/all_to_all | solution.py:414
  67.0 0.2 hidden_units.1
  67.3 10.4 %all_to_all.34.parts_ref = bf16[16,4,1664]{2,1,0:T(4,128)(2,1)S(1)} all-to-all(bf16[16,4,1664]{2,1,0:T(4,128)(2,1)S(1)} %hidden_units.1), channel_id=1, replica_groups=mesh['kv'=16,'head'=8] {'kv'}, dimensions={0} | all-to-all | bytes 425984 | tf_op jit(solution)/shard_map/all_to_all | solution.py:414
  77.7 1.3 %down.1 = bf16[8,32,128]{2,1,0:T(8,128)(2,1)S(1)} custom-call(bf16[16,4,1664]{2,1,0:T(4,128)(2,1)S(1)} %all_to_all.34.parts_ref, bf16[3328,1024]{1,0:T(8,128)(2,1)S(1)} %bitcast.5), custom_call_target="tpu_custom_call" | custom-call | flops 218103808 | bytes 6815744 | tf_op jit(solution)/shard_map/down/pallas_call | solution.py:383
  78.9 10.1 %all_to_all.35.parts_ref = bf16[8,32,128]{2,1,0:T(8,128)(2,1)S(1)} all-to-all(bf16[8,32,128]{2,1,0:T(8,128)(2,1)S(1)} %down.1), channel_id=1, replica_groups=mesh['kv'=16,'head'=8] {'head'}, dimensions={0} | all-to-all | bytes 131072 | tf_op jit(solution)/shard_map/all_to_all | solution.py:414
  89.0 0.6 finish.1
  (17 shorter events, 0.1 us)
Async XLA Ops:
  4.0 34.0 %copy-start = (bf16[32,128]{1,0:T(8,128)(2,1)S(1)}, bf16[32,128]{1,0:T(8,128)(2,1)}, u32[]{:S(2)}) copy-start(bf16[32,128]{1,0:T(8,128)(2,1)} %res_ref.1) | copy-start | bytes 24580
  4.0 34.0 %copy-start.1 = (bf16[128]{0:T(256)(128)(2,1)S(1)}, bf16[128]{0:T(256)(128)(2,1)}, u32[]{:S(2)}) copy-start(bf16[128]{0:T(256)(128)(2,1)} %param.22) | copy-start | bytes 772
  4.0 43.2 %slice-start = ((s8[6815744]{0:T(1024)(128)(4,1)}), s8[4194304]{0:T(1024)(128)(4,1)S(1)}, s32[]{:S(2)}) async-start(s8[6815744]{0:T(1024)(128)(4,1)} %bitcast.2), calls=%async_computation.6 | async-start | bytes 8388608
  20.5 3.2 %collective-permute-start = (bf16[8,32,512]{2,1,0:T(8,128)(2,1)S(1)}, bf16[8,32,512]{2,1,0:T(8,128)(2,1)S(1)}, u32[]{:S(2)}, u32[]{:S(2)}) collective-permute-start(bf16[8,32,512]{2,1,0:T(8,128)(2,1)S(1)} %get-tuple-element.17), channel_id=1, source_target_pairs={{0,1},{1,0},{2,3},{3,2},{4,5},{5,4},{6,7},{7,6},{8,9},{9,8},{10,11... | collective-permute-start | bytes 786440 | tf_op jit(solution)/shard_map/ppermute | solution.py:418
  22.6 24.7 %slice-start.1 = ((s8[6815744]{0:T(1024)(128)(4,1)}), s8[2621440]{0:T(1024)(128)(4,1)S(1)}, s32[]{:S(2)}) async-start(s8[6815744]{0:T(1024)(128)(4,1)} %bitcast.2), calls=%async_computation.7 | async-start | bytes 5242880
  22.6 29.4 %slice-start.4 = ((s8[6815744]{0:T(1024)(128)(4,1)}), s8[4194304]{0:T(1024)(128)(4,1)S(1)}, s32[]{:S(2)}) async-start(s8[6815744]{0:T(1024)(128)(4,1)} %bitcast.6), calls=%async_computation.10 | async-start | bytes 8388608
  23.0 1.6 %collective-permute-start.1 = (bf16[8,32,512]{2,1,0:T(8,128)(2,1)S(1)}, bf16[8,32,512]{2,1,0:T(8,128)(2,1)S(1)}, u32[]{:S(2)}, u32[]{:S(2)}) collective-permute-start(bf16[8,32,512]{2,1,0:T(8,128)(2,1)S(1)} %get-tuple-element.20), channel_id=1, source_target_pairs={{0,1},{1,0},{2,3},{3,2},{4,5},{5,4},{6,7},{7,6},{8,9},{9,8},{10,11... | collective-permute-start | bytes 786440 | tf_op jit(solution)/shard_map/ppermute | solution.py:418
  38.0 13.9 %slice-start.5 = ((s8[6815744]{0:T(1024)(128)(4,1)}), s8[2621440]{0:T(1024)(128)(4,1)S(1)}, s32[]{:S(2)}) async-start(s8[6815744]{0:T(1024)(128)(4,1)} %bitcast.6), calls=%async_computation.11 | async-start | bytes 5242880
  47.2 30.5 %slice-start.2 = ((s8[6815744]{0:T(1024)(128)(4,1)}), s8[4194304]{0:T(1024)(128)(4,1)S(1)}, s32[]{:S(2)}) async-start(s8[6815744]{0:T(1024)(128)(4,1)} %bitcast.4), calls=%async_computation.8 | async-start | bytes 8388608
  47.2 30.4 %slice-start.3 = ((s8[6815744]{0:T(1024)(128)(4,1)}), s8[2621440]{0:T(1024)(128)(4,1)S(1)}, s32[]{:S(2)}) async-start(s8[6815744]{0:T(1024)(128)(4,1)} %bitcast.4), calls=%async_computation.9 | async-start | bytes 5242880
  47.3 4.7 %collective-permute-start.2 = (bf16[32,640]{1,0:T(8,128)(2,1)S(1)}, bf16[32,640]{1,0:T(8,128)(2,1)S(1)}, u32[]{:S(2)}, u32[]{:S(2)}) collective-permute-start(bf16[32,640]{1,0:T(8,128)(2,1)S(1)} %add_columns.1.mine_ref), channel_id=1, source_target_pairs={{0,1},{1,0},{2,3},{3,2},{4,5},{5,4},{6,7},{7,6},{8,9},{9,8},{10,11... | collective-permute-start | bytes 122888 | tf_op jit(solution)/shard_map/ppermute | solution.py:418

commit v7 on v4

--- a/solution.py
+++ b/solution.py
@@ -36,6 +36,10 @@
 
 def is_even():
     return lax.axis_index("head") % 2 == 0
+
+
+def place_of(kv, even):
+    return jnp.where(even, kv, N_KV - 1 - kv)
 
 
 def own_y():
@@ -147,8 +151,9 @@
         stats = jnp.where(by_head == row + ROWS, high, stats)
         stats = jnp.where(by_head == row + 2 * ROWS, sums[heads, :] - high, stats)
     for g in range(GROUP):
-        out_ref[g, :ROWS, :] = numer[pl.ds(g, ROWS, stride=GROUP), :].astype(BF16)
-        out_ref[g, ROWS:, :] = jnp.broadcast_to(stats[g : g + 1, :], (16, HD)).astype(BF16)
+        at = place_of(g, is_even())
+        out_ref[at, :ROWS, :] = numer[pl.ds(g, ROWS, stride=GROUP), :].astype(BF16)
+        out_ref[at, ROWS:, :] = jnp.broadcast_to(stats[g : g + 1, :], (16, HD)).astype(BF16)
     for copy in w_copies:
         copy.wait()
 
@@ -195,8 +200,8 @@
             at = d * 2 * HALF + y * TILE
             both = jnp.dot(attn, w_ref[:, at : at + TILE], preferred_element_type=F32)
             here = slice(y * OWN, (y + 1) * OWN)
-            keep_ref[d, :, here] = jnp.where(even, both[:, :OWN], both[:, OWN:])
-            give_ref[d, :, here] = jnp.where(even, both[:, OWN:], both[:, :OWN]).astype(BF16)
+            keep_ref[place_of(d, even), :, here] = jnp.where(even, both[:, :OWN], both[:, OWN:])
+            give_ref[place_of(d, ~even), :, here] = jnp.where(even, both[:, OWN:], both[:, :OWN]).astype(BF16)
 
 
 def project(got, weight):
@@ -300,7 +305,7 @@
     lane = lax.broadcasted_iota(jnp.int32, (ROWS, EXTRA), 1)
     squares = jnp.where(lane < 64, high, total - high).astype(BF16).astype(F32)
     for d in range(N_KV):
-        out_ref[d, :, 2 * PART :] = squares[4 * (d // 2) : 4 * (d // 2) + 4, :].astype(BF16)
+        out_ref[place_of(d, even), :, 2 * PART :] = squares[4 * (d // 2) : 4 * (d // 2) + 4, :].astype(BF16)
     for tile in range(tiles):
         for which in range(2):
             weight = (gate_w, up_w)[which]
@@ -311,7 +316,7 @@
                 at = which * PART + column % 13 * 128
                 for r in range(8):
                     piece = result[4 * r : 4 * r + 4, part * 128 : (part + 1) * 128]
-                    out_ref[2 * r + column // 13, :, at : at + 128] = piece.astype(BF16)
+                    out_ref[place_of(2 * r + column // 13, even), :, at : at + 128] = piece.astype(BF16)
 
 
 def gate_up(mine, other, w_gate, w_up):
@@ -352,7 +357,8 @@
 
 def down_kernel(parts_ref, w_ref, out_ref, x):
     for d in range(N_KV):
-        x[4 * (d // 2) : 4 * (d // 2) + 4, d % 2 * PART : d % 2 * PART + PART] = parts_ref[d].astype(F32)
+        piece = parts_ref[place_of(d, is_even())].astype(F32)
+        x[4 * (d // 2) : 4 * (d // 2) + 4, d % 2 * PART : d % 2 * PART + PART] = piece
     total = jnp.dot(x[...].astype(BF16), w_ref[...], preferred_element_type=F32)
     for i in range(KVH):
         out_ref[i] = total[:, i * OWN : (i + 1) * OWN].astype(BF16)
@@ -392,6 +398,14 @@
 
 def exchange(value, axis, groups=None):
     return lax.all_to_all(value, axis, 0, 0, axis_index_groups=groups, tiled=True)
+
+
+def exchange_kv(value):
+    groups = [
+        [kv * KVH + head for kv in (range(N_KV) if head % 2 == 0 else reversed(range(N_KV)))]
+        for head in range(KVH)
+    ]
+    return exchange(value, ("kv", "head"), groups)
 
 
 def swap(value, step):
@@ -416,13 +430,13 @@
     partials, weight = attention_partials(
         block_table, lengths, queries, key_cache, value_cache, new_keys, new_values, out_weight[0, 0]
     )
-    keep, give = project(exchange(partials, "kv"), weight)
-    parts = exchange(add_pair(keep, swap(give, 1)), "kv")
+    keep, give = project(exchange_kv(partials), weight)
+    parts = exchange_kv(add_pair(keep, swap(give, 1)))
     same_core = [[2 * y + c for y in range(4)] for c in range(2)]
     parts = exchange(stream(parts, residual, norm_gain[None], w_up), "head", same_core)
     here = add_columns(parts, w_gate)
     gates, own = gate_up(here, swap(here, 1), w_gate, w_up)
-    hidden = exchange(hidden_units(exchange(gates, "kv")), "kv")
+    hidden = exchange_kv(hidden_units(exchange_kv(gates)))
     parts = exchange(down(hidden, w_down), "head")
     return finish(own, parts)
 

time: 89.1 us -> 89 us (level)
  blocking collectives: 71.4 us -> 69.1 us
  starting transfers between devices: 5.66 us -> 7.93 us
    all_to_all x6, blocking collectives: 71.4 us -> 69.1 us  [exchange(): lax.all_to_all(value, axis, 0, 0, axis_index_groups=groups, tiled=True)]
    ppermute x2, starting transfers between devices: 5.66 us -> 7.93 us  [swap(): return lax.ppermute(value, 'head', [(j, j ^ step) for j in range(KVH)])]
where the time goes in v7:
time: 89 us; the launch traced here: 88.8 us
  blocking collectives  69.1 us (78%)
  Pallas kernels  9.16 us (10%)
  starting transfers between devices  7.93 us (9%)
  waiting for transfers between devices  2.41 us (3%)
    all_to_all x6, blocking collectives, exchange(): lax.all_to_all(value, axis, 0, 0, axis_index_groups=groups, tiled=True)  69.1 us
    ppermute x2, starting transfers between devices, swap(): return lax.ppermute(value, 'head', [(j, j ^ step) for j in range(KVH)])  7.93 us
    pallas_call x1, Pallas kernels, attention_partials(): pl.pallas_call(attention_kernel, out_shape=[pltpu.VMEM((GROUP, ROWS + 16,...  3.39 us
    pallas_call x1, Pallas kernels, gate_up(): pl.pallas_call(gate_kernel, out_shape=[shape(wide, BF16), shape((ROWS, OW...  2.43 us
    ppermute x2, waiting for transfers between devices, swap(): return lax.ppermute(value, 'head', [(j, j ^ step) for j in range(KVH)])  2.41 us
  transfers between devices with their start and end apart: 2, of which 2 were waited for; matrix products, arithmetic and copies ran while one was open for 0% of the time, Pallas kernels for 0%

profile of v7, /device:TPU:1, one launch (start us, length us, event | category | flops | bytes accessed | tf_op | source)
XLA Modules:
  0.0 88.8 jit_solution(6746825175301285262)
XLA Ops:
  0.0 3.4 %attention.1 = (bf16[16,48,128]{2,1,0:T(8,128)(2,1)S(1)}, bf16[128,16384]{1,0:T(8,128)(2,1)S(1)}) custom-call(s32[2,24]{1,0:T(2,128)} %table_hbm.1, s32[16]{0:T(128)} %lengths_hbm.1, bf16[32,2048]{1,0:T(8,128)(2,1)} %q_hbm.1, bf16[24,1,128,128]{3,2,1,0:T(8,128)(2,1)} %k_hbm.1, bf16[24,1,128,128]{3,2,1,0:T(8,128)(2,1)} %v_hbm.1, bf16[32,128]{1,0:T(8,128)(2,1)} %new_k_hbm.1, ...), custom_call_target="tpu_custom_call" | custom-call | flops 50331648 | bytes 1572864 | tf_op jit(solution)/shard_map/attention/pallas_call | solution.py:166
  3.4 0.0 copy-start
  3.4 13.1 %all_to_all.30.got_ref = bf16[16,48,128]{2,1,0:T(8,128)(2,1)S(1)} all-to-all(bf16[16,48,128]{2,1,0:T(8,128)(2,1)S(1)} %get-tuple-element.11), channel_id=1, replica_groups={{0,8,16,24,32,40,48,56,64,72,80,88,96,104,112,120},{121,113,105,97,89,8..., dimensions={0} | all-to-all | bytes 393216 | tf_op jit(solution)/shard_map/all_to_all | solution.py:400
  16.5 1.1 %project.1 = (f32[16,32,512]{2,1,0:T(8,128)S(1)}, bf16[16,32,512]{2,1,0:T(8,128)(2,1)S(1)}) custom-call(bf16[16,48,128]{2,1,0:T(8,128)(2,1)S(1)} %all_to_all.30.got_ref, bf16[128,16384]{1,0:T(8,128)(2,1)S(1)} %get-tuple-element.12.w_ref), custom_call_target="tpu_custom_call" | custom-call | flops 134217728 | bytes 4194304 | tf_op jit(solution)/shard_map/project/pallas_call | solution.py:209
  17.6 4.5 %collective-permute-start = (bf16[16,32,512]{2,1,0:T(8,128)(2,1)S(1)}, bf16[16,32,512]{2,1,0:T(8,128)(2,1)S(1)}, u32[]{:S(2)}, u32[]{:S(2)}) collective-permute-start(bf16[16,32,512]{2,1,0:T(8,128)(2,1)S(1)} %get-tuple-element.14), channel_id=1, source_target_pairs={{0,1},{1,0},{2,3},{3,2},{4,5},{5,4},{6,7},{7,6},{8,9},{9,8},{10,11... | collective-permute-start | bytes 1572872 | tf_op jit(solution)/shard_map/ppermute | solution.py:412
  22.1 1.5 %collective-permute-done.got_ref = bf16[16,32,512]{2,1,0:T(8,128)(2,1)S(1)} collective-permute-done((bf16[16,32,512]{2,1,0:T(8,128)(2,1)S(1)}, bf16[16,32,512]{2,1,0:T(8,128)(2,1)S(1)}, u32[]{:S(2)}, u32[]{:S(2)}) %collective-permute-start) | collective-permute-done | bytes 524320 | tf_op jit(solution)/shard_map/ppermute | solution.py:412
  23.6 0.1 add_pair.1
  23.7 12.6 %all_to_all.31.parts_ref = bf16[16,32,512]{2,1,0:T(8,128)(2,1)S(1)} all-to-all(bf16[16,32,512]{2,1,0:T(8,128)(2,1)S(1)} %add_pair.1), channel_id=1, replica_groups={{0,8,16,24,32,40,48,56,64,72,80,88,96,104,112,120},{121,113,105,97,89,8..., dimensions={0} | all-to-all | bytes 1048576 | tf_op jit(solution)/shard_map/all_to_all | solution.py:400
  36.3 0.0 copy-done.1
  36.3 0.0 slice-start.1
  36.3 0.1 stream.1
  36.4 9.1 %all_to_all.32.parts_ref = bf16[4,32,640]{2,1,0:T(8,128)(2,1)S(1)} all-to-all(bf16[4,32,640]{2,1,0:T(8,128)(2,1)S(1)} %stream.1), channel_id=1, replica_groups={{0,2,4,6},{1,3,5,7},{8,10,12,14},{9,11,13,15},{16,18,20,22},{17,19,21,2..., dimensions={0} | all-to-all | bytes 327680 | tf_op jit(solution)/shard_map/all_to_all | solution.py:400
  45.5 0.0 slice-done
  45.6 0.0 slice-start.3
  45.6 3.4 %collective-permute-start.1 = (bf16[32,640]{1,0:T(8,128)(2,1)S(1)}, bf16[32,640]{1,0:T(8,128)(2,1)S(1)}, u32[]{:S(2)}, u32[]{:S(2)}) collective-permute-start(bf16[32,640]{1,0:T(8,128)(2,1)S(1)} %add_columns.1.mine_ref), channel_id=1, source_target_pairs={{0,1},{1,0},{2,3},{3,2},{4,5},{5,4},{6,7},{7,6},{8,9},{9,8},{10,11... | collective-permute-start | bytes 122888 | tf_op jit(solution)/shard_map/ppermute | solution.py:412
  49.0 0.9 collective-permute-done.1.other_ref
  49.9 2.4 %gate_up.1 = (bf16[16,4,3456]{2,1,0:T(4,128)(2,1)S(1)}, f32[32,128]{1,0:T(8,128)S(1)}) custom-call(bf16[32,640]{1,0:T(8,128)(2,1)S(1)} %add_columns.1.mine_ref, bf16[32,640]{1,0:T(8,128)(2,1)S(1)} %collective-permute-done.1.other_ref, bf16[1024,3328]{1,0:T(8,128)(2,1)S(1)} %bitcast.3, bf16[1024,3328]{1,0:T(8,128)(2,1)S(1)} %copy-done), custom_call_target="tpu_custom_call" | custom-call | flops 436207616 | bytes 13631488 | tf_op jit(solution)/shard_map/gate_up/pallas_call | solution.py:324
  52.3 12.6 %all_to_all.33.parts_ref = bf16[16,4,3456]{2,1,0:T(4,128)(2,1)S(1)} all-to-all(bf16[16,4,3456]{2,1,0:T(4,128)(2,1)S(1)} %get-tuple-element.16), channel_id=1, replica_groups={{0,8,16,24,32,40,48,56,64,72,80,88,96,104,112,120},{121,113,105,97,89,8..., dimensions={0} | all-to-all | bytes 884736 | tf_op jit(solution)/shard_map/all_to_all | solution.py:400
  64.9 0.2 hidden_units.1
  65.1 11.2 %all_to_all.34.parts_ref = bf16[16,4,1664]{2,1,0:T(4,128)(2,1)S(1)} all-to-all(bf16[16,4,1664]{2,1,0:T(4,128)(2,1)S(1)} %hidden_units.1), channel_id=1, replica_groups={{0,8,16,24,32,40,48,56,64,72,80,88,96,104,112,120},{121,113,105,97,89,8..., dimensions={0} | all-to-all | bytes 425984 | tf_op jit(solution)/shard_map/all_to_all | solution.py:400
  76.3 0.0 slice-done.3
  76.3 1.3 %down.1 = bf16[8,32,128]{2,1,0:T(8,128)(2,1)S(1)} custom-call(bf16[16,4,1664]{2,1,0:T(4,128)(2,1)S(1)} %all_to_all.34.parts_ref, bf16[3328,1024]{1,0:T(8,128)(2,1)S(1)} %bitcast.5), custom_call_target="tpu_custom_call" | custom-call | flops 218103808 | bytes 6815744 | tf_op jit(solution)/shard_map/down/pallas_call | solution.py:369
  77.6 10.6 %all_to_all.35.parts_ref = bf16[8,32,128]{2,1,0:T(8,128)(2,1)S(1)} all-to-all(bf16[8,32,128]{2,1,0:T(8,128)(2,1)S(1)} %down.1), channel_id=1, replica_groups=mesh['kv'=16,'head'=8] {'head'}, dimensions={0} | all-to-all | bytes 131072 | tf_op jit(solution)/shard_map/all_to_all | solution.py:400
  88.1 0.6 finish.1
  (11 shorter events, 0.0 us)
Async XLA Ops:
  0.0 36.3 %copy-start.1 = (bf16[32,128]{1,0:T(8,128)(2,1)S(1)}, bf16[32,128]{1,0:T(8,128)(2,1)}, u32[]{:S(2)}) copy-start(bf16[32,128]{1,0:T(8,128)(2,1)} %res_ref.1) | copy-start | bytes 24580
  0.0 36.3 %copy-start.2 = (bf16[128]{0:T(256)(128)(2,1)S(1)}, bf16[128]{0:T(256)(128)(2,1)}, u32[]{:S(2)}) copy-start(bf16[128]{0:T(256)(128)(2,1)} %param.22) | copy-start | bytes 772
  3.4 32.9 %copy-start = (bf16[1024,3328]{1,0:T(8,128)(2,1)S(1)}, bf16[1024,3328]{1,0:T(8,128)(2,1)}, u32[]{:S(2)}) copy-start(bf16[1024,3328]{1,0:T(8,128)(2,1)} %up_w.1) | copy-start | bytes 20447236
  16.5 29.0 %slice-start = ((s8[6815744]{0:T(1024)(128)(4,1)}), s8[4194304]{0:T(1024)(128)(4,1)S(1)}, s32[]{:S(2)}) async-start(s8[6815744]{0:T(1024)(128)(4,1)} %bitcast.2), calls=%async_computation.6 | async-start | bytes 8388608
  17.6 6.0 %collective-permute-start = (bf16[16,32,512]{2,1,0:T(8,128)(2,1)S(1)}, bf16[16,32,512]{2,1,0:T(8,128)(2,1)S(1)}, u32[]{:S(2)}, u32[]{:S(2)}) collective-permute-start(bf16[16,32,512]{2,1,0:T(8,128)(2,1)S(1)} %get-tuple-element.14), channel_id=1, source_target_pairs={{0,1},{1,0},{2,3},{3,2},{4,5},{5,4},{6,7},{7,6},{8,9},{9,8},{10,11... | collective-permute-start | bytes 1572872 | tf_op jit(solution)/shard_map/ppermute | solution.py:412
  36.3 9.2 %slice-start.1 = ((s8[6815744]{0:T(1024)(128)(4,1)}), s8[2621440]{0:T(1024)(128)(4,1)S(1)}, s32[]{:S(2)}) async-start(s8[6815744]{0:T(1024)(128)(4,1)} %bitcast.2), calls=%async_computation.7 | async-start | bytes 5242880
  45.5 30.7 %slice-start.2 = ((s8[6815744]{0:T(1024)(128)(4,1)}), s8[4194304]{0:T(1024)(128)(4,1)S(1)}, s32[]{:S(2)}) async-start(s8[6815744]{0:T(1024)(128)(4,1)} %bitcast.4), calls=%async_computation.8 | async-start | bytes 8388608
  45.6 30.7 %slice-start.3 = ((s8[6815744]{0:T(1024)(128)(4,1)}), s8[2621440]{0:T(1024)(128)(4,1)S(1)}, s32[]{:S(2)}) async-start(s8[6815744]{0:T(1024)(128)(4,1)} %bitcast.4), calls=%async_computation.9 | async-start | bytes 5242880
  45.6 4.3 %collective-permute-start.1 = (bf16[32,640]{1,0:T(8,128)(2,1)S(1)}, bf16[32,640]{1,0:T(8,128)(2,1)S(1)}, u32[]{:S(2)}, u32[]{:S(2)}) collective-permute-start(bf16[32,640]{1,0:T(8,128)(2,1)S(1)} %add_columns.1.mine_ref), channel_id=1, source_target_pairs={{0,1},{1,0},{2,3},{3,2},{4,5},{5,4},{6,7},{7,6},{8,9},{9,8},{10,11... | collective-permute-start | bytes 122888 | tf_op jit(solution)/shard_map/ppermute | solution.py:412

commit v8 on v4

--- a/solution.py
+++ b/solution.py
@@ -36,6 +36,12 @@
 
 def is_even():
     return lax.axis_index("head") % 2 == 0
+
+
+BACK = tuple(reversed(range(N_KV)))
+Z_FIRST = tuple(4 * x + z for z in range(4) for x in range(4))
+SNAKE = tuple(4 * x + (3 - z if x % 2 else z) for x in range(4) for z in range(4))
+MERGE_ORDER, PROJ_ORDER, GATE_ORDER, HIDDEN_ORDER = BACK, Z_FIRST, SNAKE, Z_FIRST
 
 
 def own_y():
@@ -147,8 +153,9 @@
         stats = jnp.where(by_head == row + ROWS, high, stats)
         stats = jnp.where(by_head == row + 2 * ROWS, sums[heads, :] - high, stats)
     for g in range(GROUP):
-        out_ref[g, :ROWS, :] = numer[pl.ds(g, ROWS, stride=GROUP), :].astype(BF16)
-        out_ref[g, ROWS:, :] = jnp.broadcast_to(stats[g : g + 1, :], (16, HD)).astype(BF16)
+        at = MERGE_ORDER.index(g)
+        out_ref[at, :ROWS, :] = numer[pl.ds(g, ROWS, stride=GROUP), :].astype(BF16)
+        out_ref[at, ROWS:, :] = jnp.broadcast_to(stats[g : g + 1, :], (16, HD)).astype(BF16)
     for copy in w_copies:
         copy.wait()
 
@@ -195,8 +202,9 @@
             at = d * 2 * HALF + y * TILE
             both = jnp.dot(attn, w_ref[:, at : at + TILE], preferred_element_type=F32)
             here = slice(y * OWN, (y + 1) * OWN)
-            keep_ref[d, :, here] = jnp.where(even, both[:, :OWN], both[:, OWN:])
-            give_ref[d, :, here] = jnp.where(even, both[:, OWN:], both[:, :OWN]).astype(BF16)
+            place = PROJ_ORDER.index(d)
+            keep_ref[place, :, here] = jnp.where(even, both[:, :OWN], both[:, OWN:])
+            give_ref[place, :, here] = jnp.where(even, both[:, OWN:], both[:, :OWN]).astype(BF16)
 
 
 def project(got, weight):
@@ -300,7 +308,7 @@
     lane = lax.broadcasted_iota(jnp.int32, (ROWS, EXTRA), 1)
     squares = jnp.where(lane < 64, high, total - high).astype(BF16).astype(F32)
     for d in range(N_KV):
-        out_ref[d, :, 2 * PART :] = squares[4 * (d // 2) : 4 * (d // 2) + 4, :].astype(BF16)
+        out_ref[GATE_ORDER.index(d), :, 2 * PART :] = squares[4 * (d // 2) : 4 * (d // 2) + 4, :].astype(BF16)
     for tile in range(tiles):
         for which in range(2):
             weight = (gate_w, up_w)[which]
@@ -311,7 +319,7 @@
                 at = which * PART + column % 13 * 128
                 for r in range(8):
                     piece = result[4 * r : 4 * r + 4, part * 128 : (part + 1) * 128]
-                    out_ref[2 * r + column // 13, :, at : at + 128] = piece.astype(BF16)
+                    out_ref[GATE_ORDER.index(2 * r + column // 13), :, at : at + 128] = piece.astype(BF16)
 
 
 def gate_up(mine, other, w_gate, w_up):
@@ -352,7 +360,8 @@
 
 def down_kernel(parts_ref, w_ref, out_ref, x):
     for d in range(N_KV):
-        x[4 * (d // 2) : 4 * (d // 2) + 4, d % 2 * PART : d % 2 * PART + PART] = parts_ref[d].astype(F32)
+        piece = parts_ref[HIDDEN_ORDER.index(d)].astype(F32)
+        x[4 * (d // 2) : 4 * (d // 2) + 4, d % 2 * PART : d % 2 * PART + PART] = piece
     total = jnp.dot(x[...].astype(BF16), w_ref[...], preferred_element_type=F32)
     for i in range(KVH):
         out_ref[i] = total[:, i * OWN : (i + 1) * OWN].astype(BF16)
@@ -392,6 +401,11 @@
 
 def exchange(value, axis, groups=None):
     return lax.all_to_all(value, axis, 0, 0, axis_index_groups=groups, tiled=True)
+
+
+def exchange_kv(value, order):
+    groups = [[kv * KVH + head for kv in order] for head in range(KVH)]
+    return exchange(value, ("kv", "head"), groups)
 
 
 def swap(value, step):
@@ -416,13 +430,13 @@
     partials, weight = attention_partials(
         block_table, lengths, queries, key_cache, value_cache, new_keys, new_values, out_weight[0, 0]
     )
-    keep, give = project(exchange(partials, "kv"), weight)
-    parts = exchange(add_pair(keep, swap(give, 1)), "kv")
+    keep, give = project(exchange_kv(partials, MERGE_ORDER), weight)
+    parts = exchange_kv(add_pair(keep, swap(give, 1)), PROJ_ORDER)
     same_core = [[2 * y + c for y in range(4)] for c in range(2)]
     parts = exchange(stream(parts, residual, norm_gain[None], w_up), "head", same_core)
     here = add_columns(parts, w_gate)
     gates, own = gate_up(here, swap(here, 1), w_gate, w_up)
-    hidden = exchange(hidden_units(exchange(gates, "kv")), "kv")
+    hidden = exchange_kv(hidden_units(exchange_kv(gates, GATE_ORDER)), HIDDEN_ORDER)
     parts = exchange(down(hidden, w_down), "head")
     return finish(own, parts)
 

time: 89.1 us -> 88.1 us (0.989)
  no operation moved by 1% of the time
where the time goes in v8:
time: 88.1 us; the launch traced here: 87.8 us
  blocking collectives  71.2 us (81%)
  Pallas kernels  9.15 us (10%)
  starting transfers between devices  4.97 us (6%)
  waiting for transfers between devices  2.41 us (3%)
    all_to_all x6, blocking collectives, exchange(): lax.all_to_all(value, axis, 0, 0, axis_index_groups=groups, tiled=True)  71.2 us
    ppermute x2, starting transfers between devices, swap(): return lax.ppermute(value, 'head', [(j, j ^ step) for j in range(KVH)])  4.97 us
    pallas_call x1, Pallas kernels, attention_partials(): pl.pallas_call(attention_kernel, out_shape=[pltpu.VMEM((GROUP, ROWS + 16,...  3.39 us
    pallas_call x1, Pallas kernels, gate_up(): pl.pallas_call(gate_kernel, out_shape=[shape(wide, BF16), shape((ROWS, OW...  2.43 us
    ppermute x2, waiting for transfers between devices, swap(): return lax.ppermute(value, 'head', [(j, j ^ step) for j in range(KVH)])  2.41 us
  transfers between devices with their start and end apart: 2, of which 2 were waited for; matrix products, arithmetic and copies ran while one was open for 0% of the time, Pallas kernels for 0%

profile of v8, /device:TPU:1, one launch (start us, length us, event | category | flops | bytes accessed | tf_op | source)
XLA Modules:
  0.0 87.8 jit_solution(11616185698520190378)
XLA Ops:
  0.0 3.4 %attention.1 = (bf16[16,48,128]{2,1,0:T(8,128)(2,1)S(1)}, bf16[128,16384]{1,0:T(8,128)(2,1)S(1)}) custom-call(s32[2,24]{1,0:T(2,128)} %table_hbm.1, s32[16]{0:T(128)} %lengths_hbm.1, bf16[32,2048]{1,0:T(8,128)(2,1)} %q_hbm.1, bf16[24,1,128,128]{3,2,1,0:T(8,128)(2,1)} %k_hbm.1, bf16[24,1,128,128]{3,2,1,0:T(8,128)(2,1)} %v_hbm.1, bf16[32,128]{1,0:T(8,128)(2,1)} %new_k_hbm.1, ...), custom_call_target="tpu_custom_call" | custom-call | flops 50331648 | bytes 1572864 | tf_op jit(solution)/shard_map/attention/pallas_call | solution.py:168
  3.4 0.0 copy-start
  3.4 13.3 %all_to_all.30.got_ref = bf16[16,48,128]{2,1,0:T(8,128)(2,1)S(1)} all-to-all(bf16[16,48,128]{2,1,0:T(8,128)(2,1)S(1)} %get-tuple-element.11), channel_id=1, replica_groups={{120,112,104,96,88,80,72,64,56,48,40,32,24,16,8,0},{121,113,105,97,89,8..., dimensions={0} | all-to-all | bytes 393216 | tf_op jit(solution)/shard_map/all_to_all | solution.py:403
  16.8 1.1 %project.1 = (f32[16,32,512]{2,1,0:T(8,128)S(1)}, bf16[16,32,512]{2,1,0:T(8,128)(2,1)S(1)}) custom-call(bf16[16,48,128]{2,1,0:T(8,128)(2,1)S(1)} %all_to_all.30.got_ref, bf16[128,16384]{1,0:T(8,128)(2,1)S(1)} %get-tuple-element.12.w_ref), custom_call_target="tpu_custom_call" | custom-call | flops 134217728 | bytes 4194304 | tf_op jit(solution)/shard_map/project/pallas_call | solution.py:212
  17.8 1.7 %collective-permute-start = (bf16[16,32,512]{2,1,0:T(8,128)(2,1)S(1)}, bf16[16,32,512]{2,1,0:T(8,128)(2,1)S(1)}, u32[]{:S(2)}, u32[]{:S(2)}) collective-permute-start(bf16[16,32,512]{2,1,0:T(8,128)(2,1)S(1)} %get-tuple-element.14), channel_id=1, source_target_pairs={{0,1},{1,0},{2,3},{3,2},{4,5},{5,4},{6,7},{7,6},{8,9},{9,8},{10,11... | collective-permute-start | bytes 1572872 | tf_op jit(solution)/shard_map/ppermute | solution.py:412
  19.5 1.5 %collective-permute-done.got_ref = bf16[16,32,512]{2,1,0:T(8,128)(2,1)S(1)} collective-permute-done((bf16[16,32,512]{2,1,0:T(8,128)(2,1)S(1)}, bf16[16,32,512]{2,1,0:T(8,128)(2,1)S(1)}, u32[]{:S(2)}, u32[]{:S(2)}) %collective-permute-start) | collective-permute-done | bytes 524320 | tf_op jit(solution)/shard_map/ppermute | solution.py:412
  21.0 0.1 add_pair.1
  21.1 15.6 %all_to_all.31.parts_ref = bf16[16,32,512]{2,1,0:T(8,128)(2,1)S(1)} all-to-all(bf16[16,32,512]{2,1,0:T(8,128)(2,1)S(1)} %add_pair.1), channel_id=1, replica_groups={{0,32,64,96,8,40,72,104,16,48,80,112,24,56,88,120},{1,33,65,97,9,41,73,..., dimensions={0} | all-to-all | bytes 1048576 | tf_op jit(solution)/shard_map/all_to_all | solution.py:403
  36.7 0.0 copy-done.1
  36.7 0.0 copy-done.2
  36.7 0.0 copy-done
  36.7 0.0 slice-start.1
  36.8 0.1 stream.1
  36.8 9.1 %all_to_all.32.parts_ref = bf16[4,32,640]{2,1,0:T(8,128)(2,1)S(1)} all-to-all(bf16[4,32,640]{2,1,0:T(8,128)(2,1)S(1)} %stream.1), channel_id=1, replica_groups={{0,2,4,6},{1,3,5,7},{8,10,12,14},{9,11,13,15},{16,18,20,22},{17,19,21,2..., dimensions={0} | all-to-all | bytes 327680 | tf_op jit(solution)/shard_map/all_to_all | solution.py:403
  46.0 0.0 slice-start.3
  46.0 3.3 %collective-permute-start.1 = (bf16[32,640]{1,0:T(8,128)(2,1)S(1)}, bf16[32,640]{1,0:T(8,128)(2,1)S(1)}, u32[]{:S(2)}, u32[]{:S(2)}) collective-permute-start(bf16[32,640]{1,0:T(8,128)(2,1)S(1)} %add_columns.1.mine_ref), channel_id=1, source_target_pairs={{0,1},{1,0},{2,3},{3,2},{4,5},{5,4},{6,7},{7,6},{8,9},{9,8},{10,11... | collective-permute-start | bytes 122888 | tf_op jit(solution)/shard_map/ppermute | solution.py:412
  49.3 0.9 collective-permute-done.1.other_ref
  50.2 2.4 %gate_up.1 = (bf16[16,4,3456]{2,1,0:T(4,128)(2,1)S(1)}, f32[32,128]{1,0:T(8,128)S(1)}) custom-call(bf16[32,640]{1,0:T(8,128)(2,1)S(1)} %add_columns.1.mine_ref, bf16[32,640]{1,0:T(8,128)(2,1)S(1)} %collective-permute-done.1.other_ref, bf16[1024,3328]{1,0:T(8,128)(2,1)S(1)} %bitcast.3, bf16[1024,3328]{1,0:T(8,128)(2,1)S(1)} %copy-done), custom_call_target="tpu_custom_call" | custom-call | flops 436207616 | bytes 13631488 | tf_op jit(solution)/shard_map/gate_up/pallas_call | solution.py:327
  52.6 11.6 %all_to_all.33.parts_ref = bf16[16,4,3456]{2,1,0:T(4,128)(2,1)S(1)} all-to-all(bf16[16,4,3456]{2,1,0:T(4,128)(2,1)S(1)} %get-tuple-element.16), channel_id=1, replica_groups={{0,8,16,24,56,48,40,32,64,72,80,88,120,112,104,96},{1,9,17,25,57,49,41,..., dimensions={0} | all-to-all | bytes 884736 | tf_op jit(solution)/shard_map/all_to_all | solution.py:403
  64.2 0.2 hidden_units.1
  64.4 11.4 %all_to_all.34.parts_ref = bf16[16,4,1664]{2,1,0:T(4,128)(2,1)S(1)} all-to-all(bf16[16,4,1664]{2,1,0:T(4,128)(2,1)S(1)} %hidden_units.1), channel_id=1, replica_groups={{0,32,64,96,8,40,72,104,16,48,80,112,24,56,88,120},{1,33,65,97,9,41,73,..., dimensions={0} | all-to-all | bytes 425984 | tf_op jit(solution)/shard_map/all_to_all | solution.py:403
  75.8 1.3 %down.1 = bf16[8,32,128]{2,1,0:T(8,128)(2,1)S(1)} custom-call(bf16[16,4,1664]{2,1,0:T(4,128)(2,1)S(1)} %all_to_all.34.parts_ref, bf16[3328,1024]{1,0:T(8,128)(2,1)S(1)} %bitcast.5), custom_call_target="tpu_custom_call" | custom-call | flops 218103808 | bytes 6815744 | tf_op jit(solution)/shard_map/down/pallas_call | solution.py:372
  77.0 10.2 %all_to_all.35.parts_ref = bf16[8,32,128]{2,1,0:T(8,128)(2,1)S(1)} all-to-all(bf16[8,32,128]{2,1,0:T(8,128)(2,1)S(1)} %down.1), channel_id=1, replica_groups=mesh['kv'=16,'head'=8] {'head'}, dimensions={0} | all-to-all | bytes 131072 | tf_op jit(solution)/shard_map/all_to_all | solution.py:403
  87.2 0.6 finish.1
  (11 shorter events, 0.0 us)
Async XLA Ops:
  0.0 36.7 %copy-start.1 = (bf16[32,128]{1,0:T(8,128)(2,1)S(1)}, bf16[32,128]{1,0:T(8,128)(2,1)}, u32[]{:S(2)}) copy-start(bf16[32,128]{1,0:T(8,128)(2,1)} %res_ref.1) | copy-start | bytes 24580
  0.0 36.7 %copy-start.2 = (bf16[128]{0:T(256)(128)(2,1)S(1)}, bf16[128]{0:T(256)(128)(2,1)}, u32[]{:S(2)}) copy-start(bf16[128]{0:T(256)(128)(2,1)} %param.22) | copy-start | bytes 772
  3.4 33.3 %copy-start = (bf16[1024,3328]{1,0:T(8,128)(2,1)S(1)}, bf16[1024,3328]{1,0:T(8,128)(2,1)}, u32[]{:S(2)}) copy-start(bf16[1024,3328]{1,0:T(8,128)(2,1)} %up_w.1) | copy-start | bytes 20447236
  16.8 29.2 %slice-start = ((s8[6815744]{0:T(1024)(128)(4,1)}), s8[4194304]{0:T(1024)(128)(4,1)S(1)}, s32[]{:S(2)}) async-start(s8[6815744]{0:T(1024)(128)(4,1)} %bitcast.2), calls=%async_computation.6 | async-start | bytes 8388608
  17.8 3.2 %collective-permute-start = (bf16[16,32,512]{2,1,0:T(8,128)(2,1)S(1)}, bf16[16,32,512]{2,1,0:T(8,128)(2,1)S(1)}, u32[]{:S(2)}, u32[]{:S(2)}) collective-permute-start(bf16[16,32,512]{2,1,0:T(8,128)(2,1)S(1)} %get-tuple-element.14), channel_id=1, source_target_pairs={{0,1},{1,0},{2,3},{3,2},{4,5},{5,4},{6,7},{7,6},{8,9},{9,8},{10,11... | collective-permute-start | bytes 1572872 | tf_op jit(solution)/shard_map/ppermute | solution.py:412
  36.7 9.2 %slice-start.1 = ((s8[6815744]{0:T(1024)(128)(4,1)}), s8[2621440]{0:T(1024)(128)(4,1)S(1)}, s32[]{:S(2)}) async-start(s8[6815744]{0:T(1024)(128)(4,1)} %bitcast.2), calls=%async_computation.7 | async-start | bytes 5242880
  46.0 29.8 %slice-start.2 = ((s8[6815744]{0:T(1024)(128)(4,1)}), s8[4194304]{0:T(1024)(128)(4,1)S(1)}, s32[]{:S(2)}) async-start(s8[6815744]{0:T(1024)(128)(4,1)} %bitcast.4), calls=%async_computation.8 | async-start | bytes 8388608
  46.0 29.8 %slice-start.3 = ((s8[6815744]{0:T(1024)(128)(4,1)}), s8[2621440]{0:T(1024)(128)(4,1)S(1)}, s32[]{:S(2)}) async-start(s8[6815744]{0:T(1024)(128)(4,1)} %bitcast.4), calls=%async_computation.9 | async-start | bytes 5242880
  46.0 4.2 %collective-permute-start.1 = (bf16[32,640]{1,0:T(8,128)(2,1)S(1)}, bf16[32,640]{1,0:T(8,128)(2,1)S(1)}, u32[]{:S(2)}, u32[]{:S(2)}) collective-permute-start(bf16[32,640]{1,0:T(8,128)(2,1)S(1)} %add_columns.1.mine_ref), channel_id=1, source_target_pairs={{0,1},{1,0},{2,3},{3,2},{4,5},{5,4},{6,7},{7,6},{8,9},{9,8},{10,11... | collective-permute-start | bytes 122888 | tf_op jit(solution)/shard_map/ppermute | solution.py:412

commit v9 on v8

--- a/solution.py
+++ b/solution.py
@@ -41,7 +41,10 @@
 BACK = tuple(reversed(range(N_KV)))
 Z_FIRST = tuple(4 * x + z for z in range(4) for x in range(4))
 SNAKE = tuple(4 * x + (3 - z if x % 2 else z) for x in range(4) for z in range(4))
-MERGE_ORDER, PROJ_ORDER, GATE_ORDER, HIDDEN_ORDER = BACK, Z_FIRST, SNAKE, Z_FIRST
+SNAKE_BACK = tuple(reversed(SNAKE))
+MERGE_ORDER, PROJ_ORDER, GATE_ORDER, HIDDEN_ORDER = BACK, SNAKE, SNAKE_BACK, SNAKE
+Y_ORDER = (3, 2, 1, 0)
+HEAD_ORDER = tuple(reversed(range(KVH)))
 
 
 def own_y():
@@ -270,7 +273,7 @@
     row = lax.broadcasted_iota(jnp.int32, (ROWS, OWN), 0)
     gains = jnp.zeros((ROWS, OWN), F32)
     for y in range(4):
-        gains = jnp.where(row == y, parts_ref[y, :, HALF:].astype(F32), gains)
+        gains = jnp.where(row == Y_ORDER[y], parts_ref[y, :, HALF:].astype(F32), gains)
     out_ref[:, HALF:] = gains.astype(BF16)
 
 
@@ -364,7 +367,7 @@
         x[4 * (d // 2) : 4 * (d // 2) + 4, d % 2 * PART : d % 2 * PART + PART] = piece
     total = jnp.dot(x[...].astype(BF16), w_ref[...], preferred_element_type=F32)
     for i in range(KVH):
-        out_ref[i] = total[:, i * OWN : (i + 1) * OWN].astype(BF16)
+        out_ref[HEAD_ORDER.index(i)] = total[:, i * OWN : (i + 1) * OWN].astype(BF16)
 
 
 def down(parts, w_down):
@@ -432,12 +435,12 @@
     )
     keep, give = project(exchange_kv(partials, MERGE_ORDER), weight)
     parts = exchange_kv(add_pair(keep, swap(give, 1)), PROJ_ORDER)
-    same_core = [[2 * y + c for y in range(4)] for c in range(2)]
+    same_core = [[2 * y + c for y in Y_ORDER] for c in range(2)]
     parts = exchange(stream(parts, residual, norm_gain[None], w_up), "head", same_core)
     here = add_columns(parts, w_gate)
     gates, own = gate_up(here, swap(here, 1), w_gate, w_up)
     hidden = exchange_kv(hidden_units(exchange_kv(gates, GATE_ORDER)), HIDDEN_ORDER)
-    parts = exchange(down(hidden, w_down), "head")
+    parts = exchange(down(hidden, w_down), "head", [list(HEAD_ORDER)])
     return finish(own, parts)
 
 

time: 88.1 us -> 86.9 us (0.986)
  blocking collectives: 71.2 us -> 69.4 us
    all_to_all x6, blocking collectives: 71.2 us -> 69.4 us  [exchange(): lax.all_to_all(value, axis, 0, 0, axis_index_groups=groups, tiled=True)]
where the time goes in v9:
time: 86.9 us; the launch traced here: 86.6 us
  blocking collectives  69.4 us (80%)
  Pallas kernels  9.17 us (11%)
  starting transfers between devices  5.51 us (6%)
  waiting for transfers between devices  2.41 us (3%)
    all_to_all x6, blocking collectives, exchange(): lax.all_to_all(value, axis, 0, 0, axis_index_groups=groups, tiled=True)  69.4 us
    ppermute x2, starting transfers between devices, swap(): return lax.ppermute(value, 'head', [(j, j ^ step) for j in range(KVH)])  5.51 us
    pallas_call x1, Pallas kernels, attention_partials(): pl.pallas_call(attention_kernel, out_shape=[pltpu.VMEM((GROUP, ROWS + 16,...  3.41 us
    pallas_call x1, Pallas kernels, gate_up(): pl.pallas_call(gate_kernel, out_shape=[shape(wide, BF16), shape((ROWS, OW...  2.43 us
    ppermute x2, waiting for transfers between devices, swap(): return lax.ppermute(value, 'head', [(j, j ^ step) for j in range(KVH)])  2.41 us
  transfers between devices with their start and end apart: 2, of which 2 were waited for; matrix products, arithmetic and copies ran while one was open for 0% of the time, Pallas kernels for 0%

profile of v9, /device:TPU:1, one launch (start us, length us, event | category | flops | bytes accessed | tf_op | source)
XLA Modules:
  0.0 86.6 jit_solution(18340168444659969917)
XLA Ops:
  0.0 3.4 %attention.1 = (bf16[16,48,128]{2,1,0:T(8,128)(2,1)S(1)}, bf16[128,16384]{1,0:T(8,128)(2,1)S(1)}) custom-call(s32[2,24]{1,0:T(2,128)} %table_hbm.1, s32[16]{0:T(128)} %lengths_hbm.1, bf16[32,2048]{1,0:T(8,128)(2,1)} %q_hbm.1, bf16[24,1,128,128]{3,2,1,0:T(8,128)(2,1)} %k_hbm.1, bf16[24,1,128,128]{3,2,1,0:T(8,128)(2,1)} %v_hbm.1, bf16[32,128]{1,0:T(8,128)(2,1)} %new_k_hbm.1, ...), custom_call_target="tpu_custom_call" | custom-call | flops 50331648 | bytes 1572864 | tf_op jit(solution)/shard_map/attention/pallas_call | solution.py:171
  3.4 0.0 copy-start
  3.4 13.3 %all_to_all.30.got_ref = bf16[16,48,128]{2,1,0:T(8,128)(2,1)S(1)} all-to-all(bf16[16,48,128]{2,1,0:T(8,128)(2,1)S(1)} %get-tuple-element.11), channel_id=1, replica_groups={{120,112,104,96,88,80,72,64,56,48,40,32,24,16,8,0},{121,113,105,97,89,8..., dimensions={0} | all-to-all | bytes 393216 | tf_op jit(solution)/shard_map/all_to_all | solution.py:406
  16.8 1.1 %project.1 = (f32[16,32,512]{2,1,0:T(8,128)S(1)}, bf16[16,32,512]{2,1,0:T(8,128)(2,1)S(1)}) custom-call(bf16[16,48,128]{2,1,0:T(8,128)(2,1)S(1)} %all_to_all.30.got_ref, bf16[128,16384]{1,0:T(8,128)(2,1)S(1)} %get-tuple-element.12.w_ref), custom_call_target="tpu_custom_call" | custom-call | flops 134217728 | bytes 4194304 | tf_op jit(solution)/shard_map/project/pallas_call | solution.py:215
  17.8 1.7 %collective-permute-start = (bf16[16,32,512]{2,1,0:T(8,128)(2,1)S(1)}, bf16[16,32,512]{2,1,0:T(8,128)(2,1)S(1)}, u32[]{:S(2)}, u32[]{:S(2)}) collective-permute-start(bf16[16,32,512]{2,1,0:T(8,128)(2,1)S(1)} %get-tuple-element.14), channel_id=1, source_target_pairs={{0,1},{1,0},{2,3},{3,2},{4,5},{5,4},{6,7},{7,6},{8,9},{9,8},{10,11... | collective-permute-start | bytes 1572872 | tf_op jit(solution)/shard_map/ppermute | solution.py:415
  19.5 1.5 %collective-permute-done.got_ref = bf16[16,32,512]{2,1,0:T(8,128)(2,1)S(1)} collective-permute-done((bf16[16,32,512]{2,1,0:T(8,128)(2,1)S(1)}, bf16[16,32,512]{2,1,0:T(8,128)(2,1)S(1)}, u32[]{:S(2)}, u32[]{:S(2)}) %collective-permute-start) | collective-permute-done | bytes 524320 | tf_op jit(solution)/shard_map/ppermute | solution.py:415
  21.0 0.1 add_pair.1
  21.1 14.2 %all_to_all.31.parts_ref = bf16[16,32,512]{2,1,0:T(8,128)(2,1)S(1)} all-to-all(bf16[16,32,512]{2,1,0:T(8,128)(2,1)S(1)} %add_pair.1), channel_id=1, replica_groups={{0,8,16,24,56,48,40,32,64,72,80,88,120,112,104,96},{1,9,17,25,57,49,41,..., dimensions={0} | all-to-all | bytes 1048576 | tf_op jit(solution)/shard_map/all_to_all | solution.py:406
  35.4 0.0 copy-done.1
  35.4 0.0 copy-done.2
  35.4 0.0 slice-start.1
  35.4 0.1 stream.1
  35.5 8.4 %all_to_all.32.parts_ref = bf16[4,32,640]{2,1,0:T(8,128)(2,1)S(1)} all-to-all(bf16[4,32,640]{2,1,0:T(8,128)(2,1)S(1)} %stream.1), channel_id=1, replica_groups={{6,4,2,0},{7,5,3,1},{14,12,10,8},{15,13,11,9},{22,20,18,16},{23,21,19,1..., dimensions={0} | all-to-all | bytes 327680 | tf_op jit(solution)/shard_map/all_to_all | solution.py:406
  43.9 0.0 slice-done
  44.0 0.0 slice-start.3
  44.0 3.8 %collective-permute-start.1 = (bf16[32,640]{1,0:T(8,128)(2,1)S(1)}, bf16[32,640]{1,0:T(8,128)(2,1)S(1)}, u32[]{:S(2)}, u32[]{:S(2)}) collective-permute-start(bf16[32,640]{1,0:T(8,128)(2,1)S(1)} %add_columns.1.mine_ref), channel_id=1, source_target_pairs={{0,1},{1,0},{2,3},{3,2},{4,5},{5,4},{6,7},{7,6},{8,9},{9,8},{10,11... | collective-permute-start | bytes 122888 | tf_op jit(solution)/shard_map/ppermute | solution.py:415
  47.8 0.9 %collective-permute-done.1.other_ref = bf16[32,640]{1,0:T(8,128)(2,1)S(1)} collective-permute-done((bf16[32,640]{1,0:T(8,128)(2,1)S(1)}, bf16[32,640]{1,0:T(8,128)(2,1)S(1)}, u32[]{:S(2)}, u32[]{:S(2)}) %collective-permute-start.1) | collective-permute-done | bytes 40992 | tf_op jit(solution)/shard_map/ppermute | solution.py:415
  48.7 2.4 %gate_up.1 = (bf16[16,4,3456]{2,1,0:T(4,128)(2,1)S(1)}, f32[32,128]{1,0:T(8,128)S(1)}) custom-call(bf16[32,640]{1,0:T(8,128)(2,1)S(1)} %add_columns.1.mine_ref, bf16[32,640]{1,0:T(8,128)(2,1)S(1)} %collective-permute-done.1.other_ref, bf16[1024,3328]{1,0:T(8,128)(2,1)S(1)} %bitcast.3, bf16[1024,3328]{1,0:T(8,128)(2,1)S(1)} %copy-done), custom_call_target="tpu_custom_call" | custom-call | flops 436207616 | bytes 13631488 | tf_op jit(solution)/shard_map/gate_up/pallas_call | solution.py:330
  51.1 12.0 %all_to_all.33.parts_ref = bf16[16,4,3456]{2,1,0:T(4,128)(2,1)S(1)} all-to-all(bf16[16,4,3456]{2,1,0:T(4,128)(2,1)S(1)} %get-tuple-element.16), channel_id=1, replica_groups={{96,104,112,120,88,80,72,64,32,40,48,56,24,16,8,0},{97,105,113,121,89,8..., dimensions={0} | all-to-all | bytes 884736 | tf_op jit(solution)/shard_map/all_to_all | solution.py:406
  63.2 0.2 hidden_units.1
  63.4 11.4 %all_to_all.34.parts_ref = bf16[16,4,1664]{2,1,0:T(4,128)(2,1)S(1)} all-to-all(bf16[16,4,1664]{2,1,0:T(4,128)(2,1)S(1)} %hidden_units.1), channel_id=1, replica_groups={{0,8,16,24,56,48,40,32,64,72,80,88,120,112,104,96},{1,9,17,25,57,49,41,..., dimensions={0} | all-to-all | bytes 425984 | tf_op jit(solution)/shard_map/all_to_all | solution.py:406
  74.8 1.3 %down.1 = bf16[8,32,128]{2,1,0:T(8,128)(2,1)S(1)} custom-call(bf16[16,4,1664]{2,1,0:T(4,128)(2,1)S(1)} %all_to_all.34.parts_ref, bf16[3328,1024]{1,0:T(8,128)(2,1)S(1)} %bitcast.5), custom_call_target="tpu_custom_call" | custom-call | flops 218103808 | bytes 6815744 | tf_op jit(solution)/shard_map/down/pallas_call | solution.py:375
  76.1 9.9 %all_to_all.35.parts_ref = bf16[8,32,128]{2,1,0:T(8,128)(2,1)S(1)} all-to-all(bf16[8,32,128]{2,1,0:T(8,128)(2,1)S(1)} %down.1), channel_id=1, replica_groups={{7,6,5,4,3,2,1,0},{15,14,13,12,11,10,9,8},{23,22,21,20,19,18,17,16},{31..., dimensions={0} | all-to-all | bytes 131072 | tf_op jit(solution)/shard_map/all_to_all | solution.py:406
  86.0 0.6 finish.1
  (11 shorter events, 0.0 us)
Async XLA Ops:
  0.0 35.4 %copy-start.1 = (bf16[32,128]{1,0:T(8,128)(2,1)S(1)}, bf16[32,128]{1,0:T(8,128)(2,1)}, u32[]{:S(2)}) copy-start(bf16[32,128]{1,0:T(8,128)(2,1)} %res_ref.1) | copy-start | bytes 24580
  0.0 35.4 %copy-start.2 = (bf16[128]{0:T(256)(128)(2,1)S(1)}, bf16[128]{0:T(256)(128)(2,1)}, u32[]{:S(2)}) copy-start(bf16[128]{0:T(256)(128)(2,1)} %param.22) | copy-start | bytes 772
  3.4 32.0 %copy-start = (bf16[1024,3328]{1,0:T(8,128)(2,1)S(1)}, bf16[1024,3328]{1,0:T(8,128)(2,1)}, u32[]{:S(2)}) copy-start(bf16[1024,3328]{1,0:T(8,128)(2,1)} %up_w.1) | copy-start | bytes 20447236
  16.8 27.2 %slice-start = ((s8[6815744]{0:T(1024)(128)(4,1)}), s8[4194304]{0:T(1024)(128)(4,1)S(1)}, s32[]{:S(2)}) async-start(s8[6815744]{0:T(1024)(128)(4,1)} %bitcast.2), calls=%async_computation.6 | async-start | bytes 8388608
  17.8 3.2 %collective-permute-start = (bf16[16,32,512]{2,1,0:T(8,128)(2,1)S(1)}, bf16[16,32,512]{2,1,0:T(8,128)(2,1)S(1)}, u32[]{:S(2)}, u32[]{:S(2)}) collective-permute-start(bf16[16,32,512]{2,1,0:T(8,128)(2,1)S(1)} %get-tuple-element.14), channel_id=1, source_target_pairs={{0,1},{1,0},{2,3},{3,2},{4,5},{5,4},{6,7},{7,6},{8,9},{9,8},{10,11... | collective-permute-start | bytes 1572872 | tf_op jit(solution)/shard_map/ppermute | solution.py:415
  35.4 8.5 %slice-start.1 = ((s8[6815744]{0:T(1024)(128)(4,1)}), s8[2621440]{0:T(1024)(128)(4,1)S(1)}, s32[]{:S(2)}) async-start(s8[6815744]{0:T(1024)(128)(4,1)} %bitcast.2), calls=%async_computation.7 | async-start | bytes 5242880
  43.9 30.9 %slice-start.2 = ((s8[6815744]{0:T(1024)(128)(4,1)}), s8[4194304]{0:T(1024)(128)(4,1)S(1)}, s32[]{:S(2)}) async-start(s8[6815744]{0:T(1024)(128)(4,1)} %bitcast.4), calls=%async_computation.8 | async-start | bytes 8388608
  44.0 30.9 %slice-start.3 = ((s8[6815744]{0:T(1024)(128)(4,1)}), s8[2621440]{0:T(1024)(128)(4,1)S(1)}, s32[]{:S(2)}) async-start(s8[6815744]{0:T(1024)(128)(4,1)} %bitcast.4), calls=%async_computation.9 | async-start | bytes 5242880
  44.0 4.7 %collective-permute-start.1 = (bf16[32,640]{1,0:T(8,128)(2,1)S(1)}, bf16[32,640]{1,0:T(8,128)(2,1)S(1)}, u32[]{:S(2)}, u32[]{:S(2)}) collective-permute-start(bf16[32,640]{1,0:T(8,128)(2,1)S(1)} %add_columns.1.mine_ref), channel_id=1, source_target_pairs={{0,1},{1,0},{2,3},{3,2},{4,5},{5,4},{6,7},{7,6},{8,9},{9,8},{10,11... | collective-permute-start | bytes 122888 | tf_op jit(solution)/shard_map/ppermute | solution.py:415

commit v10 on v9

--- a/solution.py
+++ b/solution.py
@@ -39,12 +39,10 @@
 
 
 BACK = tuple(reversed(range(N_KV)))
-Z_FIRST = tuple(4 * x + z for z in range(4) for x in range(4))
 SNAKE = tuple(4 * x + (3 - z if x % 2 else z) for x in range(4) for z in range(4))
-SNAKE_BACK = tuple(reversed(SNAKE))
-MERGE_ORDER, PROJ_ORDER, GATE_ORDER, HIDDEN_ORDER = BACK, SNAKE, SNAKE_BACK, SNAKE
+MERGE_ORDER, PROJ_ORDER, GATE_ORDER, HIDDEN_ORDER = BACK, BACK, SNAKE, BACK
 Y_ORDER = (3, 2, 1, 0)
-HEAD_ORDER = tuple(reversed(range(KVH)))
+HEAD_ORDER = (7, 5, 3, 1, 6, 4, 2, 0)
 
 
 def own_y():

time: 86.9 us -> 85.8 us (0.987)
  no operation moved by 1% of the time
where the time goes in v10:
time: 85.8 us; the launch traced here: 85.5 us
  blocking collectives  68.7 us (80%)
  Pallas kernels  9.16 us (11%)
  starting transfers between devices  5.12 us (6%)
  waiting for transfers between devices  2.41 us (3%)
    all_to_all x6, blocking collectives, exchange(): lax.all_to_all(value, axis, 0, 0, axis_index_groups=groups, tiled=True)  68.7 us
    ppermute x2, starting transfers between devices, swap(): return lax.ppermute(value, 'head', [(j, j ^ step) for j in range(KVH)])  5.12 us
    pallas_call x1, Pallas kernels, attention_partials(): pl.pallas_call(attention_kernel, out_shape=[pltpu.VMEM((GROUP, ROWS + 16,...  3.4 us
    pallas_call x1, Pallas kernels, gate_up(): pl.pallas_call(gate_kernel, out_shape=[shape(wide, BF16), shape((ROWS, OW...  2.43 us
    ppermute x2, waiting for transfers between devices, swap(): return lax.ppermute(value, 'head', [(j, j ^ step) for j in range(KVH)])  2.41 us
  transfers between devices with their start and end apart: 2, of which 2 were waited for; matrix products, arithmetic and copies ran while one was open for 0% of the time, Pallas kernels for 0%

profile of v10, /device:TPU:1, one launch (start us, length us, event | category | flops | bytes accessed | tf_op | source)
XLA Modules:
  0.0 85.5 jit_solution(12837322157889384695)
XLA Ops:
  0.0 3.4 %attention.1 = (bf16[16,48,128]{2,1,0:T(8,128)(2,1)S(1)}, bf16[128,16384]{1,0:T(8,128)(2,1)S(1)}) custom-call(s32[2,24]{1,0:T(2,128)} %table_hbm.1, s32[16]{0:T(128)} %lengths_hbm.1, bf16[32,2048]{1,0:T(8,128)(2,1)} %q_hbm.1, bf16[24,1,128,128]{3,2,1,0:T(8,128)(2,1)} %k_hbm.1, bf16[24,1,128,128]{3,2,1,0:T(8,128)(2,1)} %v_hbm.1, bf16[32,128]{1,0:T(8,128)(2,1)} %new_k_hbm.1, ...), custom_call_target="tpu_custom_call" | custom-call | flops 50331648 | bytes 1572864 | tf_op jit(solution)/shard_map/attention/pallas_call | solution.py:169
  3.4 0.0 copy-start
  3.4 13.3 %all_to_all.30.got_ref = bf16[16,48,128]{2,1,0:T(8,128)(2,1)S(1)} all-to-all(bf16[16,48,128]{2,1,0:T(8,128)(2,1)S(1)} %get-tuple-element.11), channel_id=1, replica_groups={{120,112,104,96,88,80,72,64,56,48,40,32,24,16,8,0},{121,113,105,97,89,8..., dimensions={0} | all-to-all | bytes 393216 | tf_op jit(solution)/shard_map/all_to_all | solution.py:404
  16.7 1.1 %project.1 = (f32[16,32,512]{2,1,0:T(8,128)S(1)}, bf16[16,32,512]{2,1,0:T(8,128)(2,1)S(1)}) custom-call(bf16[16,48,128]{2,1,0:T(8,128)(2,1)S(1)} %all_to_all.30.got_ref, bf16[128,16384]{1,0:T(8,128)(2,1)S(1)} %get-tuple-element.12.w_ref), custom_call_target="tpu_custom_call" | custom-call | flops 134217728 | bytes 4194304 | tf_op jit(solution)/shard_map/project/pallas_call | solution.py:213
  17.8 1.7 %collective-permute-start = (bf16[16,32,512]{2,1,0:T(8,128)(2,1)S(1)}, bf16[16,32,512]{2,1,0:T(8,128)(2,1)S(1)}, u32[]{:S(2)}, u32[]{:S(2)}) collective-permute-start(bf16[16,32,512]{2,1,0:T(8,128)(2,1)S(1)} %get-tuple-element.14), channel_id=1, source_target_pairs={{0,1},{1,0},{2,3},{3,2},{4,5},{5,4},{6,7},{7,6},{8,9},{9,8},{10,11... | collective-permute-start | bytes 1572872 | tf_op jit(solution)/shard_map/ppermute | solution.py:413
  19.5 1.5 %collective-permute-done.got_ref = bf16[16,32,512]{2,1,0:T(8,128)(2,1)S(1)} collective-permute-done((bf16[16,32,512]{2,1,0:T(8,128)(2,1)S(1)}, bf16[16,32,512]{2,1,0:T(8,128)(2,1)S(1)}, u32[]{:S(2)}, u32[]{:S(2)}) %collective-permute-start) | collective-permute-done | bytes 524320 | tf_op jit(solution)/shard_map/ppermute | solution.py:413
  21.0 0.1 add_pair.1
  21.1 13.2 %all_to_all.31.parts_ref = bf16[16,32,512]{2,1,0:T(8,128)(2,1)S(1)} all-to-all(bf16[16,32,512]{2,1,0:T(8,128)(2,1)S(1)} %add_pair.1), channel_id=1, replica_groups={{120,112,104,96,88,80,72,64,56,48,40,32,24,16,8,0},{121,113,105,97,89,8..., dimensions={0} | all-to-all | bytes 1048576 | tf_op jit(solution)/shard_map/all_to_all | solution.py:404
  34.3 0.0 copy-done.1
  34.3 0.0 copy-done.2
  34.3 0.0 slice-start.1
  34.3 0.1 stream.1
  34.4 8.4 %all_to_all.32.parts_ref = bf16[4,32,640]{2,1,0:T(8,128)(2,1)S(1)} all-to-all(bf16[4,32,640]{2,1,0:T(8,128)(2,1)S(1)} %stream.1), channel_id=1, replica_groups={{6,4,2,0},{7,5,3,1},{14,12,10,8},{15,13,11,9},{22,20,18,16},{23,21,19,1..., dimensions={0} | all-to-all | bytes 327680 | tf_op jit(solution)/shard_map/all_to_all | solution.py:404
  42.9 0.0 slice-start.3
  42.9 3.4 %collective-permute-start.1 = (bf16[32,640]{1,0:T(8,128)(2,1)S(1)}, bf16[32,640]{1,0:T(8,128)(2,1)S(1)}, u32[]{:S(2)}, u32[]{:S(2)}) collective-permute-start(bf16[32,640]{1,0:T(8,128)(2,1)S(1)} %add_columns.1.mine_ref), channel_id=1, source_target_pairs={{0,1},{1,0},{2,3},{3,2},{4,5},{5,4},{6,7},{7,6},{8,9},{9,8},{10,11... | collective-permute-start | bytes 122888 | tf_op jit(solution)/shard_map/ppermute | solution.py:413
  46.3 0.9 %collective-permute-done.1.other_ref = bf16[32,640]{1,0:T(8,128)(2,1)S(1)} collective-permute-done((bf16[32,640]{1,0:T(8,128)(2,1)S(1)}, bf16[32,640]{1,0:T(8,128)(2,1)S(1)}, u32[]{:S(2)}, u32[]{:S(2)}) %collective-permute-start.1) | collective-permute-done | bytes 40992 | tf_op jit(solution)/shard_map/ppermute | solution.py:413
  47.2 2.4 %gate_up.1 = (bf16[16,4,3456]{2,1,0:T(4,128)(2,1)S(1)}, f32[32,128]{1,0:T(8,128)S(1)}) custom-call(bf16[32,640]{1,0:T(8,128)(2,1)S(1)} %add_columns.1.mine_ref, bf16[32,640]{1,0:T(8,128)(2,1)S(1)} %collective-permute-done.1.other_ref, bf16[1024,3328]{1,0:T(8,128)(2,1)S(1)} %bitcast.3, bf16[1024,3328]{1,0:T(8,128)(2,1)S(1)} %copy-done), custom_call_target="tpu_custom_call" | custom-call | flops 436207616 | bytes 13631488 | tf_op jit(solution)/shard_map/gate_up/pallas_call | solution.py:328
  49.6 14.0 %all_to_all.33.parts_ref = bf16[16,4,3456]{2,1,0:T(4,128)(2,1)S(1)} all-to-all(bf16[16,4,3456]{2,1,0:T(4,128)(2,1)S(1)} %get-tuple-element.16), channel_id=1, replica_groups={{0,8,16,24,56,48,40,32,64,72,80,88,120,112,104,96},{1,9,17,25,57,49,41,..., dimensions={0} | all-to-all | bytes 884736 | tf_op jit(solution)/shard_map/all_to_all | solution.py:404
  63.6 0.2 hidden_units.1
  63.8 10.0 %all_to_all.34.parts_ref = bf16[16,4,1664]{2,1,0:T(4,128)(2,1)S(1)} all-to-all(bf16[16,4,1664]{2,1,0:T(4,128)(2,1)S(1)} %hidden_units.1), channel_id=1, replica_groups={{120,112,104,96,88,80,72,64,56,48,40,32,24,16,8,0},{121,113,105,97,89,8..., dimensions={0} | all-to-all | bytes 425984 | tf_op jit(solution)/shard_map/all_to_all | solution.py:404
  73.8 0.0 slice-done.3
  73.8 1.3 %down.1 = bf16[8,32,128]{2,1,0:T(8,128)(2,1)S(1)} custom-call(bf16[16,4,1664]{2,1,0:T(4,128)(2,1)S(1)} %all_to_all.34.parts_ref, bf16[3328,1024]{1,0:T(8,128)(2,1)S(1)} %bitcast.5), custom_call_target="tpu_custom_call" | custom-call | flops 218103808 | bytes 6815744 | tf_op jit(solution)/shard_map/down/pallas_call | solution.py:373
  75.1 9.8 %all_to_all.35.parts_ref = bf16[8,32,128]{2,1,0:T(8,128)(2,1)S(1)} all-to-all(bf16[8,32,128]{2,1,0:T(8,128)(2,1)S(1)} %down.1), channel_id=1, replica_groups={{7,5,3,1,6,4,2,0},{15,13,11,9,14,12,10,8},{23,21,19,17,22,20,18,16},{31..., dimensions={0} | all-to-all | bytes 131072 | tf_op jit(solution)/shard_map/all_to_all | solution.py:404
  84.9 0.6 finish.1
  (11 shorter events, 0.0 us)
Async XLA Ops:
  0.0 34.3 %copy-start.1 = (bf16[32,128]{1,0:T(8,128)(2,1)S(1)}, bf16[32,128]{1,0:T(8,128)(2,1)}, u32[]{:S(2)}) copy-start(bf16[32,128]{1,0:T(8,128)(2,1)} %res_ref.1) | copy-start | bytes 24580
  0.0 34.3 %copy-start.2 = (bf16[128]{0:T(256)(128)(2,1)S(1)}, bf16[128]{0:T(256)(128)(2,1)}, u32[]{:S(2)}) copy-start(bf16[128]{0:T(256)(128)(2,1)} %param.22) | copy-start | bytes 772
  3.4 30.9 %copy-start = (bf16[1024,3328]{1,0:T(8,128)(2,1)S(1)}, bf16[1024,3328]{1,0:T(8,128)(2,1)}, u32[]{:S(2)}) copy-start(bf16[1024,3328]{1,0:T(8,128)(2,1)} %up_w.1) | copy-start | bytes 20447236
  16.7 26.1 %slice-start = ((s8[6815744]{0:T(1024)(128)(4,1)}), s8[4194304]{0:T(1024)(128)(4,1)S(1)}, s32[]{:S(2)}) async-start(s8[6815744]{0:T(1024)(128)(4,1)} %bitcast.2), calls=%async_computation.6 | async-start | bytes 8388608
  17.8 3.2 %collective-permute-start = (bf16[16,32,512]{2,1,0:T(8,128)(2,1)S(1)}, bf16[16,32,512]{2,1,0:T(8,128)(2,1)S(1)}, u32[]{:S(2)}, u32[]{:S(2)}) collective-permute-start(bf16[16,32,512]{2,1,0:T(8,128)(2,1)S(1)} %get-tuple-element.14), channel_id=1, source_target_pairs={{0,1},{1,0},{2,3},{3,2},{4,5},{5,4},{6,7},{7,6},{8,9},{9,8},{10,11... | collective-permute-start | bytes 1572872 | tf_op jit(solution)/shard_map/ppermute | solution.py:413
  34.3 8.5 %slice-start.1 = ((s8[6815744]{0:T(1024)(128)(4,1)}), s8[2621440]{0:T(1024)(128)(4,1)S(1)}, s32[]{:S(2)}) async-start(s8[6815744]{0:T(1024)(128)(4,1)} %bitcast.2), calls=%async_computation.7 | async-start | bytes 5242880
  42.8 31.0 %slice-start.2 = ((s8[6815744]{0:T(1024)(128)(4,1)}), s8[4194304]{0:T(1024)(128)(4,1)S(1)}, s32[]{:S(2)}) async-start(s8[6815744]{0:T(1024)(128)(4,1)} %bitcast.4), calls=%async_computation.8 | async-start | bytes 8388608
  42.9 31.0 %slice-start.3 = ((s8[6815744]{0:T(1024)(128)(4,1)}), s8[2621440]{0:T(1024)(128)(4,1)S(1)}, s32[]{:S(2)}) async-start(s8[6815744]{0:T(1024)(128)(4,1)} %bitcast.4), calls=%async_computation.9 | async-start | bytes 5242880
  42.9 4.3 %collective-permute-start.1 = (bf16[32,640]{1,0:T(8,128)(2,1)S(1)}, bf16[32,640]{1,0:T(8,128)(2,1)S(1)}, u32[]{:S(2)}, u32[]{:S(2)}) collective-permute-start(bf16[32,640]{1,0:T(8,128)(2,1)S(1)} %add_columns.1.mine_ref), channel_id=1, source_target_pairs={{0,1},{1,0},{2,3},{3,2},{4,5},{5,4},{6,7},{7,6},{8,9},{9,8},{10,11... | collective-permute-start | bytes 122888 | tf_op jit(solution)/shard_map/ppermute | solution.py:413

commit v11 on v10

--- a/solution.py
+++ b/solution.py
@@ -39,8 +39,7 @@
 
 
 BACK = tuple(reversed(range(N_KV)))
-SNAKE = tuple(4 * x + (3 - z if x % 2 else z) for x in range(4) for z in range(4))
-MERGE_ORDER, PROJ_ORDER, GATE_ORDER, HIDDEN_ORDER = BACK, BACK, SNAKE, BACK
+MERGE_ORDER, PROJ_ORDER, GATE_ORDER, HIDDEN_ORDER = BACK, BACK, BACK, BACK
 Y_ORDER = (3, 2, 1, 0)
 HEAD_ORDER = (7, 5, 3, 1, 6, 4, 2, 0)
 

time: 85.8 us -> 85.1 us (level)
  no operation moved by 1% of the time
where the time goes in v11:
time: 85.1 us; the launch traced here: 84.8 us
  blocking collectives  68 us (80%)
  Pallas kernels  9.15 us (11%)
  starting transfers between devices  5.12 us (6%)
  waiting for transfers between devices  2.41 us (3%)
    all_to_all x6, blocking collectives, exchange(): lax.all_to_all(value, axis, 0, 0, axis_index_groups=groups, tiled=True)  68 us
    ppermute x2, starting transfers between devices, swap(): return lax.ppermute(value, 'head', [(j, j ^ step) for j in range(KVH)])  5.12 us
    pallas_call x1, Pallas kernels, attention_partials(): pl.pallas_call(attention_kernel, out_shape=[pltpu.VMEM((GROUP, ROWS + 16,...  3.39 us
    pallas_call x1, Pallas kernels, gate_up(): pl.pallas_call(gate_kernel, out_shape=[shape(wide, BF16), shape((ROWS, OW...  2.43 us
    ppermute x2, waiting for transfers between devices, swap(): return lax.ppermute(value, 'head', [(j, j ^ step) for j in range(KVH)])  2.41 us
  transfers between devices with their start and end apart: 2, of which 2 were waited for; matrix products, arithmetic and copies ran while one was open for 0% of the time, Pallas kernels for 0%

profile of v11, /device:TPU:1, one launch (start us, length us, event | category | flops | bytes accessed | tf_op | source)
XLA Modules:
  0.0 84.8 jit_solution(569669080945639850)
XLA Ops:
  0.0 3.4 %attention.1 = (bf16[16,48,128]{2,1,0:T(8,128)(2,1)S(1)}, bf16[128,16384]{1,0:T(8,128)(2,1)S(1)}) custom-call(s32[2,24]{1,0:T(2,128)} %table_hbm.1, s32[16]{0:T(128)} %lengths_hbm.1, bf16[32,2048]{1,0:T(8,128)(2,1)} %q_hbm.1, bf16[24,1,128,128]{3,2,1,0:T(8,128)(2,1)} %k_hbm.1, bf16[24,1,128,128]{3,2,1,0:T(8,128)(2,1)} %v_hbm.1, bf16[32,128]{1,0:T(8,128)(2,1)} %new_k_hbm.1, ...), custom_call_target="tpu_custom_call" | custom-call | flops 50331648 | bytes 1572864 | tf_op jit(solution)/shard_map/attention/pallas_call | solution.py:168
  3.4 0.0 copy-start
  3.4 13.3 %all_to_all.30.got_ref = bf16[16,48,128]{2,1,0:T(8,128)(2,1)S(1)} all-to-all(bf16[16,48,128]{2,1,0:T(8,128)(2,1)S(1)} %get-tuple-element.11), channel_id=1, replica_groups={{120,112,104,96,88,80,72,64,56,48,40,32,24,16,8,0},{121,113,105,97,89,8..., dimensions={0} | all-to-all | bytes 393216 | tf_op jit(solution)/shard_map/all_to_all | solution.py:403
  16.7 1.1 %project.1 = (f32[16,32,512]{2,1,0:T(8,128)S(1)}, bf16[16,32,512]{2,1,0:T(8,128)(2,1)S(1)}) custom-call(bf16[16,48,128]{2,1,0:T(8,128)(2,1)S(1)} %all_to_all.30.got_ref, bf16[128,16384]{1,0:T(8,128)(2,1)S(1)} %get-tuple-element.12.w_ref), custom_call_target="tpu_custom_call" | custom-call | flops 134217728 | bytes 4194304 | tf_op jit(solution)/shard_map/project/pallas_call | solution.py:212
  17.8 1.7 %collective-permute-start = (bf16[16,32,512]{2,1,0:T(8,128)(2,1)S(1)}, bf16[16,32,512]{2,1,0:T(8,128)(2,1)S(1)}, u32[]{:S(2)}, u32[]{:S(2)}) collective-permute-start(bf16[16,32,512]{2,1,0:T(8,128)(2,1)S(1)} %get-tuple-element.14), channel_id=1, source_target_pairs={{0,1},{1,0},{2,3},{3,2},{4,5},{5,4},{6,7},{7,6},{8,9},{9,8},{10,11... | collective-permute-start | bytes 1572872 | tf_op jit(solution)/shard_map/ppermute | solution.py:412
  19.5 1.5 %collective-permute-done.got_ref = bf16[16,32,512]{2,1,0:T(8,128)(2,1)S(1)} collective-permute-done((bf16[16,32,512]{2,1,0:T(8,128)(2,1)S(1)}, bf16[16,32,512]{2,1,0:T(8,128)(2,1)S(1)}, u32[]{:S(2)}, u32[]{:S(2)}) %collective-permute-start) | collective-permute-done | bytes 524320 | tf_op jit(solution)/shard_map/ppermute | solution.py:412
  21.0 0.1 add_pair.1
  21.1 13.2 %all_to_all.31.parts_ref = bf16[16,32,512]{2,1,0:T(8,128)(2,1)S(1)} all-to-all(bf16[16,32,512]{2,1,0:T(8,128)(2,1)S(1)} %add_pair.1), channel_id=1, replica_groups={{120,112,104,96,88,80,72,64,56,48,40,32,24,16,8,0},{121,113,105,97,89,8..., dimensions={0} | all-to-all | bytes 1048576 | tf_op jit(solution)/shard_map/all_to_all | solution.py:403
  34.3 0.0 copy-done.1
  34.3 0.0 copy-done
  34.3 0.0 slice-start.1
  34.3 0.1 stream.1
  34.4 8.4 %all_to_all.32.parts_ref = bf16[4,32,640]{2,1,0:T(8,128)(2,1)S(1)} all-to-all(bf16[4,32,640]{2,1,0:T(8,128)(2,1)S(1)} %stream.1), channel_id=1, replica_groups={{6,4,2,0},{7,5,3,1},{14,12,10,8},{15,13,11,9},{22,20,18,16},{23,21,19,1..., dimensions={0} | all-to-all | bytes 327680 | tf_op jit(solution)/shard_map/all_to_all | solution.py:403
  42.8 0.0 slice-done.1
  42.9 0.0 slice-start.3
  42.9 3.4 %collective-permute-start.1 = (bf16[32,640]{1,0:T(8,128)(2,1)S(1)}, bf16[32,640]{1,0:T(8,128)(2,1)S(1)}, u32[]{:S(2)}, u32[]{:S(2)}) collective-permute-start(bf16[32,640]{1,0:T(8,128)(2,1)S(1)} %add_columns.1.mine_ref), channel_id=1, source_target_pairs={{0,1},{1,0},{2,3},{3,2},{4,5},{5,4},{6,7},{7,6},{8,9},{9,8},{10,11... | collective-permute-start | bytes 122888 | tf_op jit(solution)/shard_map/ppermute | solution.py:412
  46.3 0.9 %collective-permute-done.1.other_ref = bf16[32,640]{1,0:T(8,128)(2,1)S(1)} collective-permute-done((bf16[32,640]{1,0:T(8,128)(2,1)S(1)}, bf16[32,640]{1,0:T(8,128)(2,1)S(1)}, u32[]{:S(2)}, u32[]{:S(2)}) %collective-permute-start.1) | collective-permute-done | bytes 40992 | tf_op jit(solution)/shard_map/ppermute | solution.py:412
  47.2 2.4 %gate_up.1 = (bf16[16,4,3456]{2,1,0:T(4,128)(2,1)S(1)}, f32[32,128]{1,0:T(8,128)S(1)}) custom-call(bf16[32,640]{1,0:T(8,128)(2,1)S(1)} %add_columns.1.mine_ref, bf16[32,640]{1,0:T(8,128)(2,1)S(1)} %collective-permute-done.1.other_ref, bf16[1024,3328]{1,0:T(8,128)(2,1)S(1)} %bitcast.3, bf16[1024,3328]{1,0:T(8,128)(2,1)S(1)} %copy-done), custom_call_target="tpu_custom_call" | custom-call | flops 436207616 | bytes 13631488 | tf_op jit(solution)/shard_map/gate_up/pallas_call | solution.py:327
  49.6 12.6 %all_to_all.33.parts_ref = bf16[16,4,3456]{2,1,0:T(4,128)(2,1)S(1)} all-to-all(bf16[16,4,3456]{2,1,0:T(4,128)(2,1)S(1)} %get-tuple-element.16), channel_id=1, replica_groups={{120,112,104,96,88,80,72,64,56,48,40,32,24,16,8,0},{121,113,105,97,89,8..., dimensions={0} | all-to-all | bytes 884736 | tf_op jit(solution)/shard_map/all_to_all | solution.py:403
  62.2 0.2 hidden_units.1
  62.4 10.7 %all_to_all.34.parts_ref = bf16[16,4,1664]{2,1,0:T(4,128)(2,1)S(1)} all-to-all(bf16[16,4,1664]{2,1,0:T(4,128)(2,1)S(1)} %hidden_units.1), channel_id=1, replica_groups={{120,112,104,96,88,80,72,64,56,48,40,32,24,16,8,0},{121,113,105,97,89,8..., dimensions={0} | all-to-all | bytes 425984 | tf_op jit(solution)/shard_map/all_to_all | solution.py:403
  73.2 1.3 %down.1 = bf16[8,32,128]{2,1,0:T(8,128)(2,1)S(1)} custom-call(bf16[16,4,1664]{2,1,0:T(4,128)(2,1)S(1)} %all_to_all.34.parts_ref, bf16[3328,1024]{1,0:T(8,128)(2,1)S(1)} %bitcast.5), custom_call_target="tpu_custom_call" | custom-call | flops 218103808 | bytes 6815744 | tf_op jit(solution)/shard_map/down/pallas_call | solution.py:372
  74.5 9.8 %all_to_all.35.parts_ref = bf16[8,32,128]{2,1,0:T(8,128)(2,1)S(1)} all-to-all(bf16[8,32,128]{2,1,0:T(8,128)(2,1)S(1)} %down.1), channel_id=1, replica_groups={{7,5,3,1,6,4,2,0},{15,13,11,9,14,12,10,8},{23,21,19,17,22,20,18,16},{31..., dimensions={0} | all-to-all | bytes 131072 | tf_op jit(solution)/shard_map/all_to_all | solution.py:403
  84.2 0.6 finish.1
  (11 shorter events, 0.0 us)
Async XLA Ops:
  0.0 34.3 %copy-start.1 = (bf16[32,128]{1,0:T(8,128)(2,1)S(1)}, bf16[32,128]{1,0:T(8,128)(2,1)}, u32[]{:S(2)}) copy-start(bf16[32,128]{1,0:T(8,128)(2,1)} %res_ref.1) | copy-start | bytes 24580
  0.0 34.3 %copy-start.2 = (bf16[128]{0:T(256)(128)(2,1)S(1)}, bf16[128]{0:T(256)(128)(2,1)}, u32[]{:S(2)}) copy-start(bf16[128]{0:T(256)(128)(2,1)} %param.22) | copy-start | bytes 772
  3.4 30.9 %copy-start = (bf16[1024,3328]{1,0:T(8,128)(2,1)S(1)}, bf16[1024,3328]{1,0:T(8,128)(2,1)}, u32[]{:S(2)}) copy-start(bf16[1024,3328]{1,0:T(8,128)(2,1)} %up_w.1) | copy-start | bytes 20447236
  16.7 26.1 %slice-start = ((s8[6815744]{0:T(1024)(128)(4,1)}), s8[4194304]{0:T(1024)(128)(4,1)S(1)}, s32[]{:S(2)}) async-start(s8[6815744]{0:T(1024)(128)(4,1)} %bitcast.2), calls=%async_computation.6 | async-start | bytes 8388608
  17.8 3.2 %collective-permute-start = (bf16[16,32,512]{2,1,0:T(8,128)(2,1)S(1)}, bf16[16,32,512]{2,1,0:T(8,128)(2,1)S(1)}, u32[]{:S(2)}, u32[]{:S(2)}) collective-permute-start(bf16[16,32,512]{2,1,0:T(8,128)(2,1)S(1)} %get-tuple-element.14), channel_id=1, source_target_pairs={{0,1},{1,0},{2,3},{3,2},{4,5},{5,4},{6,7},{7,6},{8,9},{9,8},{10,11... | collective-permute-start | bytes 1572872 | tf_op jit(solution)/shard_map/ppermute | solution.py:412
  34.3 8.5 %slice-start.1 = ((s8[6815744]{0:T(1024)(128)(4,1)}), s8[2621440]{0:T(1024)(128)(4,1)S(1)}, s32[]{:S(2)}) async-start(s8[6815744]{0:T(1024)(128)(4,1)} %bitcast.2), calls=%async_computation.7 | async-start | bytes 5242880
  42.8 30.3 %slice-start.2 = ((s8[6815744]{0:T(1024)(128)(4,1)}), s8[4194304]{0:T(1024)(128)(4,1)S(1)}, s32[]{:S(2)}) async-start(s8[6815744]{0:T(1024)(128)(4,1)} %bitcast.4), calls=%async_computation.8 | async-start | bytes 8388608
  42.9 30.3 %slice-start.3 = ((s8[6815744]{0:T(1024)(128)(4,1)}), s8[2621440]{0:T(1024)(128)(4,1)S(1)}, s32[]{:S(2)}) async-start(s8[6815744]{0:T(1024)(128)(4,1)} %bitcast.4), calls=%async_computation.9 | async-start | bytes 5242880
  42.9 4.3 %collective-permute-start.1 = (bf16[32,640]{1,0:T(8,128)(2,1)S(1)}, bf16[32,640]{1,0:T(8,128)(2,1)S(1)}, u32[]{:S(2)}, u32[]{:S(2)}) collective-permute-start(bf16[32,640]{1,0:T(8,128)(2,1)S(1)} %add_columns.1.mine_ref), channel_id=1, source_target_pairs={{0,1},{1,0},{2,3},{3,2},{4,5},{5,4},{6,7},{7,6},{8,9},{9,8},{10,11... | collective-permute-start | bytes 122888 | tf_op jit(solution)/shard_map/ppermute | solution.py:412

commit v12 on v11

--- a/solution.py
+++ b/solution.py
@@ -38,8 +38,8 @@
     return lax.axis_index("head") % 2 == 0
 
 
-BACK = tuple(reversed(range(N_KV)))
-MERGE_ORDER, PROJ_ORDER, GATE_ORDER, HIDDEN_ORDER = BACK, BACK, BACK, BACK
+Z_BACK = tuple(4 * x + z for z in reversed(range(4)) for x in reversed(range(4)))
+MERGE_ORDER, PROJ_ORDER, GATE_ORDER, HIDDEN_ORDER = Z_BACK, Z_BACK, Z_BACK, Z_BACK
 Y_ORDER = (3, 2, 1, 0)
 HEAD_ORDER = (7, 5, 3, 1, 6, 4, 2, 0)
 

time: 85.1 us -> 84.5 us (level)
  no operation moved by 1% of the time
where the time goes in v12:
time: 84.5 us; the launch traced here: 84.2 us
  blocking collectives  68 us (80%)
  Pallas kernels  9.15 us (11%)
  starting transfers between devices  4.5 us (5%)
  waiting for transfers between devices  2.41 us (3%)
    all_to_all x6, blocking collectives, exchange(): lax.all_to_all(value, axis, 0, 0, axis_index_groups=groups, tiled=True)  68 us
    ppermute x2, starting transfers between devices, swap(): return lax.ppermute(value, 'head', [(j, j ^ step) for j in range(KVH)])  4.5 us
    pallas_call x1, Pallas kernels, attention_partials(): pl.pallas_call(attention_kernel, out_shape=[pltpu.VMEM((GROUP, ROWS + 16,...  3.39 us
    pallas_call x1, Pallas kernels, gate_up(): pl.pallas_call(gate_kernel, out_shape=[shape(wide, BF16), shape((ROWS, OW...  2.43 us
    ppermute x2, waiting for transfers between devices, swap(): return lax.ppermute(value, 'head', [(j, j ^ step) for j in range(KVH)])  2.41 us
  transfers between devices with their start and end apart: 2, of which 2 were waited for; matrix products, arithmetic and copies ran while one was open for 0% of the time, Pallas kernels for 0%

profile of v12, /device:TPU:1, one launch (start us, length us, event | category | flops | bytes accessed | tf_op | source)
XLA Modules:
  0.0 84.2 jit_solution(14196476085940972905)
XLA Ops:
  0.0 3.4 %attention.1 = (bf16[16,48,128]{2,1,0:T(8,128)(2,1)S(1)}, bf16[128,16384]{1,0:T(8,128)(2,1)S(1)}) custom-call(s32[2,24]{1,0:T(2,128)} %table_hbm.1, s32[16]{0:T(128)} %lengths_hbm.1, bf16[32,2048]{1,0:T(8,128)(2,1)} %q_hbm.1, bf16[24,1,128,128]{3,2,1,0:T(8,128)(2,1)} %k_hbm.1, bf16[24,1,128,128]{3,2,1,0:T(8,128)(2,1)} %v_hbm.1, bf16[32,128]{1,0:T(8,128)(2,1)} %new_k_hbm.1, ...), custom_call_target="tpu_custom_call" | custom-call | flops 50331648 | bytes 1572864 | tf_op jit(solution)/shard_map/attention/pallas_call | solution.py:168
  3.4 0.0 copy-start
  3.4 13.4 %all_to_all.30.got_ref = bf16[16,48,128]{2,1,0:T(8,128)(2,1)S(1)} all-to-all(bf16[16,48,128]{2,1,0:T(8,128)(2,1)S(1)} %get-tuple-element.11), channel_id=1, replica_groups={{120,88,56,24,112,80,48,16,104,72,40,8,96,64,32,0},{121,89,57,25,113,81..., dimensions={0} | all-to-all | bytes 393216 | tf_op jit(solution)/shard_map/all_to_all | solution.py:403
  16.8 1.1 %project.1 = (f32[16,32,512]{2,1,0:T(8,128)S(1)}, bf16[16,32,512]{2,1,0:T(8,128)(2,1)S(1)}) custom-call(bf16[16,48,128]{2,1,0:T(8,128)(2,1)S(1)} %all_to_all.30.got_ref, bf16[128,16384]{1,0:T(8,128)(2,1)S(1)} %get-tuple-element.12.w_ref), custom_call_target="tpu_custom_call" | custom-call | flops 134217728 | bytes 4194304 | tf_op jit(solution)/shard_map/project/pallas_call | solution.py:212
  17.8 1.8 %collective-permute-start = (bf16[16,32,512]{2,1,0:T(8,128)(2,1)S(1)}, bf16[16,32,512]{2,1,0:T(8,128)(2,1)S(1)}, u32[]{:S(2)}, u32[]{:S(2)}) collective-permute-start(bf16[16,32,512]{2,1,0:T(8,128)(2,1)S(1)} %get-tuple-element.14), channel_id=1, source_target_pairs={{0,1},{1,0},{2,3},{3,2},{4,5},{5,4},{6,7},{7,6},{8,9},{9,8},{10,11... | collective-permute-start | bytes 1572872 | tf_op jit(solution)/shard_map/ppermute | solution.py:412
  19.6 1.5 %collective-permute-done.got_ref = bf16[16,32,512]{2,1,0:T(8,128)(2,1)S(1)} collective-permute-done((bf16[16,32,512]{2,1,0:T(8,128)(2,1)S(1)}, bf16[16,32,512]{2,1,0:T(8,128)(2,1)S(1)}, u32[]{:S(2)}, u32[]{:S(2)}) %collective-permute-start) | collective-permute-done | bytes 524320 | tf_op jit(solution)/shard_map/ppermute | solution.py:412
  21.2 0.1 add_pair.1
  21.3 13.5 %all_to_all.31.parts_ref = bf16[16,32,512]{2,1,0:T(8,128)(2,1)S(1)} all-to-all(bf16[16,32,512]{2,1,0:T(8,128)(2,1)S(1)} %add_pair.1), channel_id=1, replica_groups={{120,88,56,24,112,80,48,16,104,72,40,8,96,64,32,0},{121,89,57,25,113,81..., dimensions={0} | all-to-all | bytes 1048576 | tf_op jit(solution)/shard_map/all_to_all | solution.py:403
  34.8 0.0 copy-done.1
  34.8 0.0 copy-done
  34.8 0.0 slice-start.1
  34.8 0.1 stream.1
  34.9 8.4 %all_to_all.32.parts_ref = bf16[4,32,640]{2,1,0:T(8,128)(2,1)S(1)} all-to-all(bf16[4,32,640]{2,1,0:T(8,128)(2,1)S(1)} %stream.1), channel_id=1, replica_groups={{6,4,2,0},{7,5,3,1},{14,12,10,8},{15,13,11,9},{22,20,18,16},{23,21,19,1..., dimensions={0} | all-to-all | bytes 327680 | tf_op jit(solution)/shard_map/all_to_all | solution.py:403
  43.4 0.0 slice-start.3
  43.4 2.7 %collective-permute-start.1 = (bf16[32,640]{1,0:T(8,128)(2,1)S(1)}, bf16[32,640]{1,0:T(8,128)(2,1)S(1)}, u32[]{:S(2)}, u32[]{:S(2)}) collective-permute-start(bf16[32,640]{1,0:T(8,128)(2,1)S(1)} %add_columns.1.mine_ref), channel_id=1, source_target_pairs={{0,1},{1,0},{2,3},{3,2},{4,5},{5,4},{6,7},{7,6},{8,9},{9,8},{10,11... | collective-permute-start | bytes 122888 | tf_op jit(solution)/shard_map/ppermute | solution.py:412
  46.1 0.9 %collective-permute-done.1.other_ref = bf16[32,640]{1,0:T(8,128)(2,1)S(1)} collective-permute-done((bf16[32,640]{1,0:T(8,128)(2,1)S(1)}, bf16[32,640]{1,0:T(8,128)(2,1)S(1)}, u32[]{:S(2)}, u32[]{:S(2)}) %collective-permute-start.1) | collective-permute-done | bytes 40992 | tf_op jit(solution)/shard_map/ppermute | solution.py:412
  47.0 2.4 %gate_up.1 = (bf16[16,4,3456]{2,1,0:T(4,128)(2,1)S(1)}, f32[32,128]{1,0:T(8,128)S(1)}) custom-call(bf16[32,640]{1,0:T(8,128)(2,1)S(1)} %add_columns.1.mine_ref, bf16[32,640]{1,0:T(8,128)(2,1)S(1)} %collective-permute-done.1.other_ref, bf16[1024,3328]{1,0:T(8,128)(2,1)S(1)} %bitcast.3, bf16[1024,3328]{1,0:T(8,128)(2,1)S(1)} %copy-done), custom_call_target="tpu_custom_call" | custom-call | flops 436207616 | bytes 13631488 | tf_op jit(solution)/shard_map/gate_up/pallas_call | solution.py:327
  49.4 12.7 %all_to_all.33.parts_ref = bf16[16,4,3456]{2,1,0:T(4,128)(2,1)S(1)} all-to-all(bf16[16,4,3456]{2,1,0:T(4,128)(2,1)S(1)} %get-tuple-element.16), channel_id=1, replica_groups={{120,88,56,24,112,80,48,16,104,72,40,8,96,64,32,0},{121,89,57,25,113,81..., dimensions={0} | all-to-all | bytes 884736 | tf_op jit(solution)/shard_map/all_to_all | solution.py:403
  62.2 0.2 hidden_units.1
  62.4 10.5 %all_to_all.34.parts_ref = bf16[16,4,1664]{2,1,0:T(4,128)(2,1)S(1)} all-to-all(bf16[16,4,1664]{2,1,0:T(4,128)(2,1)S(1)} %hidden_units.1), channel_id=1, replica_groups={{120,88,56,24,112,80,48,16,104,72,40,8,96,64,32,0},{121,89,57,25,113,81..., dimensions={0} | all-to-all | bytes 425984 | tf_op jit(solution)/shard_map/all_to_all | solution.py:403
  72.9 0.0 slice-done.3
  72.9 1.3 %down.1 = bf16[8,32,128]{2,1,0:T(8,128)(2,1)S(1)} custom-call(bf16[16,4,1664]{2,1,0:T(4,128)(2,1)S(1)} %all_to_all.34.parts_ref, bf16[3328,1024]{1,0:T(8,128)(2,1)S(1)} %bitcast.5), custom_call_target="tpu_custom_call" | custom-call | flops 218103808 | bytes 6815744 | tf_op jit(solution)/shard_map/down/pallas_call | solution.py:372
  74.2 9.4 %all_to_all.35.parts_ref = bf16[8,32,128]{2,1,0:T(8,128)(2,1)S(1)} all-to-all(bf16[8,32,128]{2,1,0:T(8,128)(2,1)S(1)} %down.1), channel_id=1, replica_groups={{7,5,3,1,6,4,2,0},{15,13,11,9,14,12,10,8},{23,21,19,17,22,20,18,16},{31..., dimensions={0} | all-to-all | bytes 131072 | tf_op jit(solution)/shard_map/all_to_all | solution.py:403
  83.6 0.6 finish.1
  (11 shorter events, 0.0 us)
Async XLA Ops:
  0.0 34.8 %copy-start.1 = (bf16[32,128]{1,0:T(8,128)(2,1)S(1)}, bf16[32,128]{1,0:T(8,128)(2,1)}, u32[]{:S(2)}) copy-start(bf16[32,128]{1,0:T(8,128)(2,1)} %res_ref.1) | copy-start | bytes 24580
  0.0 34.8 %copy-start.2 = (bf16[128]{0:T(256)(128)(2,1)S(1)}, bf16[128]{0:T(256)(128)(2,1)}, u32[]{:S(2)}) copy-start(bf16[128]{0:T(256)(128)(2,1)} %param.22) | copy-start | bytes 772
  3.4 31.4 %copy-start = (bf16[1024,3328]{1,0:T(8,128)(2,1)S(1)}, bf16[1024,3328]{1,0:T(8,128)(2,1)}, u32[]{:S(2)}) copy-start(bf16[1024,3328]{1,0:T(8,128)(2,1)} %up_w.1) | copy-start | bytes 20447236
  16.8 26.6 %slice-start = ((s8[6815744]{0:T(1024)(128)(4,1)}), s8[4194304]{0:T(1024)(128)(4,1)S(1)}, s32[]{:S(2)}) async-start(s8[6815744]{0:T(1024)(128)(4,1)} %bitcast.2), calls=%async_computation.6 | async-start | bytes 8388608
  17.8 3.3 %collective-permute-start = (bf16[16,32,512]{2,1,0:T(8,128)(2,1)S(1)}, bf16[16,32,512]{2,1,0:T(8,128)(2,1)S(1)}, u32[]{:S(2)}, u32[]{:S(2)}) collective-permute-start(bf16[16,32,512]{2,1,0:T(8,128)(2,1)S(1)} %get-tuple-element.14), channel_id=1, source_target_pairs={{0,1},{1,0},{2,3},{3,2},{4,5},{5,4},{6,7},{7,6},{8,9},{9,8},{10,11... | collective-permute-start | bytes 1572872 | tf_op jit(solution)/shard_map/ppermute | solution.py:412
  34.8 8.5 %slice-start.1 = ((s8[6815744]{0:T(1024)(128)(4,1)}), s8[2621440]{0:T(1024)(128)(4,1)S(1)}, s32[]{:S(2)}) async-start(s8[6815744]{0:T(1024)(128)(4,1)} %bitcast.2), calls=%async_computation.7 | async-start | bytes 5242880
  43.4 29.5 %slice-start.2 = ((s8[6815744]{0:T(1024)(128)(4,1)}), s8[4194304]{0:T(1024)(128)(4,1)S(1)}, s32[]{:S(2)}) async-start(s8[6815744]{0:T(1024)(128)(4,1)} %bitcast.4), calls=%async_computation.8 | async-start | bytes 8388608
  43.4 29.5 %slice-start.3 = ((s8[6815744]{0:T(1024)(128)(4,1)}), s8[2621440]{0:T(1024)(128)(4,1)S(1)}, s32[]{:S(2)}) async-start(s8[6815744]{0:T(1024)(128)(4,1)} %bitcast.4), calls=%async_computation.9 | async-start | bytes 5242880
  43.4 3.6 %collective-permute-start.1 = (bf16[32,640]{1,0:T(8,128)(2,1)S(1)}, bf16[32,640]{1,0:T(8,128)(2,1)S(1)}, u32[]{:S(2)}, u32[]{:S(2)}) collective-permute-start(bf16[32,640]{1,0:T(8,128)(2,1)S(1)} %add_columns.1.mine_ref), channel_id=1, source_target_pairs={{0,1},{1,0},{2,3},{3,2},{4,5},{5,4},{6,7},{7,6},{8,9},{9,8},{10,11... | collective-permute-start | bytes 122888 | tf_op jit(solution)/shard_map/ppermute | solution.py:412
